TPU v7x, 32 devices: a whole 2x2x4 slice. The times are simulated.
32 devices in a mesh: leaf: 4 (over z), oct: 8 (over y, x, core).
Axes of the slice: x: 2, y: 2, z: 4, core: 2. Of those that a mesh axis runs over, the one named last changes fastest.
Arguments:
- fibre_solve: bfloat16 [384, 256, 256], P(('leaf', 'oct')), may hold values from -0.375 to 0.375
- fibre_rhs: bfloat16 [384, 256], P(('leaf', 'oct')), may hold values from -6 to 6
- fibre_points: float32 [384, 256], P(('leaf', 'oct')), may hold values from 0 to 1
- fibre_owner: int32 [384, 1], P(('leaf', 'oct')), may hold values from 0 to 7; in each aligned block of 12 rows (0 to 11, 12 to 23, ...) at most 3 rows name the same one
- shell_points: float32 [3, 128], P(None, ('leaf', 'oct')), may hold values from 0 to 1
- shell_block: bfloat16 [3, 128, 98304], P(None, ('leaf', 'oct')), may hold values from -0.01953125 to 0.01953125
- density: float32 [98304], P(('leaf', 'oct')), may hold values from -6 to 6
Outputs:
- fibre_flow: float32 [3, 24576], P(None, ('leaf', 'oct'))
- shell_flow: float32 [3, 128], P(None, ('leaf', 'oct'))
Inputs may be any that keep to these rules, and one draw needn't show every extreme that they name: `fibre_owner`: among the 12 fibres of one device (an aligned block) no child box is named more than 3 times, and some child box is named exactly 3 times.
All inputs are finite; a program needn't handle non-finite values.
Results may differ from a plain program's by a relative error of at most 0.0012.
Values may be sent and summed in bfloat16 or wider, within the bound.
No kernel may reach another device: no remote copies, remote signals or barrier semaphores. Data moves between devices by JAX's collectives and lax.ppermute only.
A program may use at most 64 MiB of HBM per device.

v0:
```python
import math

import jax
import jax.numpy as jnp
from jax import lax
from jax.sharding import PartitionSpec as P

smooth_sq = 0.01
stokes_scale = 1.0 / (8.0 * math.pi)


def with_halo(cells, sides, width):
    for axis, dim in sides:
        count = lax.axis_size(axis)
        ends = count - 1
        head = lax.slice_in_dim(cells, 0, width, axis=dim)
        tail = lax.slice_in_dim(cells, cells.shape[dim] - width, cells.shape[dim], axis=dim)
        cells = jnp.concatenate(
            [
                lax.ppermute(tail, axis, [(i, (i + 1) % count) for i in range(ends)]),
                cells,
                lax.ppermute(head, axis, [((i + 1) % count, i) for i in range(ends)]),
            ],
            axis=dim,
        )
    return cells


def stokeslet(targets, sources):
    offset = targets[:, :, None] - sources[0:3, None, :]
    dist_sq = jnp.sum(offset * offset, axis=0)
    shifted = dist_sq + smooth_sq
    weight = 1.0 / (shifted * jnp.sqrt(shifted))
    forces = sources[3:6]
    projected = jnp.sum(offset * forces[:, None, :], axis=0) + sources[6][None, :]
    direct = weight * (dist_sq + 2.0 * smooth_sq)
    stretch = jnp.einsum("ts,cs->ct", direct, forces, precision=lax.Precision.HIGHEST)
    pointing = jnp.sum(offset * (weight * projected)[None], axis=2)
    return stokes_scale * (stretch + pointing)


def place_records(forces, points, owner_box, leaf_index):
    count_f = points.shape[0]
    node_count = points.shape[1] // 4
    local_xyz = points[:, : 3 * node_count].reshape(count_f, 3, node_count)
    quad_weight = points[:, 3 * node_count :]
    corner = jnp.stack(
        [2 * leaf_index + owner_box % 2, owner_box // 2 % 2, owner_box // 4], axis=1
    ).astype(jnp.float32)
    position = local_xyz + corner[:, :, None]
    pushes = forces[:, : 3 * node_count].reshape(count_f, 3, node_count) * quad_weight[:, None, :]
    source = forces[:, 3 * node_count :] * quad_weight
    return jnp.concatenate([position, pushes, source[:, None, :]], axis=1)


def near_flow(targets, column):
    spread = lax.all_gather(targets[None], "oct", axis=0, tiled=True)

    def per_set(target_set):
        running = jnp.zeros(target_set.shape, jnp.float32)
        for neighbour in range(3):
            running = running + stokeslet(target_set, column[neighbour])
        return running

    return lax.psum_scatter(lax.map(per_set, spread), "oct", scatter_dimension=0, tiled=True)[0]


def shards(fibre_solve, fibre_rhs, fibre_points, fibre_owner, shell_points, shell_block, density):
    fib_count = fibre_rhs.shape[0]
    node_count = fibre_points.shape[1] // 4
    octants = lax.axis_size("oct")
    leaves = lax.axis_size("leaf")
    leaf_index = lax.axis_index("leaf")
    forces = jnp.einsum("fij,fj->fi", fibre_solve, fibre_rhs, preferred_element_type=jnp.float32)
    owner_box = fibre_owner[:, 0]
    records = place_records(forces, fibre_points, owner_box, leaf_index)
    owner_hot = (owner_box[:, None] == jnp.arange(octants, dtype=jnp.int32)[None, :]).astype(
        jnp.float32
    )
    partial_value = jnp.dot(
        owner_hot.T, jnp.sum(records[:, 3:7], axis=2), precision=lax.Precision.HIGHEST
    )
    dens_all = lax.all_gather(density.astype(jnp.bfloat16), ("leaf", "oct"), axis=0, tiled=True)
    partial_all = lax.all_gather(partial_value[None], ("leaf", "oct"), axis=0, tiled=True)
    moments = jnp.sum(partial_all.reshape(leaves, octants, octants, 4), axis=1).reshape(
        leaves * octants, 4
    )
    shell_product = jnp.einsum(
        "cpk,k->cp", shell_block, dens_all, preferred_element_type=jnp.float32
    )
    zero_ints = 0 * shell_points[0].astype(jnp.int32)
    shell_corner = jnp.stack([2 * leaf_index + zero_ints, zero_ints, zero_ints]).astype(jnp.float32)
    shell_abs = 2.0 * shell_points + shell_corner
    box_id = jnp.arange(leaves * octants, dtype=jnp.int32)
    box_leaf = box_id // 8
    child_box = box_id % 8
    centres = (
        jnp.stack([2 * box_leaf + child_box % 2, child_box // 2 % 2, child_box // 4]).astype(
            jnp.float32
        )
        + 0.5
    )
    far_mask = (jnp.abs(box_leaf - leaf_index) >= 2).astype(jnp.float32)
    far_sources = jnp.concatenate([centres, moments.T * far_mask[None, :]], axis=0)
    own_total = fib_count * node_count
    own_records = records.transpose(1, 0, 2).reshape(7, own_total)
    targets = jnp.concatenate([own_records[0:3], shell_abs], axis=1)
    column = with_halo(own_records[None], (("leaf", 0),), 1)
    flow_sum = near_flow(targets, column) + stokeslet(targets, far_sources)
    fibre_flow = flow_sum[:, :own_total]
    shell_flow = shell_product + flow_sum[:, own_total:]
    return (fibre_flow, shell_flow)


def solution(mesh):
    placed = (
        P(("leaf", "oct"), None, None),
        P(("leaf", "oct"), None),
        P(("leaf", "oct"), None),
        P(("leaf", "oct"), None),
        P(None, ("leaf", "oct")),
        P(None, ("leaf", "oct"), None),
        P(("leaf", "oct")),
    )
    return jax.shard_map(
        shards,
        mesh=mesh,
        in_specs=placed,
        out_specs=(P(None, ("leaf", "oct")), P(None, ("leaf", "oct"))),
        check_vma=False,
    )
```

profile of v0, /device:TPU:9, one launch (start us, length us, event | category | flops | bytes accessed | tf_op | source)
XLA Modules:
  0.0 349.8 jit_solution(4824190761310288602)
XLA Ops:
  13.9 3.4 collective-permute-start
  18.4 34.4 %all-gather.3 = f32[32,8,4]{1,2,0:T(4,128)S(1)} all-gather(f32[1,8,4]{1,2,0:T(4,128)S(1)} %convolution_bitcast_fusion), channel_id=3, replica_groups=mesh['leaf'=4,'oct'=8] {'leaf','oct'}, dimensions={0}, use_global_device_ids=true | all-gather | bytes 4224 | tf_op jit(solution)/shard_map/all_gather | solution.py:84
  53.0 37.2 %all_gather.11 = bf16[98304]{0:T(1024)(128)(2,1)S(1)} all-gather(bf16[3072]{0:T(1024)(128)(2,1)S(1)} %convert_element_type.33), channel_id=1, replica_groups=mesh['leaf'=4,'oct'=8] {'leaf','oct'}, dimensions={0}, use_global_device_ids=true | all-gather | bytes 202752 | tf_op jit(solution)/shard_map/all_gather | solution.py:83
  90.4 8.4 %fusion.105 = f32[1,3,4]{2,0,1:T(1,128)S(1)} fusion(bf16[3,4,98304]{2,1,0:T(4,128)(2,1)S(1)} %copy-done, bf16[98304,1,1]{0,1,2:T(2,128)(2,1)S(1)} %reshape.403), kind=kOutput, calls=%fused_computation.159 | convolution fusion | flops 2359296 | bytes 2555952 | tf_op jit(solution)/shard_map/cpk,k->cp/dot_general | solution.py:88
  99.1 9.4 %all-gather.2 = f32[8,3,772]{2,1,0:T(4,128)S(1)} all-gather(f32[1,3,772]{2,1,0:T(4,128)S(1)} %get-tuple-element.93), channel_id=2, replica_groups=mesh['leaf'=4,'oct'=8] {'oct'}, dimensions={0}, use_global_device_ids=true | all-gather | bytes 83376 | tf_op jit(solution)/shard_map/all_gather | solution.py:57
  108.5 175.6 %while.10 = (s32[]{:T(128)}, f32[8,3,772]{2,1,0:T(4,128)S(1)}, f32[8,3,772]{2,1,0:T(4,128)S(1)}, f32[1,7,768]{2,1,0:T(8,128)S(1)}, f32[7,12,64]{2,1,0:T(8,128)S(1)}, /*index=5*/f32[1,7,768]{2,1,0:T(8,128)S(1)}, s32[]{:T(128)}) while((s32[]{:T(128)}, f32[8,3,772]{2,1,0:T(4,128)S(1)}, f32[8,3,772]{2,1,0:T(4,128)S(1)}, ...), condition=%wide.region_10.11_spmd, body=%wide.region_0.10_spmd.sunk | while | flops 120957728 | bytes 50303692 | solution.py:65
  109.0 3.4 fusion.127
  127.3 3.3 fusion.134
  131.0 3.4 fusion.127
  149.3 3.3 fusion.134
  152.9 3.4 fusion.127
  171.2 3.3 fusion.134
  174.8 3.4 fusion.127
  193.1 3.3 fusion.134
  196.8 3.4 fusion.127
  215.1 3.3 fusion.134
  218.7 3.4 fusion.127
  233.7 3.3 fusion.133
  237.0 3.3 fusion.134
  240.7 3.4 fusion.127
  258.9 3.3 fusion.134
  262.6 3.4 fusion.127
  280.9 3.3 fusion.134
  285.6 54.6 %all-reduce.4.cloned.1.call-done = f32[8,3,772]{2,1,0:T(4,128)} async-done(((f32[8,3,772]{2,1,0:T(4,128)}), f32[8,3,772]{2,1,0:T(4,128)}) %all-reduce.4.cloned.1.call-update) | async-done | bytes 74128
  (182 shorter events, 130.6 us)
Async XLA Ops:
  7.2 83.3 %copy-start = (bf16[3,4,98304]{2,1,0:T(4,128)(2,1)S(1)}, bf16[3,4,98304]{2,1,0:T(4,128)(2,1)}, u32[]{:S(2)}) copy-start(bf16[3,4,98304]{2,1,0:T(4,128)(2,1)} %param.14) | copy-start | bytes 7077892
  7.2 11.1 %copy-start.3 = (s32[12,1]{0,1:T(1,128)S(1)}, s32[12,1]{0,1:T(1,128)}, u32[]{:S(2)}) copy-start(s32[12,1]{0,1:T(1,128)} %param.12) | copy-start | bytes 148
  7.2 83.2 %copy-start.2 = (f32[3,4]{1,0:T(4,128)S(1)}, f32[3,4]{1,0:T(4,128)}, u32[]{:S(2)}) copy-start(f32[3,4]{1,0:T(4,128)} %param.13) | copy-start | bytes 148
  7.2 333.0 %all-reduce.4.cloned.1.call-start = ((), (), s32[]{:S(2)}) async-start(), calls=%async_computation | async-start | bytes 229376
  12.0 96.5 %collective-permute-start.1 = (f32[1,7,768]{2,1,0:T(8,128)S(1)}, f32[1,7,768]{2,1,0:T(8,128)S(1)}, u32[]{:S(2)}, u32[]{:S(2)}) collective-permute-start(f32[1,7,768]{2,1,0:T(8,128)S(1)} %broadcast_in_dim_reshape.3), channel_id=1, source_target_pairs={{8,0},{16,8},{24,16},{9,1},{17,9},{25,17},{10,2},{18,10},{26,18},{... | collective-permute-start | bytes 64520 | tf_op jit(solution)/shard_map/ppermute | solution.py:22
  13.9 94.6 %collective-permute-start = (f32[1,7,768]{2,1,0:T(8,128)S(1)}, f32[1,7,768]{2,1,0:T(8,128)S(1)}, u32[]{:S(2)}, u32[]{:S(2)}) collective-permute-start(f32[1,7,768]{2,1,0:T(8,128)S(1)} %broadcast_in_dim_reshape.3), channel_id=1, source_target_pairs={{0,8},{8,16},{16,24},{1,9},{9,17},{17,25},{2,10},{10,18},{18,26},{... | collective-permute-start | bytes 64520 | tf_op jit(solution)/shard_map/ppermute | solution.py:20
  108.5 176.5 %copy-start.4 = (u32[32]{0:T(128)S(1)}, u32[32]{0:T(128)}, u32[]{:S(2)}) copy-start(u32[32]{0:T(128)} %constant.146) | copy-start | bytes 388
  284.2 0.6 copy-start.1
Sparse Core Ops, SparseCore 0:
  285.0 55.1 all-reduce.3
where the time goes:
time: 351 us; the launch traced here: 350 us
  other arithmetic  97.3 us (28%)
  matrix products  90.8 us (26%)
  blocking collectives  81 us (23%)
  waiting for transfers between devices  54.6 us (16%)
  between operations  14.2 us (4%)
  local copies, waits for them, and re-layouts  5.6 us (2%)
  starting transfers between devices  5.31 us (2%)
    dot_general x25, matrix products, stokeslet(): jnp.einsum('ts,cs->ct', direct, forces, precision=lax.Precision.HIGHEST)  80.4 us
    reduce_sum x25, other arithmetic, stokeslet(): dist_sq = jnp.sum(offset * offset, axis=0)  62.2 us
    unnamed x2, waiting for transfers between devices  54.6 us
    all_gather x1, blocking collectives, shards(): lax.all_gather(density.astype(jnp.bfloat16), ('leaf', 'oct'), axis=0, til...  37.2 us
    all_gather x1, blocking collectives, shards(): lax.all_gather(partial_value[None], ('leaf', 'oct'), axis=0, tiled=True)  34.4 us
    mul x25, other arithmetic, stokeslet(): pointing = jnp.sum(offset * (weight * projected)[None], axis=2)  23.3 us
    all_gather x1, blocking collectives, near_flow(): spread = lax.all_gather(targets[None], 'oct', axis=0, tiled=True)  9.41 us
    reduce_sum x9, other arithmetic, stokeslet(): pointing = jnp.sum(offset * (weight * projected)[None], axis=2)  8.46 us
  transfers between devices with their start and end apart: 3, of which 1 were waited for; matrix products, arithmetic and copies ran while one was open for 3% of the time, Pallas kernels for 0%

commit v1 on v0

v1 whole, which is shorter than its diff:
```python
import functools
import math

import jax
import jax.numpy as jnp
from jax import lax
from jax.experimental import pallas as pl
from jax.experimental.pallas import tpu as pltpu
from jax.sharding import PartitionSpec as P

smooth_sq = 0.01
stokes_scale = 1.0 / (8.0 * math.pi)
F32 = jnp.float32
BF16 = jnp.bfloat16
VMEM = pl.BlockSpec(memory_space=pltpu.VMEM)
PARAMS = pltpu.CompilerParams(vmem_limit_bytes=40 * 2**20)


def split3(value):
    high = value.astype(BF16).astype(F32)
    rest = value - high
    middle = rest.astype(BF16).astype(F32)
    return high, middle, (rest - middle).astype(BF16).astype(F32)


def prepare_kernel(solve_ref, rhs_ref, points_ref, owner_ref, density_ref, record_ref, extra_ref):
    fibres, quads = rhs_ref.shape
    nodes = quads // 4
    width = record_ref.shape[1]
    rhs = rhs_ref[...]
    row = lax.broadcasted_iota(jnp.int32, (fibres, quads), 0)
    forces = jnp.zeros((fibres, quads), F32)
    for f in range(fibres):
        product = lax.dot_general(
            rhs, solve_ref[f], (((1,), (1,)), ((), ())), preferred_element_type=F32
        )
        forces = jnp.where(row == f, product, forces)
    points = points_ref[...]
    quad_weight = points[:, 3 * nodes :]
    pushes = forces * jnp.concatenate([quad_weight] * 4, axis=1)
    owner = owner_ref[...]
    corner = [owner % 2, owner // 2 % 2, owner // 4]
    place = [
        points[:, c * nodes : (c + 1) * nodes] + (corner[c].astype(F32) - 1.0) for c in range(3)
    ]
    record_ref[3:4, :] = jnp.zeros((1, width), F32)
    for f in range(fibres):
        lanes = slice(f * nodes, (f + 1) * nodes)
        for c in range(3):
            record_ref[c : c + 1, lanes] = place[c][f : f + 1, :]
        for c in range(4):
            record_ref[4 + c : 5 + c, lanes] = pushes[f : f + 1, c * nodes : (c + 1) * nodes]
    lane = lax.broadcasted_iota(jnp.int32, (fibres, width), 1)
    owned = lane == owner + 8 * lax.axis_index("leaf")
    for c in range(4):
        box_sum = jnp.sum(pushes[:, c * nodes : (c + 1) * nodes], axis=1, keepdims=True)
        extra_ref[c : c + 1, :] = jnp.sum(jnp.where(owned, box_sum, 0.0), axis=0, keepdims=True)
    rows = density_ref.shape[0]
    extra_ref[4 : 4 + rows, :] = density_ref[...].astype(BF16).astype(F32)


def prepare(fibre_solve, fibre_rhs, fibre_points, fibre_owner, density_rows):
    width = fibre_points.shape[0] * fibre_points.shape[1] // 4
    extra_rows = 4 + density_rows.shape[0]
    return pl.pallas_call(
        prepare_kernel,
        out_shape=(
            jax.ShapeDtypeStruct((8, width), F32),
            jax.ShapeDtypeStruct((extra_rows, width), F32),
        ),
        in_specs=[VMEM] * 5,
        out_specs=(VMEM, VMEM),
        compiler_params=PARAMS,
        name="prepare",
    )(fibre_solve, fibre_rhs, fibre_points, fibre_owner, density_rows)


def target_rows(place):
    sq = jnp.sum(place * place, axis=0, keepdims=True)
    high, middle, low = split3(place)
    one = jnp.ones_like(sq)
    zero = jnp.zeros_like(sq)
    sq_parts = split3(sq)
    return jnp.concatenate(
        [-2.0 * high, one] * 3
        + [-2.0 * middle, zero] * 2
        + [-2.0 * low, zero]
        + list(sq_parts)
        + [zero] * 5,
        axis=0,
    ).astype(BF16)


def source_rows(place):
    sq = jnp.sum(place * place, axis=0, keepdims=True) + smooth_sq
    high, middle, low = split3(jnp.concatenate([place, sq], axis=0))
    one = jnp.ones((3, place.shape[1]), F32)
    zero = jnp.zeros((5, place.shape[1]), F32)
    return jnp.concatenate([high, middle, low, high, middle, high, one, zero], axis=0).astype(BF16)


def source_terms(place, push, source):
    sq = jnp.sum(place * place, axis=0, keepdims=True) + 2.0 * smooth_sq
    rest = source - jnp.sum(place * push, axis=0, keepdims=True)
    terms = jnp.concatenate(
        [push, rest, sq * push - rest * place] + [place[a : a + 1] * push for a in range(3)], axis=0
    )
    return jnp.concatenate(split3(terms), axis=0).astype(BF16)


def add_sources(target_ref, rows, terms, total_ref, block):
    targets = target_ref.shape[1]
    width = rows.shape[1]
    step = min(block, width)
    for t in range(0, targets, block):
        total = None
        for s in range(0, width, step):
            d = lax.dot_general(
                rows[:, s : s + step],
                target_ref[:, t : t + block],
                (((0,), (0,)), ((), ())),
                preferred_element_type=F32,
            )
            inverse = lax.rsqrt(d)
            cube = inverse * inverse * inverse
            high = cube.astype(BF16)
            low = (cube - high.astype(F32)).astype(BF16)
            term = terms[:, s : s + step]
            part = jnp.dot(
                jnp.concatenate([term, term], axis=1),
                jnp.concatenate([high, low], axis=0),
                preferred_element_type=F32,
            )
            total = part if total is None else total + part
        total_ref[:, t : t + block] += total


def point_columns(points):
    count = points.shape[1]
    eye = lax.broadcasted_iota(jnp.int32, (count, count), 0) == lax.broadcasted_iota(
        jnp.int32, (count, count), 1
    )
    return [
        2.0 * jnp.sum(jnp.where(eye, points[c : c + 1], 0.0), axis=1, keepdims=True) - 1.0
        for c in range(3)
    ]


def direct(columns, place, push, source):
    offset = [columns[c] - place[c : c + 1] for c in range(3)]
    sq = offset[0] * offset[0] + offset[1] * offset[1] + offset[2] * offset[2]
    inverse = lax.rsqrt(sq + smooth_sq)
    cube = inverse * inverse * inverse
    along = source + (
        offset[0] * push[0:1] + offset[1] * push[1:2] + offset[2] * push[2:3]
    )
    spread = cube * (sq + 2.0 * smooth_sq)
    along = cube * along
    return [spread * push[c : c + 1] + along * offset[c] for c in range(3)]


def fold(value, lanes):
    total = value[:, :lanes]
    for at in range(lanes, value.shape[1], lanes):
        total = total + value[:, at : at + lanes]
    return total


def near_kernel(shift, first, *refs):
    if first:
        records_ref, own_ref, shell_ref, total_ref, shell_total_ref, target_ref, sum_ref = refs
    else:
        (records_ref, own_ref, shell_ref, total_in, shell_in) = refs[:5]
        total_ref, shell_total_ref, target_ref, sum_ref = refs[5:]
    target_ref[...] = target_rows(own_ref[0:3, :])
    sum_ref[...] = jnp.zeros_like(sum_ref)
    if first:
        shell_total_ref[...] = jnp.zeros_like(shell_total_ref)
    else:
        shell_total_ref[...] = shell_in[...]
    columns = point_columns(shell_ref[...])

    def body(j, carry):
        record = records_ref[j]
        place = record[0:3]
        if shift:
            axis = lax.broadcasted_iota(jnp.int32, place.shape, 0)
            place = place + jnp.where(axis == 0, float(shift), 0.0)
        push, source = record[4:7], record[7:8]
        add_sources(target_ref, source_rows(place), source_terms(place, push, source), sum_ref, 256)
        for c, value in enumerate(direct(columns, place, push, source)):
            shell_total_ref[c] += fold(value, 128)
        return carry

    lax.fori_loop(0, records_ref.shape[0], body, 0)
    terms = sum_ref.shape[0] // 3
    total = sum_ref[0:terms] + sum_ref[terms : 2 * terms] + sum_ref[2 * terms :]
    total_ref[...] = total if first else total + total_in[...]


def near(records, own, shell_points, shift, totals):
    targets = own.shape[1]
    count = shell_points.shape[1]
    out = (
        jax.ShapeDtypeStruct((16, targets), F32),
        jax.ShapeDtypeStruct((3, count, 128), F32),
    )
    pairs = records.shape[0] * records.shape[2] * targets
    return pl.pallas_call(
        functools.partial(near_kernel, shift, totals is None),
        out_shape=out,
        in_specs=[VMEM] * (3 if totals is None else 5),
        out_specs=(VMEM, VMEM),
        scratch_shapes=[pltpu.VMEM((32, targets), BF16), pltpu.VMEM((48, targets), F32)],
        compiler_params=PARAMS,
        cost_estimate=pl.CostEstimate(
            flops=500 * pairs, bytes_accessed=records.size * 4, transcendentals=pairs
        ),
        name="near",
    )(records, own, shell_points, *(totals or ()))


def finish_kernel(
    leaves,
    octants,
    own_ref,
    shell_ref,
    extras_ref,
    block_ref,
    total_in,
    shell_in,
    flow_ref,
    shell_flow_ref,
    target_ref,
    sum_ref,
):
    leaf, octant = lax.axis_index("leaf"), lax.axis_index("oct")
    width = extras_ref.shape[2]
    moments = jnp.zeros((4, width), F32)
    for at in range(leaves * octants):
        moments = moments + extras_ref[at, 0:4, :]
    boxes = -(-leaves * 8 // 128) * 128
    moments = moments[:, :boxes]
    box = lax.broadcasted_iota(jnp.int32, (1, boxes), 1)
    away = box // 8 - leaf
    far = (jnp.abs(away) >= 2) & (box < leaves * 8)
    child = box % 8
    place = jnp.concatenate(
        [
            (2 * away + child % 2).astype(F32) - 0.5,
            (child // 2 % 2).astype(F32) - 0.5,
            (child // 4).astype(F32) - 0.5,
        ],
        axis=0,
    )
    push = jnp.where(far, moments[0:3], 0.0)
    source = jnp.where(far, moments[3:4], 0.0)
    x = own_ref[0:3, :]
    target_ref[...] = target_rows(x)
    sum_ref[...] = jnp.zeros_like(sum_ref)
    add_sources(target_ref, source_rows(place), source_terms(place, push, source), sum_ref, 256)
    terms = sum_ref.shape[0] // 3
    total = total_in[...] + (
        sum_ref[0:terms] + sum_ref[terms : 2 * terms] + sum_ref[2 * terms :]
    )
    push_sum, rest_sum, constant = total[0:3], total[3:4], total[4:7]
    cross = [total[7 + 3 * a : 10 + 3 * a] for a in range(3)]
    flow = (
        jnp.sum(x * x, axis=0, keepdims=True) * push_sum
        + constant
        + x * (jnp.sum(x * push_sum, axis=0, keepdims=True) + rest_sum)
    )
    for a in range(3):
        flow = flow - 2.0 * x[a : a + 1] * cross[a]
    turned = [
        jnp.sum(x * cross[c], axis=0, keepdims=True) for c in range(3)
    ]
    flow_ref[...] = stokes_scale * (flow - jnp.concatenate(turned, axis=0))
    columns = point_columns(shell_ref[...])
    shell = [
        jnp.sum(shell_in[c] + fold(value, 128), axis=1, keepdims=True)
        for c, value in enumerate(direct(columns, place, push, source))
    ]
    rows = extras_ref.shape[1] - 4
    count = block_ref.shape[1]

    def body(at, sums):
        owner = ((at // octants) ^ leaf) * octants + ((at % octants) ^ octant)
        for r in range(rows):
            start = pl.multiple_of((owner * rows + r) * width, 128)
            dens = extras_ref[at, 4 + r : 5 + r, :]
            sums = tuple(
                sums[c] + block_ref[c, :, pl.ds(start, width)].astype(F32) * dens for c in range(3)
            )
        return sums

    zero = jnp.zeros((count, width), F32)
    sums = lax.fori_loop(0, leaves * octants, body, (zero, zero, zero))
    product = [jnp.sum(sums[c], axis=1, keepdims=True) for c in range(3)]
    eye = lax.broadcasted_iota(jnp.int32, (count, count), 0) == lax.broadcasted_iota(
        jnp.int32, (count, count), 1
    )
    for c in range(3):
        column = product[c] + stokes_scale * shell[c]
        shell_flow_ref[c : c + 1, :] = jnp.sum(jnp.where(eye, column, 0.0), axis=0, keepdims=True)


def finish(leaves, octants, own, shell_points, extras, shell_block, totals):
    targets = own.shape[1]
    return pl.pallas_call(
        functools.partial(finish_kernel, leaves, octants),
        out_shape=(
            jax.ShapeDtypeStruct((3, targets), F32),
            jax.ShapeDtypeStruct(shell_points.shape, F32),
        ),
        in_specs=[VMEM] * 6,
        out_specs=(VMEM, VMEM),
        scratch_shapes=[pltpu.VMEM((32, targets), BF16), pltpu.VMEM((48, targets), F32)],
        compiler_params=PARAMS,
        name="finish",
    )(own, shell_points, extras, shell_block, *totals)


def exchange(value, axis, bit):
    count = lax.axis_size(axis)
    return lax.ppermute(value, axis, [(i, i ^ bit) for i in range(count)])


def gather(value, axis, bits):
    for bit in bits:
        value = jnp.concatenate([value, exchange(value, axis, bit)], axis=0)
    return value


def shards(fibre_solve, fibre_rhs, fibre_points, fibre_owner, shell_points, shell_block, density):
    octants = lax.axis_size("oct")
    leaves = lax.axis_size("leaf")
    width = fibre_points.shape[0] * fibre_points.shape[1] // 4
    record, extra = prepare(
        fibre_solve, fibre_rhs, fibre_points, fibre_owner, density.reshape(-1, width)
    )
    octant_bits = [1 << b for b in range(octants.bit_length() - 1)]
    leaf_bits = [1 << b for b in range(leaves.bit_length() - 1)]
    records = gather(record[None], "oct", octant_bits)
    extras = gather(extra[None], "oct", octant_bits)
    from_left = lax.ppermute(records, "leaf", [(i, i + 1) for i in range(leaves - 1)])
    from_right = lax.ppermute(records, "leaf", [(i + 1, i) for i in range(leaves - 1)])
    extras = gather(extras, "leaf", leaf_bits)
    totals = near(records, record, shell_points, 0, None)
    totals = near(from_left, record, shell_points, -2, totals)
    totals = near(from_right, record, shell_points, 2, totals)
    return finish(leaves, octants, record, shell_points, extras, shell_block, totals)


def solution(mesh):
    placed = (
        P(("leaf", "oct"), None, None),
        P(("leaf", "oct"), None),
        P(("leaf", "oct"), None),
        P(("leaf", "oct"), None),
        P(None, ("leaf", "oct")),
        P(None, ("leaf", "oct"), None),
        P(("leaf", "oct")),
    )
    return jax.shard_map(
        shards,
        mesh=mesh,
        in_specs=placed,
        out_specs=(P(None, ("leaf", "oct")), P(None, ("leaf", "oct"))),
        check_vma=False,
    )
```

time: 351 us -> 56.8 us (0.16)
  the two profiles are of different devices: /device:TPU:9 before, /device:TPU:0 now
where the time goes in v1:
time: 56.8 us; the launch traced here: 56.4 us
  Pallas kernels  29.4 us (52%)
  starting transfers between devices  15.8 us (28%)
  waiting for transfers between devices  5.93 us (10%)
  local copies, waits for them, and re-layouts  4.39 us (8%)
  between operations  0.78 us (1%)
    pallas_call x3, Pallas kernels, near(): pl.pallas_call(functools.partial(near_kernel, shift, totals is None), out...  26.6 us
    ppermute x8, starting transfers between devices, exchange(): return lax.ppermute(value, axis, [(i, i ^ bit) for i in range(count)])  9.99 us
    ppermute x8, waiting for transfers between devices, exchange(): return lax.ppermute(value, axis, [(i, i ^ bit) for i in range(count)])  5.93 us
    ppermute x1, starting transfers between devices, shards(): lax.ppermute(records, 'leaf', [(i, i + 1) for i in range(leaves - 1)])  4.56 us
    unnamed x15, local copies, waits for them, and re-layouts  3.61 us
    pallas_call x1, Pallas kernels, finish(): pl.pallas_call(functools.partial(finish_kernel, leaves, octants), out_sha...  2.07 us
    ppermute x1, starting transfers between devices, shards(): lax.ppermute(records, 'leaf', [(i + 1, i) for i in range(leaves - 1)])  1.29 us
  transfers between devices with their start and end apart: 10, of which 3 were waited for; matrix products, arithmetic and copies ran while one was open for 0% of the time, Pallas kernels for 47%

profile of v1, /device:TPU:0, one launch (start us, length us, event | category | flops | bytes accessed | tf_op | source)
XLA Modules:
  0.0 56.4 jit_solution(11502396916190411045)
XLA Ops:
  0.6 0.7 %copy.9.owner_ref = s32[12,1]{1,0:T(8,128)S(1)} copy(s32[12,1]{0,1:T(1,128)} %param.10) | data formatting | bytes 96 | tf_op args[3]
  1.4 0.7 %reshape.7.density_ref = f32[4,768]{1,0:T(4,128)S(1)} reshape(f32[3072]{0:T(1024)} %param.13) | data formatting | bytes 24576 | tf_op jit(solution)/shard_map/reshape | solution.py:340
  2.1 1.4 %copy-done.1 = bf16[12,256,256]{2,1,0:T(8,128)(2,1)S(1)} copy-done((bf16[12,256,256]{2,1,0:T(8,128)(2,1)S(1)}, bf16[12,256,256]{2,1,0:T(8,128)(2,1)}, u32[]{:S(2)}) %copy-start.1) | copy-done | bytes 1572888
  3.5 0.7 %copy-done.2 = f32[12,256]{1,0:T(8,128)S(1)} copy-done((f32[12,256]{1,0:T(8,128)S(1)}, f32[12,256]{1,0:T(8,128)}, u32[]{:S(2)}) %copy-start.2) | copy-done | bytes 12312
  4.2 0.7 %copy-done.3 = bf16[12,256]{1,0:T(8,128)(2,1)S(1)} copy-done((bf16[12,256]{1,0:T(8,128)(2,1)S(1)}, bf16[12,256]{1,0:T(8,128)(2,1)}, u32[]{:S(2)}) %copy-start.3) | copy-done | bytes 6168
  4.9 0.7 %prepare.1 = (f32[8,768]{1,0:T(8,128)S(1)}, f32[8,768]{1,0:T(8,128)S(1)}) custom-call(bf16[12,256,256]{2,1,0:T(8,128)(2,1)S(1)} %copy-done.1, bf16[12,256]{1,0:T(8,128)(2,1)S(1)} %copy-done.3, f32[12,256]{1,0:T(8,128)S(1)} %copy-done.2, s32[12,1]{1,0:T(8,128)S(1)} %copy.9.owner_ref, f32[4,768]{1,0:T(4,128)S(1)} %reshape.7.density_ref), custom_call_target="tpu_custom_call" | custom-call | tf_op jit(solution)/shard_map/prepare/pallas_call | solution.py:65
  5.6 0.5 collective-permute-start
  6.1 0.1 collective-permute-start.5
  6.2 0.8 %collective-permute-done = f32[1,8,768]{2,1,0:T(8,128)S(1)} collective-permute-done((f32[1,8,768]{2,1,0:T(8,128)S(1)}, f32[1,8,768]{2,1,0:T(8,128)S(1)}, u32[]{:S(2)}, u32[]{:S(2)}) %collective-permute-start) | collective-permute-done | bytes 24608 | tf_op jit(solution)/shard_map/ppermute | solution.py:326
  7.0 2.8 %collective-permute-start.1 = (f32[2,8,768]{2,1,0:T(8,128)S(1)}, f32[2,8,768]{2,1,0:T(8,128)S(1)}, u32[]{:S(2)}, u32[]{:S(2)}) collective-permute-start(f32[2,8,768]{2,1,0:T(8,128)S(1)} %pad_maximum_fusion.4), channel_id=1, source_target_pairs={{0,2},{1,3},{2,0},{3,1},{4,6},{5,7},{6,4},{7,5},{8,10},{9,11},{10,... | collective-permute-start | bytes 147464 | tf_op jit(solution)/shard_map/ppermute | solution.py:326
  9.8 0.2 collective-permute-start.6
  10.0 1.9 %collective-permute-done.1 = f32[2,8,768]{2,1,0:T(8,128)S(1)} collective-permute-done((f32[2,8,768]{2,1,0:T(8,128)S(1)}, f32[2,8,768]{2,1,0:T(8,128)S(1)}, u32[]{:S(2)}, u32[]{:S(2)}) %collective-permute-start.1) | collective-permute-done | bytes 49184 | tf_op jit(solution)/shard_map/ppermute | solution.py:326
  11.9 2.2 %collective-permute-start.2 = (f32[4,8,768]{2,1,0:T(8,128)S(1)}, f32[4,8,768]{2,1,0:T(8,128)S(1)}, u32[]{:S(2)}, u32[]{:S(2)}) collective-permute-start(f32[4,8,768]{2,1,0:T(8,128)S(1)} %pad_maximum_fusion.2), channel_id=1, source_target_pairs={{0,4},{1,5},{2,6},{3,7},{4,0},{5,1},{6,2},{7,3},{8,12},{9,13},{10,... | collective-permute-start | bytes 294920 | tf_op jit(solution)/shard_map/ppermute | solution.py:326
  14.2 1.4 %collective-permute-start.7 = (f32[4,8,768]{2,1,0:T(8,128)S(1)}, f32[4,8,768]{2,1,0:T(8,128)S(1)}, u32[]{:S(2)}, u32[]{:S(2)}) collective-permute-start(f32[4,8,768]{2,1,0:T(8,128)S(1)} %pad_maximum_fusion.3), channel_id=1, source_target_pairs={{0,4},{1,5},{2,6},{3,7},{4,0},{5,1},{6,2},{7,3},{8,12},{9,13},{10,... | collective-permute-start | bytes 294920 | tf_op jit(solution)/shard_map/ppermute | solution.py:326
  15.6 3.3 %collective-permute-done.7 = f32[4,8,768]{2,1,0:T(8,128)S(1)} collective-permute-done((f32[4,8,768]{2,1,0:T(8,128)S(1)}, f32[4,8,768]{2,1,0:T(8,128)S(1)}, u32[]{:S(2)}, u32[]{:S(2)}) %collective-permute-start.7) | collective-permute-done | bytes 98336 | tf_op jit(solution)/shard_map/ppermute | solution.py:326
  18.9 1.3 %collective-permute-start.8 = (f32[8,8,768]{2,1,0:T(8,128)S(1)}, f32[8,8,768]{2,1,0:T(8,128)S(1)}, u32[]{:S(2)}, u32[]{:S(2)}) collective-permute-start(f32[8,8,768]{2,1,0:T(8,128)S(1)} %pad_maximum_fusion.1.refs_0_), channel_id=1, source_target_pairs={{8,0},{16,8},{24,16},{9,1},{17,9},{25,17},{10,2},{18,10},{26,18},{... | collective-permute-start | bytes 589832 | tf_op jit(solution)/shard_map/ppermute | solution.py:347
  20.2 4.6 %collective-permute-start.9 = (f32[8,8,768]{2,1,0:T(8,128)S(1)}, f32[8,8,768]{2,1,0:T(8,128)S(1)}, u32[]{:S(2)}, u32[]{:S(2)}) collective-permute-start(f32[8,8,768]{2,1,0:T(8,128)S(1)} %pad_maximum_fusion.1.refs_0_), channel_id=1, source_target_pairs={{0,8},{8,16},{16,24},{1,9},{9,17},{17,25},{2,10},{10,18},{18,26},{... | collective-permute-start | bytes 589832 | tf_op jit(solution)/shard_map/ppermute | solution.py:346
  24.8 1.6 %collective-permute-start.3 = (f32[8,8,768]{2,1,0:T(8,128)S(1)}, f32[8,8,768]{2,1,0:T(8,128)S(1)}, u32[]{:S(2)}, u32[]{:S(2)}) collective-permute-start(f32[8,8,768]{2,1,0:T(8,128)S(1)} %pad_maximum_fusion), channel_id=1, source_target_pairs={{0,8},{8,0},{16,24},{24,16},{1,9},{9,1},{17,25},{25,17},{2,10},{10... | collective-permute-start | bytes 589832 | tf_op jit(solution)/shard_map/ppermute | solution.py:326
  26.4 8.9 %near.3 = (f32[16,768]{1,0:T(8,128)S(1)}, f32[3,4,128]{2,1,0:T(4,128)S(1)}) custom-call(f32[8,8,768]{2,1,0:T(8,128)S(1)} %pad_maximum_fusion.1.refs_0_, f32[8,768]{1,0:T(8,128)S(1)} %get-tuple-element.10.refs_1_.own_ref, f32[3,4]{1,0:T(4,128)S(1)} %copy-done.4), custom_call_target="tpu_custom_call" | custom-call | flops 2359296000 | bytes 196608 | tf_op jit(solution)/shard_map/near/pallas_call | solution.py:209
  35.3 1.1 %collective-permute-start.4 = (f32[16,8,768]{2,1,0:T(8,128)S(1)}, f32[16,8,768]{2,1,0:T(8,128)S(1)}, u32[]{:S(2)}, u32[]{:S(2)}) collective-permute-start(f32[16,8,768]{2,1,0:T(8,128)S(1)} %get-tuple-element.18), channel_id=1, source_target_pairs={{0,16},{8,24},{16,0},{24,8},{1,17},{9,25},{17,1},{25,9},{2,18},{10... | collective-permute-start | bytes 1179656 | tf_op jit(solution)/shard_map/ppermute | solution.py:326
  36.5 8.9 %near.4 = (f32[16,768]{1,0:T(8,128)S(1)}, f32[3,4,128]{2,1,0:T(4,128)S(1)}) custom-call(f32[8,8,768]{2,1,0:T(8,128)S(1)} %collective-permute-done.9.refs_0_, f32[8,768]{1,0:T(8,128)S(1)} %get-tuple-element.10.refs_1_.own_ref, f32[3,4]{1,0:T(4,128)S(1)} %copy-done.4, f32[16,768]{1,0:T(8,128)S(1)} %get-tuple-element.12.refs_3_, ...), custom_call_target="tpu_custom_call" | custom-call | flops 2359296000 | bytes 196608 | tf_op jit(solution)/shard_map/near/pallas_call | solution.py:209
  45.3 0.0 copy-start
  45.4 8.9 %near.5 = (f32[16,768]{1,0:T(8,128)S(1)}, f32[3,4,128]{2,1,0:T(4,128)S(1)}) custom-call(f32[8,8,768]{2,1,0:T(8,128)S(1)} %collective-permute-done.8.refs_0_, f32[8,768]{1,0:T(8,128)S(1)} %get-tuple-element.10.refs_1_.own_ref, f32[3,4]{1,0:T(4,128)S(1)} %copy-done.4, f32[16,768]{1,0:T(8,128)S(1)} %get-tuple-element.14.refs_3_, ...), custom_call_target="tpu_custom_call" | custom-call | flops 2359296000 | bytes 196608 | tf_op jit(solution)/shard_map/near/pallas_call | solution.py:209
  54.3 2.1 %finish.1 = (f32[3,768]{1,0:T(4,128)}, f32[3,4]{1,0:T(4,128)}) custom-call(f32[8,768]{1,0:T(8,128)S(1)} %get-tuple-element.10.refs_1_.own_ref, f32[3,4]{1,0:T(4,128)S(1)} %copy-done.4, f32[32,8,768]{2,1,0:T(8,128)S(1)} %constant_dynamic-update-slice_fusion.5.extras_ref, bf16[3,4,98304]{2,1,0:T(4,128)(2,1)S(1)} %copy-done, ...), custom_call_target="tpu_custom_call" | custom-call | tf_op jit(solution)/shard_map/finish/pallas_call | solution.py:310
  (25 shorter events, 0.2 us)
Async XLA Ops:
  0.6 25.8 %copy-start.4 = (f32[3,4]{1,0:T(4,128)S(1)}, f32[3,4]{1,0:T(4,128)}, u32[]{:S(2)}) copy-start(f32[3,4]{1,0:T(4,128)} %shell_ref.1) | copy-start | bytes 148
  2.1 1.4 %copy-start.1 = (bf16[12,256,256]{2,1,0:T(8,128)(2,1)S(1)}, bf16[12,256,256]{2,1,0:T(8,128)(2,1)}, u32[]{:S(2)}) copy-start(bf16[12,256,256]{2,1,0:T(8,128)(2,1)} %solve_ref.1) | copy-start | bytes 4718596
  3.5 0.7 %copy-start.2 = (f32[12,256]{1,0:T(8,128)S(1)}, f32[12,256]{1,0:T(8,128)}, u32[]{:S(2)}) copy-start(f32[12,256]{1,0:T(8,128)} %points_ref.1) | copy-start | bytes 36868
  4.2 0.7 %copy-start.3 = (bf16[12,256]{1,0:T(8,128)(2,1)S(1)}, bf16[12,256]{1,0:T(8,128)(2,1)}, u32[]{:S(2)}) copy-start(bf16[12,256]{1,0:T(8,128)(2,1)} %rhs_ref.1) | copy-start | bytes 18436
  5.6 1.4 %collective-permute-start = (f32[1,8,768]{2,1,0:T(8,128)S(1)}, f32[1,8,768]{2,1,0:T(8,128)S(1)}, u32[]{:S(2)}, u32[]{:S(2)}) collective-permute-start(f32[1,8,768]{2,1,0:T(8,128)S(1)} %bitcast.8), channel_id=1, source_target_pairs={{0,1},{1,0},{2,3},{3,2},{4,5},{5,4},{6,7},{7,6},{8,9},{9,8},{10,11... | collective-permute-start | bytes 73736 | tf_op jit(solution)/shard_map/ppermute | solution.py:326
  6.1 3.7 %collective-permute-start.5 = (f32[1,8,768]{2,1,0:T(8,128)S(1)}, f32[1,8,768]{2,1,0:T(8,128)S(1)}, u32[]{:S(2)}, u32[]{:S(2)}) collective-permute-start(f32[1,8,768]{2,1,0:T(8,128)S(1)} %bitcast.4), channel_id=1, source_target_pairs={{0,1},{1,0},{2,3},{3,2},{4,5},{5,4},{6,7},{7,6},{8,9},{9,8},{10,11... | collective-permute-start | bytes 73736 | tf_op jit(solution)/shard_map/ppermute | solution.py:326
  7.0 4.9 %collective-permute-start.1 = (f32[2,8,768]{2,1,0:T(8,128)S(1)}, f32[2,8,768]{2,1,0:T(8,128)S(1)}, u32[]{:S(2)}, u32[]{:S(2)}) collective-permute-start(f32[2,8,768]{2,1,0:T(8,128)S(1)} %pad_maximum_fusion.4), channel_id=1, source_target_pairs={{0,2},{1,3},{2,0},{3,1},{4,6},{5,7},{6,4},{7,5},{8,10},{9,11},{10,... | collective-permute-start | bytes 147464 | tf_op jit(solution)/shard_map/ppermute | solution.py:326
  9.8 4.3 %collective-permute-start.6 = (f32[2,8,768]{2,1,0:T(8,128)S(1)}, f32[2,8,768]{2,1,0:T(8,128)S(1)}, u32[]{:S(2)}, u32[]{:S(2)}) collective-permute-start(f32[2,8,768]{2,1,0:T(8,128)S(1)} %pad_maximum_fusion.5), channel_id=1, source_target_pairs={{0,2},{1,3},{2,0},{3,1},{4,6},{5,7},{6,4},{7,5},{8,10},{9,11},{10,... | collective-permute-start | bytes 147464 | tf_op jit(solution)/shard_map/ppermute | solution.py:326
  11.9 12.8 %collective-permute-start.2 = (f32[4,8,768]{2,1,0:T(8,128)S(1)}, f32[4,8,768]{2,1,0:T(8,128)S(1)}, u32[]{:S(2)}, u32[]{:S(2)}) collective-permute-start(f32[4,8,768]{2,1,0:T(8,128)S(1)} %pad_maximum_fusion.2), channel_id=1, source_target_pairs={{0,4},{1,5},{2,6},{3,7},{4,0},{5,1},{6,2},{7,3},{8,12},{9,13},{10,... | collective-permute-start | bytes 294920 | tf_op jit(solution)/shard_map/ppermute | solution.py:326
  14.2 4.7 %collective-permute-start.7 = (f32[4,8,768]{2,1,0:T(8,128)S(1)}, f32[4,8,768]{2,1,0:T(8,128)S(1)}, u32[]{:S(2)}, u32[]{:S(2)}) collective-permute-start(f32[4,8,768]{2,1,0:T(8,128)S(1)} %pad_maximum_fusion.3), channel_id=1, source_target_pairs={{0,4},{1,5},{2,6},{3,7},{4,0},{5,1},{6,2},{7,3},{8,12},{9,13},{10,... | collective-permute-start | bytes 294920 | tf_op jit(solution)/shard_map/ppermute | solution.py:326
  18.9 26.5 %collective-permute-start.8 = (f32[8,8,768]{2,1,0:T(8,128)S(1)}, f32[8,8,768]{2,1,0:T(8,128)S(1)}, u32[]{:S(2)}, u32[]{:S(2)}) collective-permute-start(f32[8,8,768]{2,1,0:T(8,128)S(1)} %pad_maximum_fusion.1.refs_0_), channel_id=1, source_target_pairs={{8,0},{16,8},{24,16},{9,1},{17,9},{25,17},{10,2},{18,10},{26,18},{... | collective-permute-start | bytes 589832 | tf_op jit(solution)/shard_map/ppermute | solution.py:347
  20.2 16.3 %collective-permute-start.9 = (f32[8,8,768]{2,1,0:T(8,128)S(1)}, f32[8,8,768]{2,1,0:T(8,128)S(1)}, u32[]{:S(2)}, u32[]{:S(2)}) collective-permute-start(f32[8,8,768]{2,1,0:T(8,128)S(1)} %pad_maximum_fusion.1.refs_0_), channel_id=1, source_target_pairs={{0,8},{8,16},{16,24},{1,9},{9,17},{17,25},{2,10},{10,18},{18,26},{... | collective-permute-start | bytes 589832 | tf_op jit(solution)/shard_map/ppermute | solution.py:346
  24.8 10.5 %collective-permute-start.3 = (f32[8,8,768]{2,1,0:T(8,128)S(1)}, f32[8,8,768]{2,1,0:T(8,128)S(1)}, u32[]{:S(2)}, u32[]{:S(2)}) collective-permute-start(f32[8,8,768]{2,1,0:T(8,128)S(1)} %pad_maximum_fusion), channel_id=1, source_target_pairs={{0,8},{8,0},{16,24},{24,16},{1,9},{9,1},{17,25},{25,17},{2,10},{10... | collective-permute-start | bytes 589832 | tf_op jit(solution)/shard_map/ppermute | solution.py:326
  35.3 18.9 %collective-permute-start.4 = (f32[16,8,768]{2,1,0:T(8,128)S(1)}, f32[16,8,768]{2,1,0:T(8,128)S(1)}, u32[]{:S(2)}, u32[]{:S(2)}) collective-permute-start(f32[16,8,768]{2,1,0:T(8,128)S(1)} %get-tuple-element.18), channel_id=1, source_target_pairs={{0,16},{8,24},{16,0},{24,8},{1,17},{9,25},{17,1},{25,9},{2,18},{10... | collective-permute-start | bytes 1179656 | tf_op jit(solution)/shard_map/ppermute | solution.py:326
  45.3 9.0 %copy-start = (bf16[3,4,98304]{2,1,0:T(4,128)(2,1)S(1)}, bf16[3,4,98304]{2,1,0:T(4,128)(2,1)}, u32[]{:S(2)}) copy-start(bf16[3,4,98304]{2,1,0:T(4,128)(2,1)} %block_ref.1) | copy-start | bytes 7077892

commit v2 on v1

v2 whole, which is shorter than its diff:
```python
import functools
import math

import jax
import jax.numpy as jnp
from jax import lax
from jax.experimental import pallas as pl
from jax.experimental.pallas import tpu as pltpu
from jax.sharding import PartitionSpec as P

smooth_sq = 0.01
stokes_scale = 1.0 / (8.0 * math.pi)
F32 = jnp.float32
BF16 = jnp.bfloat16
VMEM = pl.BlockSpec(memory_space=pltpu.VMEM)
WHOLE = pltpu.CompilerParams(vmem_limit_bytes=64 * 2**20 - 2**17)
PARAMS = pltpu.CompilerParams(vmem_limit_bytes=40 * 2**20)


def split3(value):
    high = value.astype(BF16).astype(F32)
    rest = value - high
    middle = rest.astype(BF16).astype(F32)
    return high, middle, (rest - middle).astype(BF16).astype(F32)


def prepare_kernel(
    solve_hbm,
    rhs_hbm,
    points_hbm,
    owner_hbm,
    density_hbm,
    record_ref,
    dens_ref,
    solve_ref,
    rhs_ref,
    points_ref,
    density_ref,
    owner_ref,
    solve_sem,
    sem,
):
    fibres, quads = rhs_ref.shape
    nodes = quads // 4
    width = record_ref.shape[1]
    copies = [
        pltpu.make_async_copy(owner_hbm, owner_ref, sem.at[0]),
        pltpu.make_async_copy(points_hbm, points_ref, sem.at[1]),
        pltpu.make_async_copy(rhs_hbm, rhs_ref, sem.at[2]),
        pltpu.make_async_copy(density_hbm, density_ref, sem.at[3]),
    ]
    solves = [
        pltpu.make_async_copy(solve_hbm.at[f], solve_ref.at[f], solve_sem.at[f])
        for f in range(fibres)
    ]
    for copy in copies + solves:
        copy.start()
    for copy in copies:
        copy.wait()
    rows = dens_ref.shape[0]
    dens_ref[...] = jnp.concatenate(
        [density_ref[r * width : (r + 1) * width].reshape(1, width) for r in range(rows)], axis=0
    ).astype(BF16)
    row = lax.broadcasted_iota(jnp.int32, (fibres, 1), 0)
    owner = jnp.zeros((fibres, 1), jnp.int32)
    for f in range(fibres):
        owner = jnp.where(row == f, owner_ref[f], owner)
    points = points_ref[...]
    corner = [owner % 2, owner // 2 % 2, owner // 4]
    place = [
        points[:, c * nodes : (c + 1) * nodes] + (corner[c].astype(F32) - 1.0) for c in range(3)
    ]
    for f in range(fibres):
        lanes = slice(f * nodes, (f + 1) * nodes)
        for c in range(3):
            record_ref[c : c + 1, lanes] = place[c][f : f + 1, :]
    quad_weight = points[:, 3 * nodes :]
    rhs = rhs_ref[...]
    forces = jnp.zeros((fibres, quads), F32)
    for f in range(fibres):
        solves[f].wait()
        product = lax.dot_general(
            rhs, solve_ref[f], (((1,), (1,)), ((), ())), preferred_element_type=F32
        )
        forces = jnp.where(row == f, product, forces)
    pushes = forces * jnp.concatenate([quad_weight] * 4, axis=1)
    for f in range(fibres):
        lanes = slice(f * nodes, (f + 1) * nodes)
        for c in range(4):
            record_ref[4 + c : 5 + c, lanes] = pushes[f : f + 1, c * nodes : (c + 1) * nodes]
    lane = lax.broadcasted_iota(jnp.int32, (fibres, width), 1)
    sums = jnp.zeros((fibres, width), F32)
    for c in range(4):
        box_sum = jnp.sum(pushes[:, c * nodes : (c + 1) * nodes], axis=1, keepdims=True)
        sums = jnp.where(lane == owner + 8 * c, box_sum, sums)
    record_ref[3:4, :] = jnp.sum(sums, axis=0, keepdims=True)


def prepare(fibre_solve, fibre_rhs, fibre_points, fibre_owner, density):
    fibres, quads = fibre_points.shape
    width = fibres * quads // 4
    hbm = pl.BlockSpec(memory_space=pltpu.HBM)
    return pl.pallas_call(
        prepare_kernel,
        out_shape=(
            jax.ShapeDtypeStruct((8, width), F32),
            jax.ShapeDtypeStruct((density.shape[0] // width, width), BF16),
        ),
        in_specs=[hbm] * 5,
        out_specs=(VMEM, VMEM),
        scratch_shapes=[
            pltpu.VMEM(fibre_solve.shape, BF16),
            pltpu.VMEM(fibre_rhs.shape, BF16),
            pltpu.VMEM(fibre_points.shape, F32),
            pltpu.VMEM(density.shape, F32),
            pltpu.SMEM((fibres,), jnp.int32),
            pltpu.SemaphoreType.DMA((fibres,)),
            pltpu.SemaphoreType.DMA((4,)),
        ],
        compiler_params=WHOLE,
        name="prepare",
    )(fibre_solve, fibre_rhs, fibre_points, fibre_owner.reshape(fibres), density)


def target_rows(place):
    sq = jnp.sum(place * place, axis=0, keepdims=True)
    high, middle, low = split3(place)
    one = jnp.ones_like(sq)
    zero = jnp.zeros_like(sq)
    sq_parts = split3(sq)
    return jnp.concatenate(
        [-2.0 * high, one] * 3
        + [-2.0 * middle, zero] * 2
        + [-2.0 * low, zero]
        + list(sq_parts)
        + [zero] * 5,
        axis=0,
    ).astype(BF16)


def source_rows(place):
    sq = jnp.sum(place * place, axis=0, keepdims=True) + smooth_sq
    high, middle, low = split3(jnp.concatenate([place, sq], axis=0))
    one = jnp.ones((3, place.shape[1]), F32)
    zero = jnp.zeros((5, place.shape[1]), F32)
    return jnp.concatenate([high, middle, low, high, middle, high, one, zero], axis=0).astype(BF16)


def source_terms(place, push, source):
    sq = jnp.sum(place * place, axis=0, keepdims=True) + 2.0 * smooth_sq
    rest = source - jnp.sum(place * push, axis=0, keepdims=True)
    terms = jnp.concatenate(
        [push, rest, sq * push - rest * place] + [place[a : a + 1] * push for a in range(3)], axis=0
    )
    return jnp.concatenate(split3(terms), axis=0).astype(BF16)


def add_sources(target_ref, groups, total_ref, block):
    targets = target_ref.shape[1]
    lead = total_ref.shape[0] // 3
    totals = {}
    for rows, terms in groups:
        width = rows.shape[1]
        step = min(block, width)
        for t in range(0, targets, block):
            for s in range(0, width, step):
                d = lax.dot_general(
                    rows[:, s : s + step],
                    target_ref[:, t : t + block],
                    (((0,), (0,)), ((), ())),
                    preferred_element_type=F32,
                )
                inverse = lax.rsqrt(d)
                cube = inverse * inverse * inverse
                high = cube.astype(BF16)
                low = (cube - high.astype(F32)).astype(BF16)
                term = terms[:, s : s + step]
                part = jnp.dot(term, high, preferred_element_type=F32)
                rest = jnp.dot(term[:lead], low, preferred_element_type=F32)
                part = jnp.concatenate([part[:lead] + rest, part[lead:]], axis=0)
                totals[t] = totals[t] + part if t in totals else part
    for t, value in totals.items():
        total_ref[:, t : t + block] += value


def point_columns(points):
    count = points.shape[1]
    eye = lax.broadcasted_iota(jnp.int32, (count, count), 0) == lax.broadcasted_iota(
        jnp.int32, (count, count), 1
    )
    return [
        2.0 * jnp.sum(jnp.where(eye, points[c : c + 1], 0.0), axis=1, keepdims=True) - 1.0
        for c in range(3)
    ]


def direct(columns, place, push, source):
    offset = [columns[c] - place[c : c + 1] for c in range(3)]
    sq = offset[0] * offset[0] + offset[1] * offset[1] + offset[2] * offset[2]
    inverse = lax.rsqrt(sq + smooth_sq)
    cube = inverse * inverse * inverse
    along = source + (
        offset[0] * push[0:1] + offset[1] * push[1:2] + offset[2] * push[2:3]
    )
    spread = cube * (sq + 2.0 * smooth_sq)
    along = cube * along
    return [spread * push[c : c + 1] + along * offset[c] for c in range(3)]


def fold(value, lanes):
    total = value[:, :lanes]
    for at in range(lanes, value.shape[1], lanes):
        total = total + value[:, at : at + lanes]
    return total


def near_kernel(shift, first, *refs):
    if first:
        records_ref, own_ref, shell_ref, total_ref, shell_total_ref, target_ref, sum_ref = refs
    else:
        (records_ref, own_ref, shell_ref, total_in, shell_in) = refs[:5]
        total_ref, shell_total_ref, target_ref, sum_ref = refs[5:]
    target_ref[...] = target_rows(own_ref[0:3, :])
    sum_ref[...] = jnp.zeros_like(sum_ref)
    if first:
        shell_total_ref[...] = jnp.zeros_like(shell_total_ref)
    else:
        shell_total_ref[...] = shell_in[...]
    columns = point_columns(shell_ref[...])
    if shift is not None:
        moved = (2 * shift(lax.axis_index("leaf"))).astype(F32)
    count = records_ref.shape[0]
    unroll = max(u for u in range(1, 5) if count % u == 0)

    def body(at, carry):
        groups = []
        for j in range(unroll):
            record = records_ref[at * unroll + j]
            place = record[0:3]
            if shift is not None:
                axis = lax.broadcasted_iota(jnp.int32, place.shape, 0)
                place = place + jnp.where(axis == 0, moved, 0.0)
            push, source = record[4:7], record[7:8]
            groups.append((source_rows(place), source_terms(place, push, source)))
            for c, value in enumerate(direct(columns, place, push, source)):
                shell_total_ref[c] += fold(value, 128)
        add_sources(target_ref, groups, sum_ref, 256)
        return carry

    if count == unroll:
        body(0, 0)
    else:
        lax.fori_loop(0, count // unroll, body, 0)
    terms = sum_ref.shape[0] // 3
    total = sum_ref[0:terms] + sum_ref[terms : 2 * terms] + sum_ref[2 * terms :]
    total_ref[...] = total if first else total + total_in[...]


def near(records, own, shell_points, shift, totals):
    targets = own.shape[1]
    count = shell_points.shape[1]
    out = (
        jax.ShapeDtypeStruct((16, targets), F32),
        jax.ShapeDtypeStruct((3, count, 128), F32),
    )
    pairs = records.shape[0] * records.shape[2] * targets
    return pl.pallas_call(
        functools.partial(near_kernel, shift, totals is None),
        out_shape=out,
        in_specs=[VMEM] * (3 if totals is None else 5),
        out_specs=(VMEM, VMEM),
        scratch_shapes=[pltpu.VMEM((32, targets), BF16), pltpu.VMEM((48, targets), F32)],
        compiler_params=PARAMS,
        cost_estimate=pl.CostEstimate(
            flops=500 * pairs, bytes_accessed=records.size * 4, transcendentals=pairs
        ),
        name="near",
    )(records, own, shell_points, *(totals or ()))


def finish_kernel(
    order,
    own_ref,
    shell_ref,
    moments_ref,
    dens_ref,
    block_ref,
    total_in,
    shell_in,
    flow_ref,
    shell_flow_ref,
    target_ref,
    sum_ref,
):
    leaf, octant = lax.axis_index("leaf"), lax.axis_index("oct")
    leaves, octants = moments_ref.shape[0], len(order)
    boxes = -(-leaves * octants // 128) * 128
    moments = []
    for c in range(4):
        parts = [
            moments_ref[j][:, c * octants : (c + 1) * octants] for j in range(leaves)
        ]
        if boxes > leaves * octants:
            parts.append(jnp.zeros((1, boxes - leaves * octants), F32))
        moments.append(jnp.concatenate(parts, axis=1))
    box = lax.broadcasted_iota(jnp.int32, (1, boxes), 1)
    away = jnp.bitwise_xor(box // 8, leaf) - leaf
    far = (jnp.abs(away) >= 2) & (box < leaves * octants)
    away = jnp.where(far, away, 0)
    child = box % 8
    place = jnp.concatenate(
        [
            (2 * away + child % 2).astype(F32) - 0.5,
            (child // 2 % 2).astype(F32) - 0.5,
            (child // 4).astype(F32) - 0.5,
        ],
        axis=0,
    )
    push = jnp.where(far, jnp.concatenate(moments[0:3], axis=0), 0.0)
    source = jnp.where(far, moments[3], 0.0)
    x = own_ref[0:3, :]
    target_ref[...] = target_rows(x)
    sum_ref[...] = jnp.zeros_like(sum_ref)
    groups = [(source_rows(place), source_terms(place, push, source))]
    add_sources(target_ref, groups, sum_ref, 256)
    terms = sum_ref.shape[0] // 3
    total = total_in[...] + (
        sum_ref[0:terms] + sum_ref[terms : 2 * terms] + sum_ref[2 * terms :]
    )
    push_sum, rest_sum, constant = total[0:3], total[3:4], total[4:7]
    cross = [total[7 + 3 * a : 10 + 3 * a] for a in range(3)]
    flow = (
        jnp.sum(x * x, axis=0, keepdims=True) * push_sum
        + constant
        + x * (jnp.sum(x * push_sum, axis=0, keepdims=True) + rest_sum)
    )
    for a in range(3):
        flow = flow - 2.0 * x[a : a + 1] * cross[a]
    turned = [
        jnp.sum(x * cross[c], axis=0, keepdims=True) for c in range(3)
    ]
    flow_ref[...] = stokes_scale * (flow - jnp.concatenate(turned, axis=0))
    columns = point_columns(shell_ref[...])
    shell = [
        jnp.sum(shell_in[c] + fold(value, 128), axis=1, keepdims=True)
        for c, value in enumerate(direct(columns, place, push, source))
    ]
    rows, width = dens_ref.shape[1:]
    count = block_ref.shape[1]

    def body(at, sums):
        for j in range(octants):
            dens = dens_ref[at * octants + j].astype(F32)
            owner = jnp.bitwise_xor(at, leaf) * octants + jnp.bitwise_xor(octant, order[j])
            for r in range(rows):
                start = pl.multiple_of((owner * rows + r) * width, 128)
                sums = tuple(
                    sums[c] + block_ref[c, :, pl.ds(start, width)].astype(F32) * dens[r : r + 1]
                    for c in range(3)
                )
        return sums

    zero = jnp.zeros((count, width), F32)
    sums = lax.fori_loop(0, leaves, body, (zero, zero, zero))
    product = [jnp.sum(sums[c], axis=1, keepdims=True) for c in range(3)]
    eye = lax.broadcasted_iota(jnp.int32, (count, count), 0) == lax.broadcasted_iota(
        jnp.int32, (count, count), 1
    )
    for c in range(3):
        column = product[c] + stokes_scale * shell[c]
        shell_flow_ref[c : c + 1, :] = jnp.sum(jnp.where(eye, column, 0.0), axis=0, keepdims=True)


def finish(order, own, shell_points, moments, dens, shell_block, totals):
    targets = own.shape[1]
    return pl.pallas_call(
        functools.partial(finish_kernel, order),
        out_shape=(
            jax.ShapeDtypeStruct((3, targets), F32),
            jax.ShapeDtypeStruct(shell_points.shape, F32),
        ),
        in_specs=[VMEM] * 7,
        out_specs=(VMEM, VMEM),
        scratch_shapes=[pltpu.VMEM((32, targets), BF16), pltpu.VMEM((48, targets), F32)],
        compiler_params=PARAMS,
        name="finish",
    )(own, shell_points, moments, dens, shell_block, *totals)


def exchange(value, axis, bit):
    count = lax.axis_size(axis)
    return lax.ppermute(value, axis, [(i, i ^ bit) for i in range(count)])


def together(*values):
    return lax.optimization_barrier(values)


def shards(fibre_solve, fibre_rhs, fibre_points, fibre_owner, shell_points, shell_block, density):
    octants = lax.axis_size("oct")
    leaves = lax.axis_size("leaf")
    record, dens = prepare(fibre_solve, fibre_rhs, fibre_points, fibre_owner, density)
    bits = [1 << b for b in range(octants.bit_length() - 1)]
    bits = bits[1:] + bits[:1]
    order = [0]
    records, dens = record[None], dens[None]
    fresh, totals = records, None
    for bit in bits:
        arrived, arrived_dens = exchange(records, "oct", bit), exchange(dens, "oct", bit)
        order = order + [j ^ bit for j in order]
        if bit != bits[-1]:
            totals = near(fresh, record, shell_points, None, totals)
            arrived, arrived_dens, totals = together(arrived, arrived_dens, totals)
            fresh = arrived
        else:
            fresh = jnp.concatenate([fresh, arrived], axis=0)
        records = jnp.concatenate([records, arrived], axis=0)
        dens = jnp.concatenate([dens, arrived_dens], axis=0)
    moments = jnp.sum(records[:, 3, :128], axis=0)[None, None]
    half = fresh.shape[0] // 2
    inner = exchange(records, "leaf", 1)
    inner_dens, inner_moments = exchange(dens, "leaf", 1), exchange(moments, "leaf", 1)
    totals = near(fresh[:half], record, shell_points, None, totals)
    late, totals = together(records, totals)
    pairs = [(i, i + 1) for i in range(1, leaves - 1, 2)]
    outer = lax.ppermute(late, "leaf", pairs + [(j, i) for i, j in pairs])
    totals = near(fresh[half:], record, shell_points, None, totals)
    inner, inner_dens, inner_moments, totals = together(inner, inner_dens, inner_moments, totals)
    dens = jnp.concatenate([dens, inner_dens], axis=0)
    moments = jnp.concatenate([moments, inner_moments], axis=0)
    for bit in [1 << b for b in range(1, leaves.bit_length() - 1)]:
        dens = jnp.concatenate([dens, exchange(dens, "leaf", bit)], axis=0)
        moments = jnp.concatenate([moments, exchange(moments, "leaf", bit)], axis=0)
    totals = near(inner, record, shell_points, lambda leaf: 1 - 2 * (leaf % 2), totals)
    totals = near(outer, record, shell_points, lambda leaf: 2 * (leaf % 2) - 1, totals)
    return finish(tuple(order), record, shell_points, moments, dens, shell_block, totals)


def solution(mesh):
    placed = (
        P(("leaf", "oct"), None, None),
        P(("leaf", "oct"), None),
        P(("leaf", "oct"), None),
        P(("leaf", "oct"), None),
        P(None, ("leaf", "oct")),
        P(None, ("leaf", "oct"), None),
        P(("leaf", "oct")),
    )
    return jax.shard_map(
        shards,
        mesh=mesh,
        in_specs=placed,
        out_specs=(P(None, ("leaf", "oct")), P(None, ("leaf", "oct"))),
        check_vma=False,
    )
```

time: 56.8 us -> 47.1 us (0.83)
  the two profiles are of different devices: /device:TPU:0 before, /device:TPU:8 now
where the time goes in v2:
time: 47.1 us; the launch traced here: 46.8 us
  Pallas kernels  24.3 us (52%)
  starting transfers between devices  15.3 us (32%)
  waiting for transfers between devices  3.26 us (7%)
  local copies, waits for them, and re-layouts  2.31 us (5%)
  other arithmetic  0.85 us (2%)
  between operations  0.82 us (2%)
    pallas_call x6, Pallas kernels, near(): pl.pallas_call(functools.partial(near_kernel, shift, totals is None), out...  17.9 us
    ppermute x11, starting transfers between devices, exchange(): return lax.ppermute(value, axis, [(i, i ^ bit) for i in range(count)])  10.5 us
    ppermute x1, starting transfers between devices, shards(): outer = lax.ppermute(late, 'leaf', pairs + [(j, i) for i, j in pairs])  4.78 us
    pallas_call x1, Pallas kernels, prepare(): pl.pallas_call(prepare_kernel, out_shape=(jax.ShapeDtypeStruct((8, width)...  4.47 us
    ppermute x11, waiting for transfers between devices, exchange(): return lax.ppermute(value, axis, [(i, i ^ bit) for i in range(count)])  3.26 us
    unnamed x12, local copies, waits for them, and re-layouts  2.21 us
    pallas_call x1, Pallas kernels, finish(): pl.pallas_call(functools.partial(finish_kernel, order), out_shape=(jax.Sh...  1.89 us
  transfers between devices with their start and end apart: 12, of which 3 were waited for; matrix products, arithmetic and copies ran while one was open for 4% of the time, Pallas kernels for 38%

profile of v2, /device:TPU:8, one launch (start us, length us, event | category | flops | bytes accessed | tf_op | source)
XLA Modules:
  0.0 46.8 jit_solution(8571459378674796536)
XLA Ops:
  0.6 4.5 %prepare.1 = (f32[8,768]{1,0:T(8,128)}, bf16[4,768]{1,0:T(4,128)(2,1)}) custom-call(bf16[12,256,256]{2,1,0:T(8,128)(2,1)} %solve_hbm.1, bf16[12,256]{1,0:T(8,128)(2,1)} %rhs_hbm.1, f32[12,256]{1,0:T(8,128)} %points_hbm.1, s32[12]{0:T(128)} %bitcast.18, f32[3072]{0:T(1024)} %density_hbm.1), custom_call_target="tpu_custom_call" | custom-call | tf_op jit(solution)/shard_map/prepare/pallas_call | solution.py:103
  5.1 1.6 %collective-permute-start = (f32[1,8,768]{2,1,0:T(8,128)}, f32[1,8,768]{2,1,0:T(8,128)S(1)}, u32[]{:S(2)}, u32[]{:S(2)}) collective-permute-start(f32[1,8,768]{2,1,0:T(8,128)} %bitcast.6), channel_id=1, source_target_pairs={{0,2},{1,3},{2,0},{3,1},{4,6},{5,7},{6,4},{7,5},{8,10},{9,11},{10,... | collective-permute-start | bytes 73736 | tf_op jit(solution)/shard_map/ppermute | solution.py:392
  6.7 0.5 %collective-permute-start.1 = (bf16[1,4,768]{2,1,0:T(4,128)(2,1)}, bf16[1,4,768]{2,1,0:T(4,128)(2,1)S(1)}, u32[]{:S(2)}, u32[]{:S(2)}) collective-permute-start(bf16[1,4,768]{2,1,0:T(4,128)(2,1)} %bitcast.11), channel_id=1, source_target_pairs={{0,2},{1,3},{2,0},{3,1},{4,6},{5,7},{6,4},{7,5},{8,10},{9,11},{10,... | collective-permute-start | bytes 18440 | tf_op jit(solution)/shard_map/ppermute | solution.py:392
  7.2 0.7 %constant_dynamic-update-slice_fusion.4 = (bf16[16,4,768]{2,1,0:T(4,128)(2,1)S(1)}, bf16[32,4,768]{2,1,0:T(4,128)(2,1)S(1)}) fusion(bf16[4,768]{1,0:T(4,128)(2,1)} %get-tuple-element.33), kind=kLoop, calls=%fused_computation.10 | loop fusion | bytes 18432
  7.9 0.7 %copy-done.1 = f32[8,768]{1,0:T(8,128)S(1)} copy-done((f32[8,768]{1,0:T(8,128)S(1)}, f32[8,768]{1,0:T(8,128)}, u32[]{:S(2)}) %copy-start.1) | copy-done | bytes 24600
  8.7 0.7 %copy-done.2 = f32[3,4]{1,0:T(4,128)S(1)} copy-done((f32[3,4]{1,0:T(4,128)S(1)}, f32[3,4]{1,0:T(4,128)}, u32[]{:S(2)}) %copy-start.2) | copy-done | bytes 72
  9.4 1.0 %near.6 = (f32[16,768]{1,0:T(8,128)S(1)}, f32[3,4,128]{2,1,0:T(4,128)S(1)}) custom-call(f32[1,8,768]{2,1,0:T(8,128)S(1)} %bitcast.7, f32[8,768]{1,0:T(8,128)S(1)} %copy-done.1, f32[3,4]{1,0:T(4,128)S(1)} %copy-done.2), custom_call_target="tpu_custom_call" | custom-call | flops 294912000 | bytes 24576 | tf_op jit(solution)/shard_map/near/pallas_call | solution.py:267
  10.5 1.6 %collective-permute-start.2 = (f32[2,8,768]{2,1,0:T(8,128)S(1)}, f32[2,8,768]{2,1,0:T(8,128)S(1)}, u32[]{:S(2)}, u32[]{:S(2)}) collective-permute-start(f32[2,8,768]{2,1,0:T(8,128)S(1)} %pad_maximum_fusion.3), channel_id=1, source_target_pairs={{0,4},{1,5},{2,6},{3,7},{4,0},{5,1},{6,2},{7,3},{8,12},{9,13},{10,... | collective-permute-start | bytes 147464 | tf_op jit(solution)/shard_map/ppermute | solution.py:392
  12.1 0.7 %pad_maximum_fusion.6 = bf16[2,4,768]{2,1,0:T(4,128)(2,1)S(1)} fusion(bf16[1,4,768]{2,1,0:T(4,128)(2,1)S(1)} %collective-permute-done.1, bf16[1,4,768]{2,1,0:T(4,128)(2,1)} %bitcast.12), kind=kLoop, calls=%fused_computation.17 | loop fusion | flops 6144 | bytes 24576 | tf_op jit(solution)/shard_map/concatenate | solution.py:418
  12.8 0.6 %collective-permute-start.3 = (bf16[2,4,768]{2,1,0:T(4,128)(2,1)S(1)}, bf16[2,4,768]{2,1,0:T(4,128)(2,1)S(1)}, u32[]{:S(2)}, u32[]{:S(2)}) collective-permute-start(bf16[2,4,768]{2,1,0:T(4,128)(2,1)S(1)} %pad_maximum_fusion.6), channel_id=1, source_target_pairs={{0,4},{1,5},{2,6},{3,7},{4,0},{5,1},{6,2},{7,3},{8,12},{9,13},{10,... | collective-permute-start | bytes 36872 | tf_op jit(solution)/shard_map/ppermute | solution.py:392
  13.4 1.0 %near.7 = (f32[16,768]{1,0:T(8,128)S(1)}, f32[3,4,128]{2,1,0:T(4,128)S(1)}) custom-call(f32[1,8,768]{2,1,0:T(8,128)S(1)} %collective-permute-done.refs_0_, f32[8,768]{1,0:T(8,128)S(1)} %copy-done.1, f32[3,4]{1,0:T(4,128)S(1)} %copy-done.2, f32[16,768]{1,0:T(8,128)S(1)} %get-tuple-element.38.refs_3_, f32[3,4,128]{2,1,0:T(4,128)S(1)} %get-tuple-element.39.refs_4_), custom_call_target="tpu_custom_call" | custom-call | flops 294912000 | bytes 24576 | tf_op jit(solution)/shard_map/near/pallas_call | solution.py:267
  14.4 2.2 %collective-permute-done.3 = bf16[2,4,768]{2,1,0:T(4,128)(2,1)S(1)} collective-permute-done((bf16[2,4,768]{2,1,0:T(4,128)(2,1)S(1)}, bf16[2,4,768]{2,1,0:T(4,128)(2,1)S(1)}, u32[]{:S(2)}, u32[]{:S(2)}) %collective-permute-start.3) | collective-permute-done | bytes 12320 | tf_op jit(solution)/shard_map/ppermute | solution.py:392
  16.7 0.5 %collective-permute-start.6 = (bf16[4,4,768]{2,1,0:T(4,128)(2,1)S(1)}, bf16[4,4,768]{2,1,0:T(4,128)(2,1)S(1)}, u32[]{:S(2)}, u32[]{:S(2)}) collective-permute-start(bf16[4,4,768]{2,1,0:T(4,128)(2,1)S(1)} %pad_maximum_fusion.5), channel_id=1, source_target_pairs={{0,1},{1,0},{2,3},{3,2},{4,5},{5,4},{6,7},{7,6},{8,9},{9,8},{10,11... | collective-permute-start | bytes 73736 | tf_op jit(solution)/shard_map/ppermute | solution.py:392
  17.3 0.8 %collective-permute-done.6 = bf16[4,4,768]{2,1,0:T(4,128)(2,1)S(1)} collective-permute-done((bf16[4,4,768]{2,1,0:T(4,128)(2,1)S(1)}, bf16[4,4,768]{2,1,0:T(4,128)(2,1)S(1)}, u32[]{:S(2)}, u32[]{:S(2)}) %collective-permute-start.6) | collective-permute-done | bytes 24608 | tf_op jit(solution)/shard_map/ppermute | solution.py:392
  18.2 0.5 %collective-permute-start.7 = (bf16[8,4,768]{2,1,0:T(4,128)(2,1)S(1)}, bf16[8,4,768]{2,1,0:T(4,128)(2,1)S(1)}, u32[]{:S(2)}, u32[]{:S(2)}) collective-permute-start(bf16[8,4,768]{2,1,0:T(4,128)(2,1)S(1)} %pad_maximum_fusion.4), channel_id=1, source_target_pairs={{0,8},{8,0},{16,24},{24,16},{1,9},{9,1},{17,25},{25,17},{2,10},{10... | collective-permute-start | bytes 147464 | tf_op jit(solution)/shard_map/ppermute | solution.py:392
  18.7 1.6 %collective-permute-start.5 = (f32[8,8,768]{2,1,0:T(8,128)S(1)}, f32[8,8,768]{2,1,0:T(8,128)S(1)}, u32[]{:S(2)}, u32[]{:S(2)}) collective-permute-start(f32[8,8,768]{2,1,0:T(8,128)S(1)} %pad_maximum_fusion), channel_id=1, source_target_pairs={{0,8},{8,0},{16,24},{24,16},{1,9},{9,1},{17,25},{25,17},{2,10},{10... | collective-permute-start | bytes 589832 | tf_op jit(solution)/shard_map/ppermute | solution.py:392
  20.4 2.2 %near.8 = (f32[16,768]{1,0:T(8,128)S(1)}, f32[3,4,128]{2,1,0:T(4,128)S(1)}) custom-call(f32[3,8,768]{2,1,0:T(8,128)S(1)} %get-tuple-element.62.refs_0_, f32[8,768]{1,0:T(8,128)S(1)} %copy-done.1, f32[3,4]{1,0:T(4,128)S(1)} %copy-done.2, f32[16,768]{1,0:T(8,128)S(1)} %get-tuple-element.44.refs_3_, f32[3,4,128]{2,1,0:T(4,128)S(1)} %get-tuple-element.45.refs_4_), custom_call_target="tpu_custom_call" | custom-call | flops 884736000 | bytes 73728 | tf_op jit(solution)/shard_map/near/pallas_call | solution.py:267
  22.6 0.5 %collective-permute-start.8 = (f32[1,1,128]{2,1,0:T(1,128)S(1)}, f32[1,1,128]{2,1,0:T(1,128)S(1)}, u32[]{:S(2)}, u32[]{:S(2)}) collective-permute-start(f32[1,1,128]{2,1,0:T(1,128)S(1)} %bitcast.15), channel_id=1, source_target_pairs={{0,8},{8,0},{16,24},{24,16},{1,9},{9,1},{17,25},{25,17},{2,10},{10... | collective-permute-start | bytes 1544 | tf_op jit(solution)/shard_map/ppermute | solution.py:392
  23.1 4.8 %collective-permute-start.11 = (f32[8,8,768]{2,1,0:T(8,128)S(1)}, f32[8,8,768]{2,1,0:T(8,128)S(1)}, u32[]{:S(2)}, u32[]{:S(2)}) collective-permute-start(f32[8,8,768]{2,1,0:T(8,128)S(1)} %pad_maximum_fusion), channel_id=1, source_target_pairs={{8,16},{16,8},{9,17},{17,9},{10,18},{18,10},{11,19},{19,11},{12,20... | collective-permute-start | bytes 589832 | tf_op jit(solution)/shard_map/ppermute | solution.py:426
  27.9 2.2 %near.9 = (f32[16,768]{1,0:T(8,128)S(1)}, f32[3,4,128]{2,1,0:T(4,128)S(1)}) custom-call(f32[3,8,768]{2,1,0:T(8,128)S(1)} %get-tuple-element.63.refs_0_, f32[8,768]{1,0:T(8,128)S(1)} %copy-done.1, f32[3,4]{1,0:T(4,128)S(1)} %copy-done.2, f32[16,768]{1,0:T(8,128)S(1)} %get-tuple-element.48.refs_3_, f32[3,4,128]{2,1,0:T(4,128)S(1)} %get-tuple-element.49.refs_4_), custom_call_target="tpu_custom_call" | custom-call | flops 884736000 | bytes 73728 | tf_op jit(solution)/shard_map/near/pallas_call | solution.py:267
  30.3 2.9 %collective-permute-start.9 = (f32[2,1,128]{2,1,0:T(1,128)S(1)}, f32[2,1,128]{2,1,0:T(1,128)S(1)}, u32[]{:S(2)}, u32[]{:S(2)}) collective-permute-start(f32[2,1,128]{2,1,0:T(1,128)S(1)} %pad_maximum_fusion.8), channel_id=1, source_target_pairs={{0,16},{8,24},{16,0},{24,8},{1,17},{9,25},{17,1},{25,9},{2,18},{10... | collective-permute-start | bytes 3080 | tf_op jit(solution)/shard_map/ppermute | solution.py:392
  33.2 5.8 %near.10 = (f32[16,768]{1,0:T(8,128)S(1)}, f32[3,4,128]{2,1,0:T(4,128)S(1)}) custom-call(f32[8,8,768]{2,1,0:T(8,128)S(1)} %collective-permute-done.5.refs_0_, f32[8,768]{1,0:T(8,128)S(1)} %copy-done.1, f32[3,4]{1,0:T(4,128)S(1)} %copy-done.2, f32[16,768]{1,0:T(8,128)S(1)} %get-tuple-element.56.refs_3_, f32[3,4,128]{2,1,0:T(4,128)S(1)} %get-tuple-element.57.refs_4_), custom_call_target="tpu_custom_call" | custom-call | flops 2359296000 | bytes 196608 | tf_op jit(solution)/shard_map/near/pallas_call | solution.py:267
  39.0 5.8 %near.11 = (f32[16,768]{1,0:T(8,128)S(1)}, f32[3,4,128]{2,1,0:T(4,128)S(1)}) custom-call(f32[8,8,768]{2,1,0:T(8,128)S(1)} %collective-permute-done.11.refs_0_, f32[8,768]{1,0:T(8,128)S(1)} %copy-done.1, f32[3,4]{1,0:T(4,128)S(1)} %copy-done.2, f32[16,768]{1,0:T(8,128)S(1)} %get-tuple-element.58.refs_3_, f32[3,4,128]{2,1,0:T(4,128)S(1)} %get-tuple-element.59.refs_4_), custom_call_target="tpu_custom_call" | custom-call | flops 2359296000 | bytes 196608 | tf_op jit(solution)/shard_map/near/pallas_call | solution.py:267
  44.9 1.9 %finish.1 = (f32[3,768]{1,0:T(4,128)}, f32[3,4]{1,0:T(4,128)}) custom-call(f32[8,768]{1,0:T(8,128)S(1)} %copy-done.1, f32[3,4]{1,0:T(4,128)S(1)} %copy-done.2, f32[4,1,128]{2,1,0:T(1,128)S(1)} %pad_maximum_fusion.7.moments_ref, bf16[32,4,768]{2,1,0:T(4,128)(2,1)S(1)} %constant_dynamic-update-slice_fusion.5.dens_ref, bf16[3,4,98304]{2,1,0:T(4,128)(2,1)S(1)} %copy-done, ...), custom_call_target="tpu_custom_call" | custom-call | tf_op jit(solution)/shard_map/finish/pallas_call | solution.py:376
  (32 shorter events, 0.7 us)
Async XLA Ops:
  5.1 11.6 %copy-start.3 = (bf16[4,768]{1,0:T(4,128)(2,1)S(1)}, bf16[4,768]{1,0:T(4,128)(2,1)}, u32[]{:S(2)}) copy-start(bf16[4,768]{1,0:T(4,128)(2,1)} %get-tuple-element.33) | copy-start | bytes 18436
  5.1 5.4 %collective-permute-start = (f32[1,8,768]{2,1,0:T(8,128)}, f32[1,8,768]{2,1,0:T(8,128)S(1)}, u32[]{:S(2)}, u32[]{:S(2)}) collective-permute-start(f32[1,8,768]{2,1,0:T(8,128)} %bitcast.6), channel_id=1, source_target_pairs={{0,2},{1,3},{2,0},{3,1},{4,6},{5,7},{6,4},{7,5},{8,10},{9,11},{10,... | collective-permute-start | bytes 73736 | tf_op jit(solution)/shard_map/ppermute | solution.py:392
  6.7 3.8 %collective-permute-start.1 = (bf16[1,4,768]{2,1,0:T(4,128)(2,1)}, bf16[1,4,768]{2,1,0:T(4,128)(2,1)S(1)}, u32[]{:S(2)}, u32[]{:S(2)}) collective-permute-start(bf16[1,4,768]{2,1,0:T(4,128)(2,1)} %bitcast.11), channel_id=1, source_target_pairs={{0,2},{1,3},{2,0},{3,1},{4,6},{5,7},{6,4},{7,5},{8,10},{9,11},{10,... | collective-permute-start | bytes 18440 | tf_op jit(solution)/shard_map/ppermute | solution.py:392
  7.9 0.7 %copy-start.1 = (f32[8,768]{1,0:T(8,128)S(1)}, f32[8,768]{1,0:T(8,128)}, u32[]{:S(2)}) copy-start(f32[8,768]{1,0:T(8,128)} %get-tuple-element.32.refs_1_.own_ref) | copy-start | bytes 73732
  8.7 0.7 %copy-start.2 = (f32[3,4]{1,0:T(4,128)S(1)}, f32[3,4]{1,0:T(4,128)}, u32[]{:S(2)}) copy-start(f32[3,4]{1,0:T(4,128)} %shell_ref.1) | copy-start | bytes 148
  10.5 6.1 %collective-permute-start.2 = (f32[2,8,768]{2,1,0:T(8,128)S(1)}, f32[2,8,768]{2,1,0:T(8,128)S(1)}, u32[]{:S(2)}, u32[]{:S(2)}) collective-permute-start(f32[2,8,768]{2,1,0:T(8,128)S(1)} %pad_maximum_fusion.3), channel_id=1, source_target_pairs={{0,4},{1,5},{2,6},{3,7},{4,0},{5,1},{6,2},{7,3},{8,12},{9,13},{10,... | collective-permute-start | bytes 147464 | tf_op jit(solution)/shard_map/ppermute | solution.py:392
  12.8 3.8 %collective-permute-start.3 = (bf16[2,4,768]{2,1,0:T(4,128)(2,1)S(1)}, bf16[2,4,768]{2,1,0:T(4,128)(2,1)S(1)}, u32[]{:S(2)}, u32[]{:S(2)}) collective-permute-start(bf16[2,4,768]{2,1,0:T(4,128)(2,1)S(1)} %pad_maximum_fusion.6), channel_id=1, source_target_pairs={{0,4},{1,5},{2,6},{3,7},{4,0},{5,1},{6,2},{7,3},{8,12},{9,13},{10,... | collective-permute-start | bytes 36872 | tf_op jit(solution)/shard_map/ppermute | solution.py:392
  16.6 2.1 %collective-permute-start.4 = (f32[4,8,768]{2,1,0:T(8,128)S(1)}, f32[4,8,768]{2,1,0:T(8,128)S(1)}, u32[]{:S(2)}, u32[]{:S(2)}) collective-permute-start(f32[4,8,768]{2,1,0:T(8,128)S(1)} %pad_maximum_fusion.1), channel_id=1, source_target_pairs={{0,1},{1,0},{2,3},{3,2},{4,5},{5,4},{6,7},{7,6},{8,9},{9,8},{10,11... | collective-permute-start | bytes 294920 | tf_op jit(solution)/shard_map/ppermute | solution.py:392
  16.7 1.4 %collective-permute-start.6 = (bf16[4,4,768]{2,1,0:T(4,128)(2,1)S(1)}, bf16[4,4,768]{2,1,0:T(4,128)(2,1)S(1)}, u32[]{:S(2)}, u32[]{:S(2)}) collective-permute-start(bf16[4,4,768]{2,1,0:T(4,128)(2,1)S(1)} %pad_maximum_fusion.5), channel_id=1, source_target_pairs={{0,1},{1,0},{2,3},{3,2},{4,5},{5,4},{6,7},{7,6},{8,9},{9,8},{10,11... | collective-permute-start | bytes 73736 | tf_op jit(solution)/shard_map/ppermute | solution.py:392
  18.2 12.0 %collective-permute-start.7 = (bf16[8,4,768]{2,1,0:T(4,128)(2,1)S(1)}, bf16[8,4,768]{2,1,0:T(4,128)(2,1)S(1)}, u32[]{:S(2)}, u32[]{:S(2)}) collective-permute-start(bf16[8,4,768]{2,1,0:T(4,128)(2,1)S(1)} %pad_maximum_fusion.4), channel_id=1, source_target_pairs={{0,8},{8,0},{16,24},{24,16},{1,9},{9,1},{17,25},{25,17},{2,10},{10... | collective-permute-start | bytes 147464 | tf_op jit(solution)/shard_map/ppermute | solution.py:392
  18.7 11.4 %collective-permute-start.5 = (f32[8,8,768]{2,1,0:T(8,128)S(1)}, f32[8,8,768]{2,1,0:T(8,128)S(1)}, u32[]{:S(2)}, u32[]{:S(2)}) collective-permute-start(f32[8,8,768]{2,1,0:T(8,128)S(1)} %pad_maximum_fusion), channel_id=1, source_target_pairs={{0,8},{8,0},{16,24},{24,16},{1,9},{9,1},{17,25},{25,17},{2,10},{10... | collective-permute-start | bytes 589832 | tf_op jit(solution)/shard_map/ppermute | solution.py:392
  22.6 7.5 %collective-permute-start.8 = (f32[1,1,128]{2,1,0:T(1,128)S(1)}, f32[1,1,128]{2,1,0:T(1,128)S(1)}, u32[]{:S(2)}, u32[]{:S(2)}) collective-permute-start(f32[1,1,128]{2,1,0:T(1,128)S(1)} %bitcast.15), channel_id=1, source_target_pairs={{0,8},{8,0},{16,24},{24,16},{1,9},{9,1},{17,25},{25,17},{2,10},{10... | collective-permute-start | bytes 1544 | tf_op jit(solution)/shard_map/ppermute | solution.py:392
  23.1 15.9 %collective-permute-start.11 = (f32[8,8,768]{2,1,0:T(8,128)S(1)}, f32[8,8,768]{2,1,0:T(8,128)S(1)}, u32[]{:S(2)}, u32[]{:S(2)}) collective-permute-start(f32[8,8,768]{2,1,0:T(8,128)S(1)} %pad_maximum_fusion), channel_id=1, source_target_pairs={{8,16},{16,8},{9,17},{17,9},{10,18},{18,10},{11,19},{19,11},{12,20... | collective-permute-start | bytes 589832 | tf_op jit(solution)/shard_map/ppermute | solution.py:426
  30.2 14.7 %collective-permute-start.10 = (bf16[16,4,768]{2,1,0:T(4,128)(2,1)S(1)}, bf16[16,4,768]{2,1,0:T(4,128)(2,1)S(1)}, u32[]{:S(2)}, u32[]{:S(2)}) collective-permute-start(bf16[16,4,768]{2,1,0:T(4,128)(2,1)S(1)} %get-tuple-element.64), channel_id=1, source_target_pairs={{0,16},{8,24},{16,0},{24,8},{1,17},{9,25},{17,1},{25,9},{2,18},{10... | collective-permute-start | bytes 294920 | tf_op jit(solution)/shard_map/ppermute | solution.py:392
  30.3 14.6 %collective-permute-start.9 = (f32[2,1,128]{2,1,0:T(1,128)S(1)}, f32[2,1,128]{2,1,0:T(1,128)S(1)}, u32[]{:S(2)}, u32[]{:S(2)}) collective-permute-start(f32[2,1,128]{2,1,0:T(1,128)S(1)} %pad_maximum_fusion.8), channel_id=1, source_target_pairs={{0,16},{8,24},{16,0},{24,8},{1,17},{9,25},{17,1},{25,9},{2,18},{10... | collective-permute-start | bytes 3080 | tf_op jit(solution)/shard_map/ppermute | solution.py:392
  39.0 5.9 %copy-start = (bf16[3,4,98304]{2,1,0:T(4,128)(2,1)S(1)}, bf16[3,4,98304]{2,1,0:T(4,128)(2,1)}, u32[]{:S(2)}) copy-start(bf16[3,4,98304]{2,1,0:T(4,128)(2,1)} %block_ref.1) | copy-start | bytes 7077892

commit v3 on v2

--- a/solution.py
+++ b/solution.py
@@ -13,7 +13,6 @@
 F32 = jnp.float32
 BF16 = jnp.bfloat16
 VMEM = pl.BlockSpec(memory_space=pltpu.VMEM)
-WHOLE = pltpu.CompilerParams(vmem_limit_bytes=64 * 2**20 - 2**17)
 PARAMS = pltpu.CompilerParams(vmem_limit_bytes=40 * 2**20)
 
 
@@ -24,43 +23,36 @@
     return high, middle, (rest - middle).astype(BF16).astype(F32)
 
 
-def prepare_kernel(
-    solve_hbm,
-    rhs_hbm,
-    points_hbm,
-    owner_hbm,
-    density_hbm,
-    record_ref,
-    dens_ref,
-    solve_ref,
-    rhs_ref,
-    points_ref,
-    density_ref,
-    owner_ref,
-    solve_sem,
-    sem,
-):
+def prepare_kernel(*refs):
+    solve_hbm, rhs_hbm, points_hbm, owner_hbm, density_hbm, shell_hbm = refs[:6]
+    record_ref, shell_out = refs[6:8]
+    solve_ref, rhs_ref, points_ref, density_ref, shell_ref, owner_ref, solve_sem, sem = refs[8:]
     fibres, quads = rhs_ref.shape
     nodes = quads // 4
-    width = record_ref.shape[1]
+    width = record_ref.shape[2]
+    part = math.gcd(fibres, 4)
     copies = [
         pltpu.make_async_copy(owner_hbm, owner_ref, sem.at[0]),
         pltpu.make_async_copy(points_hbm, points_ref, sem.at[1]),
         pltpu.make_async_copy(rhs_hbm, rhs_ref, sem.at[2]),
         pltpu.make_async_copy(density_hbm, density_ref, sem.at[3]),
+        pltpu.make_async_copy(shell_hbm, shell_ref, sem.at[4]),
     ]
     solves = [
-        pltpu.make_async_copy(solve_hbm.at[f], solve_ref.at[f], solve_sem.at[f])
-        for f in range(fibres)
+        pltpu.make_async_copy(
+            solve_hbm.at[pl.ds(f, part)], solve_ref.at[pl.ds(f, part)], solve_sem.at[f // part]
+        )
+        for f in range(0, fibres, part)
     ]
     for copy in copies + solves:
         copy.start()
     for copy in copies:
         copy.wait()
-    rows = dens_ref.shape[0]
-    dens_ref[...] = jnp.concatenate(
-        [density_ref[r * width : (r + 1) * width].reshape(1, width) for r in range(rows)], axis=0
-    ).astype(BF16)
+    shell_out[...] = shell_ref[...]
+    record_ref[2] = jnp.zeros(record_ref.shape[1:], F32)
+    for r in range(density_ref.shape[0] // width):
+        dens = density_ref[r * width : (r + 1) * width].reshape(1, width)
+        record_ref[2, r : r + 1, :] = dens.astype(BF16).astype(F32)
     row = lax.broadcasted_iota(jnp.int32, (fibres, 1), 0)
     owner = jnp.zeros((fibres, 1), jnp.int32)
     for f in range(fibres):
@@ -73,12 +65,13 @@
     for f in range(fibres):
         lanes = slice(f * nodes, (f + 1) * nodes)
         for c in range(3):
-            record_ref[c : c + 1, lanes] = place[c][f : f + 1, :]
+            record_ref[0, c : c + 1, lanes] = place[c][f : f + 1, :]
     quad_weight = points[:, 3 * nodes :]
     rhs = rhs_ref[...]
     forces = jnp.zeros((fibres, quads), F32)
     for f in range(fibres):
-        solves[f].wait()
+        if f % part == 0:
+            solves[f // part].wait()
         product = lax.dot_general(
             rhs, solve_ref[f], (((1,), (1,)), ((), ())), preferred_element_type=F32
         )
@@ -87,39 +80,47 @@
     for f in range(fibres):
         lanes = slice(f * nodes, (f + 1) * nodes)
         for c in range(4):
-            record_ref[4 + c : 5 + c, lanes] = pushes[f : f + 1, c * nodes : (c + 1) * nodes]
+            record_ref[1, c : c + 1, lanes] = pushes[f : f + 1, c * nodes : (c + 1) * nodes]
     lane = lax.broadcasted_iota(jnp.int32, (fibres, width), 1)
     sums = jnp.zeros((fibres, width), F32)
     for c in range(4):
         box_sum = jnp.sum(pushes[:, c * nodes : (c + 1) * nodes], axis=1, keepdims=True)
         sums = jnp.where(lane == owner + 8 * c, box_sum, sums)
-    record_ref[3:4, :] = jnp.sum(sums, axis=0, keepdims=True)
-
-
-def prepare(fibre_solve, fibre_rhs, fibre_points, fibre_owner, density):
+    record_ref[0, 3:4, :] = jnp.sum(sums, axis=0, keepdims=True)
+
+
+def prepare(fibre_solve, fibre_rhs, fibre_points, fibre_owner, density, shell_points):
     fibres, quads = fibre_points.shape
     width = fibres * quads // 4
-    hbm = pl.BlockSpec(memory_space=pltpu.HBM)
+    inputs = (
+        fibre_solve,
+        fibre_rhs,
+        fibre_points,
+        fibre_owner.reshape(fibres),
+        density,
+        shell_points,
+    )
     return pl.pallas_call(
         prepare_kernel,
         out_shape=(
-            jax.ShapeDtypeStruct((8, width), F32),
-            jax.ShapeDtypeStruct((density.shape[0] // width, width), BF16),
+            jax.ShapeDtypeStruct((3, 4, width), F32),
+            jax.ShapeDtypeStruct(shell_points.shape, F32),
         ),
-        in_specs=[hbm] * 5,
+        in_specs=[pl.BlockSpec(memory_space=pltpu.HBM)] * 6,
         out_specs=(VMEM, VMEM),
         scratch_shapes=[
             pltpu.VMEM(fibre_solve.shape, BF16),
             pltpu.VMEM(fibre_rhs.shape, BF16),
             pltpu.VMEM(fibre_points.shape, F32),
             pltpu.VMEM(density.shape, F32),
+            pltpu.VMEM(shell_points.shape, F32),
             pltpu.SMEM((fibres,), jnp.int32),
             pltpu.SemaphoreType.DMA((fibres,)),
-            pltpu.SemaphoreType.DMA((4,)),
+            pltpu.SemaphoreType.DMA((5,)),
         ],
-        compiler_params=WHOLE,
+        compiler_params=PARAMS,
         name="prepare",
-    )(fibre_solve, fibre_rhs, fibre_points, fibre_owner.reshape(fibres), density)
+    )(*[pltpu.with_memory_space_constraint(value, pltpu.HBM) for value in inputs])
 
 
 def target_rows(place):
@@ -214,13 +215,13 @@
     return total
 
 
-def near_kernel(shift, first, *refs):
+def near_kernel(shift, leaves, first, *refs):
     if first:
         records_ref, own_ref, shell_ref, total_ref, shell_total_ref, target_ref, sum_ref = refs
     else:
         (records_ref, own_ref, shell_ref, total_in, shell_in) = refs[:5]
         total_ref, shell_total_ref, target_ref, sum_ref = refs[5:]
-    target_ref[...] = target_rows(own_ref[0:3, :])
+    target_ref[...] = target_rows(own_ref[0, 0:3, :])
     sum_ref[...] = jnp.zeros_like(sum_ref)
     if first:
         shell_total_ref[...] = jnp.zeros_like(shell_total_ref)
@@ -235,19 +236,23 @@
     def body(at, carry):
         groups = []
         for j in range(unroll):
-            record = records_ref[at * unroll + j]
-            place = record[0:3]
+            record = records_ref.at[at * unroll + j]
+            place = record[0, 0:3, :]
             if shift is not None:
                 axis = lax.broadcasted_iota(jnp.int32, place.shape, 0)
                 place = place + jnp.where(axis == 0, moved, 0.0)
-            push, source = record[4:7], record[7:8]
+            push, source = record[1, 0:3, :], record[1, 3:4, :]
             groups.append((source_rows(place), source_terms(place, push, source)))
             for c, value in enumerate(direct(columns, place, push, source)):
                 shell_total_ref[c] += fold(value, 128)
         add_sources(target_ref, groups, sum_ref, 256)
         return carry
 
-    if count == unroll:
+    if shift is not None:
+        there = lax.axis_index("leaf") + shift(lax.axis_index("leaf"))
+        steps = jnp.where((there >= 0) & (there < leaves), count // unroll, 0)
+        lax.fori_loop(0, steps, body, 0)
+    elif count == unroll:
         body(0, 0)
     else:
         lax.fori_loop(0, count // unroll, body, 0)
@@ -257,15 +262,15 @@
 
 
 def near(records, own, shell_points, shift, totals):
-    targets = own.shape[1]
+    targets = own.shape[2]
     count = shell_points.shape[1]
     out = (
         jax.ShapeDtypeStruct((16, targets), F32),
         jax.ShapeDtypeStruct((3, count, 128), F32),
     )
-    pairs = records.shape[0] * records.shape[2] * targets
+    pairs = records.shape[0] * targets * targets
     return pl.pallas_call(
-        functools.partial(near_kernel, shift, totals is None),
+        functools.partial(near_kernel, shift, lax.axis_size("leaf"), totals is None),
         out_shape=out,
         in_specs=[VMEM] * (3 if totals is None else 5),
         out_specs=(VMEM, VMEM),
@@ -280,10 +285,10 @@
 
 def finish_kernel(
     order,
+    leaves,
     own_ref,
     shell_ref,
-    moments_ref,
-    dens_ref,
+    held_ref,
     block_ref,
     total_in,
     shell_in,
@@ -293,18 +298,23 @@
     sum_ref,
 ):
     leaf, octant = lax.axis_index("leaf"), lax.axis_index("oct")
-    leaves, octants = moments_ref.shape[0], len(order)
+    octants = len(order)
+    turned = (leaf + 1) // 2 % 2
     boxes = -(-leaves * octants // 128) * 128
     moments = []
     for c in range(4):
-        parts = [
-            moments_ref[j][:, c * octants : (c + 1) * octants] for j in range(leaves)
-        ]
+        parts = []
+        for j in range(leaves):
+            split = held_ref[j // 2, 2 * octants].astype(F32)
+            at = ((j % 2) * 4 + c) * octants
+            parts.append(jnp.sum(split[0:3, at : at + octants], axis=0, keepdims=True))
         if boxes > leaves * octants:
             parts.append(jnp.zeros((1, boxes - leaves * octants), F32))
         moments.append(jnp.concatenate(parts, axis=1))
     box = lax.broadcasted_iota(jnp.int32, (1, boxes), 1)
-    away = jnp.bitwise_xor(box // 8, leaf) - leaf
+    other = box // 8
+    other = jnp.bitwise_xor(other, turned * (other // 2 % 2))
+    away = jnp.bitwise_xor(other, leaf) - leaf
     far = (jnp.abs(away) >= 2) & (box < leaves * octants)
     away = jnp.where(far, away, 0)
     child = box % 8
@@ -318,7 +328,7 @@
     )
     push = jnp.where(far, jnp.concatenate(moments[0:3], axis=0), 0.0)
     source = jnp.where(far, moments[3], 0.0)
-    x = own_ref[0:3, :]
+    x = own_ref[0, 0:3, :]
     target_ref[...] = target_rows(x)
     sum_ref[...] = jnp.zeros_like(sum_ref)
     groups = [(source_rows(place), source_terms(place, push, source))]
@@ -336,22 +346,24 @@
     )
     for a in range(3):
         flow = flow - 2.0 * x[a : a + 1] * cross[a]
-    turned = [
+    across = [
         jnp.sum(x * cross[c], axis=0, keepdims=True) for c in range(3)
     ]
-    flow_ref[...] = stokes_scale * (flow - jnp.concatenate(turned, axis=0))
+    flow_ref[...] = stokes_scale * (flow - jnp.concatenate(across, axis=0))
     columns = point_columns(shell_ref[...])
     shell = [
         jnp.sum(shell_in[c] + fold(value, 128), axis=1, keepdims=True)
         for c, value in enumerate(direct(columns, place, push, source))
     ]
-    rows, width = dens_ref.shape[1:]
+    width = held_ref.shape[3]
+    rows = block_ref.shape[2] // (leaves * octants * width)
     count = block_ref.shape[1]
 
     def body(at, sums):
+        other = jnp.bitwise_xor(at, turned * (at // 2 % 2))
         for j in range(octants):
-            dens = dens_ref[at * octants + j].astype(F32)
-            owner = jnp.bitwise_xor(at, leaf) * octants + jnp.bitwise_xor(octant, order[j])
+            dens = held_ref[at // 2, (at % 2) * octants + j].astype(F32)
+            owner = jnp.bitwise_xor(other, leaf) * octants + jnp.bitwise_xor(octant, order[j])
             for r in range(rows):
                 start = pl.multiple_of((owner * rows + r) * width, 128)
                 sums = tuple(
@@ -371,20 +383,20 @@
         shell_flow_ref[c : c + 1, :] = jnp.sum(jnp.where(eye, column, 0.0), axis=0, keepdims=True)
 
 
-def finish(order, own, shell_points, moments, dens, shell_block, totals):
-    targets = own.shape[1]
+def finish(order, leaves, own, shell_points, held, shell_block, totals):
+    targets = own.shape[2]
     return pl.pallas_call(
-        functools.partial(finish_kernel, order),
+        functools.partial(finish_kernel, order, leaves),
         out_shape=(
             jax.ShapeDtypeStruct((3, targets), F32),
             jax.ShapeDtypeStruct(shell_points.shape, F32),
         ),
-        in_specs=[VMEM] * 7,
+        in_specs=[VMEM] * 6,
         out_specs=(VMEM, VMEM),
         scratch_shapes=[pltpu.VMEM((32, targets), BF16), pltpu.VMEM((48, targets), F32)],
         compiler_params=PARAMS,
         name="finish",
-    )(own, shell_points, moments, dens, shell_block, *totals)
+    )(own, shell_points, held, shell_block, *totals)
 
 
 def exchange(value, axis, bit):
@@ -399,41 +411,64 @@
 def shards(fibre_solve, fibre_rhs, fibre_points, fibre_owner, shell_points, shell_block, density):
     octants = lax.axis_size("oct")
     leaves = lax.axis_size("leaf")
-    record, dens = prepare(fibre_solve, fibre_rhs, fibre_points, fibre_owner, density)
-    bits = [1 << b for b in range(octants.bit_length() - 1)]
-    bits = bits[1:] + bits[:1]
-    order = [0]
-    records, dens = record[None], dens[None]
+    record, shell = prepare(
+        fibre_solve, fibre_rhs, fibre_points, fibre_owner, density, shell_points
+    )
+    count, width = record.shape[1:]
+
+    def inner_shift(leaf):
+        return 1 - 2 * (leaf % 2)
+
+    def outer_shift(leaf):
+        return 2 * (leaf % 2) - 1
+
+    records, order = record[None], [0]
     fresh, totals = records, None
-    for bit in bits:
-        arrived, arrived_dens = exchange(records, "oct", bit), exchange(dens, "oct", bit)
+    for bit in [1 << b for b in range(1, octants.bit_length() - 1)]:
+        arrived = exchange(records, "oct", bit)
         order = order + [j ^ bit for j in order]
-        if bit != bits[-1]:
-            totals = near(fresh, record, shell_points, None, totals)
-            arrived, arrived_dens, totals = together(arrived, arrived_dens, totals)
-            fresh = arrived
-        else:
-            fresh = jnp.concatenate([fresh, arrived], axis=0)
-        records = jnp.concatenate([records, arrived], axis=0)
-        dens = jnp.concatenate([dens, arrived_dens], axis=0)
-    moments = jnp.sum(records[:, 3, :128], axis=0)[None, None]
-    half = fresh.shape[0] // 2
+        totals = near(fresh, record, shell, None, totals)
+        arrived, totals = together(arrived, totals)
+        records, fresh = jnp.concatenate([records, arrived], axis=0), arrived
     inner = exchange(records, "leaf", 1)
-    inner_dens, inner_moments = exchange(dens, "leaf", 1), exchange(moments, "leaf", 1)
-    totals = near(fresh[:half], record, shell_points, None, totals)
-    late, totals = together(records, totals)
-    pairs = [(i, i + 1) for i in range(1, leaves - 1, 2)]
-    outer = lax.ppermute(late, "leaf", pairs + [(j, i) for i, j in pairs])
-    totals = near(fresh[half:], record, shell_points, None, totals)
-    inner, inner_dens, inner_moments, totals = together(inner, inner_dens, inner_moments, totals)
-    dens = jnp.concatenate([dens, inner_dens], axis=0)
-    moments = jnp.concatenate([moments, inner_moments], axis=0)
-    for bit in [1 << b for b in range(1, leaves.bit_length() - 1)]:
-        dens = jnp.concatenate([dens, exchange(dens, "leaf", bit)], axis=0)
-        moments = jnp.concatenate([moments, exchange(moments, "leaf", bit)], axis=0)
-    totals = near(inner, record, shell_points, lambda leaf: 1 - 2 * (leaf % 2), totals)
-    totals = near(outer, record, shell_points, lambda leaf: 2 * (leaf % 2) - 1, totals)
-    return finish(tuple(order), record, shell_points, moments, dens, shell_block, totals)
+    totals = near(fresh, record, shell, None, totals)
+    inner, totals = together(inner, totals)
+    half = records.shape[0]
+    order = order + [j ^ 1 for j in order]
+    arrived = exchange(jnp.concatenate([records, inner], axis=0), "oct", 1)
+    totals = near(inner, record, shell, inner_shift, totals)
+    arrived, totals = together(arrived, totals)
+    late, late_inner = arrived[:half], arrived[half:]
+    records = jnp.concatenate([records, late], axis=0)
+    inner = jnp.concatenate([inner, late_inner], axis=0)
+    dens = jnp.concatenate([records[:, 2], inner[:, 2]], axis=0).astype(BF16)
+    moments = jnp.concatenate(
+        [jnp.sum(part[:, 0, 3, : 4 * octants], axis=0)[None] for part in (records, inner)], axis=1
+    )
+    high = lax.reduce_precision(moments, 8, 7)
+    middle = lax.reduce_precision(moments - high, 8, 7)
+    low = lax.reduce_precision(moments - high - middle, 8, 7)
+    parts = jnp.concatenate([high, middle, low], axis=0).astype(BF16)
+    parts = jnp.pad(parts, ((0, count - 3), (0, width - parts.shape[1])))
+    held = jnp.concatenate([dens, parts[None]], axis=0)[None]
+    swaps = []
+    for leaf in range(leaves):
+        other = leaf + outer_shift(leaf)
+        for o in range(octants):
+            there = other * octants + o if 0 <= other < leaves else leaf * octants + (o ^ 1)
+            swaps.append((leaf * octants + o, there))
+    outer = lax.ppermute(records[:, :2], ("leaf", "oct"), swaps)
+    across = lax.ppermute(held, ("leaf", "oct"), swaps)
+    totals = near(late, record, shell, None, totals)
+    totals = near(late_inner, record, shell, inner_shift, totals)
+    across, outer, totals = together(across, outer, totals)
+    relayed = exchange(across, "leaf", 1)
+    totals = near(outer, record, shell, outer_shift, totals)
+    direct_pair = (lax.axis_index("leaf") + 1) // 2 % 2 == 1
+    held = jnp.concatenate([held, jnp.where(direct_pair, across, relayed)], axis=0)
+    for bit in [1 << b for b in range(2, leaves.bit_length() - 1)]:
+        held = jnp.concatenate([held, exchange(held, "leaf", bit)], axis=0)
+    return finish(tuple(order), leaves, record, shell, held, shell_block, totals)
 
 
 def solution(mesh):

time: 47.1 us -> 38.1 us (0.81)
  the two profiles are of different devices: /device:TPU:8 before, /device:TPU:9 now
where the time goes in v3:
time: 38.1 us; the launch traced here: 37.7 us
  Pallas kernels  22.4 us (59%)
  starting transfers between devices  8.44 us (22%)
  waiting for transfers between devices  5.35 us (14%)
  between operations  0.81 us (2%)
  other arithmetic  0.68 us (2%)
    pallas_call x7, Pallas kernels, near(): pl.pallas_call(functools.partial(near_kernel, shift, lax.axis_size('leaf'...  18.2 us
    ppermute x5, starting transfers between devices, exchange(): return lax.ppermute(value, axis, [(i, i ^ bit) for i in range(count)])  6.91 us
    ppermute x5, waiting for transfers between devices, exchange(): return lax.ppermute(value, axis, [(i, i ^ bit) for i in range(count)])  4.03 us
    pallas_call x1, Pallas kernels, prepare(): pl.pallas_call(prepare_kernel, out_shape=(jax.ShapeDtypeStruct((3, 4, wid...  2.24 us
    pallas_call x1, Pallas kernels, finish(): pl.pallas_call(functools.partial(finish_kernel, order, leaves), out_shape...  1.94 us
    ppermute x1, starting transfers between devices, shards(): across = lax.ppermute(held, ('leaf', 'oct'), swaps)  1.36 us
    ppermute x1, waiting for transfers between devices, shards(): outer = lax.ppermute(records[:, :2], ('leaf', 'oct'), swaps)  1.32 us
  transfers between devices with their start and end apart: 7, of which 4 were waited for; matrix products, arithmetic and copies ran while one was open for 0% of the time, Pallas kernels for 48%

profile of v3, /device:TPU:9, one launch (start us, length us, event | category | flops | bytes accessed | tf_op | source)
XLA Modules:
  0.0 37.7 jit_solution(3086367141441509066)
XLA Ops:
  0.6 2.2 %prepare.1 = (f32[3,4,768]{2,1,0:T(4,128)S(1)}, f32[3,4]{1,0:T(4,128)S(1)}) custom-call(bf16[12,256,256]{2,1,0:T(8,128)(2,1)} %refs_0_.1, bf16[12,256]{1,0:T(8,128)(2,1)} %refs_1_.1, f32[12,256]{1,0:T(8,128)} %refs_2_.1, s32[12]{0:T(128)} %bitcast.24, f32[3072]{0:T(1024)} %refs_4_.1, f32[3,4]{1,0:T(4,128)} %refs_5_.1), custom_call_target="tpu_custom_call" | custom-call | tf_op jit(solution)/shard_map/prepare/pallas_call | solution.py:103
  2.9 1.3 %collective-permute-start = (f32[1,3,4,768]{3,2,0,1:T(4,128)S(1)}, f32[1,3,4,768]{3,2,0,1:T(4,128)S(1)}, u32[]{:S(2)}, u32[]{:S(2)}) collective-permute-start(f32[1,3,4,768]{3,2,0,1:T(4,128)S(1)} %bitcast.15), channel_id=1, source_target_pairs={{0,2},{1,3},{2,0},{3,1},{4,6},{5,7},{6,4},{7,5},{8,10},{9,11},{10,... | collective-permute-start | bytes 110600 | tf_op jit(solution)/shard_map/ppermute | solution.py:404
  4.2 1.0 %near.7 = (f32[16,768]{1,0:T(8,128)S(1)}, f32[3,4,128]{2,1,0:T(4,128)S(1)}) custom-call(f32[1,3,4,768]{3,2,1,0:T(4,128)S(1)} %bitcast.16, f32[3,4,768]{2,1,0:T(4,128)S(1)} %get-tuple-element.34.refs_1_.own_ref, f32[3,4]{1,0:T(4,128)S(1)} %get-tuple-element.35.refs_2_.shell_ref), custom_call_target="tpu_custom_call" | custom-call | flops 294912000 | bytes 36864 | tf_op jit(solution)/shard_map/near/pallas_call | solution.py:272
  5.1 0.6 %collective-permute-done = f32[1,3,4,768]{3,2,0,1:T(4,128)S(1)} collective-permute-done((f32[1,3,4,768]{3,2,0,1:T(4,128)S(1)}, f32[1,3,4,768]{3,2,0,1:T(4,128)S(1)}, u32[]{:S(2)}, u32[]{:S(2)}) %collective-permute-start) | collective-permute-done | bytes 36896 | tf_op jit(solution)/shard_map/ppermute | solution.py:404
  5.8 1.3 %collective-permute-start.1 = (f32[2,3,4,768]{3,2,0,1:T(4,128)S(1)}, f32[2,3,4,768]{3,2,0,1:T(4,128)S(1)}, u32[]{:S(2)}, u32[]{:S(2)}) collective-permute-start(f32[2,3,4,768]{3,2,0,1:T(4,128)S(1)} %pad_maximum_fusion.5), channel_id=1, source_target_pairs={{0,4},{1,5},{2,6},{3,7},{4,0},{5,1},{6,2},{7,3},{8,12},{9,13},{10,... | collective-permute-start | bytes 221192 | tf_op jit(solution)/shard_map/ppermute | solution.py:404
  7.1 1.0 %near.8 = (f32[16,768]{1,0:T(8,128)S(1)}, f32[3,4,128]{2,1,0:T(4,128)S(1)}) custom-call(f32[1,3,4,768]{3,2,1,0:T(4,128)S(1)} %bitcast.21, f32[3,4,768]{2,1,0:T(4,128)S(1)} %get-tuple-element.34.refs_1_.own_ref, f32[3,4]{1,0:T(4,128)S(1)} %get-tuple-element.35.refs_2_.shell_ref, f32[16,768]{1,0:T(8,128)S(1)} %get-tuple-element.39.refs_3_, ...), custom_call_target="tpu_custom_call" | custom-call | flops 294912000 | bytes 36864 | tf_op jit(solution)/shard_map/near/pallas_call | solution.py:272
  8.0 1.0 %collective-permute-done.1 = f32[2,3,4,768]{3,2,0,1:T(4,128)S(1)} collective-permute-done((f32[2,3,4,768]{3,2,0,1:T(4,128)S(1)}, f32[2,3,4,768]{3,2,0,1:T(4,128)S(1)}, u32[]{:S(2)}, u32[]{:S(2)}) %collective-permute-start.1) | collective-permute-done | bytes 73760 | tf_op jit(solution)/shard_map/ppermute | solution.py:404
  9.1 0.1 collective-permute-start.2
  9.2 1.6 %near.9 = (f32[16,768]{1,0:T(8,128)S(1)}, f32[3,4,128]{2,1,0:T(4,128)S(1)}) custom-call(f32[2,3,4,768]{3,2,1,0:T(4,128)S(1)} %copy.11.refs_0_, f32[3,4,768]{2,1,0:T(4,128)S(1)} %get-tuple-element.34.refs_1_.own_ref, f32[3,4]{1,0:T(4,128)S(1)} %get-tuple-element.35.refs_2_.shell_ref, f32[16,768]{1,0:T(8,128)S(1)} %get-tuple-element.44.refs_3_, ...), custom_call_target="tpu_custom_call" | custom-call | flops 589824000 | bytes 73728 | tf_op jit(solution)/shard_map/near/pallas_call | solution.py:272
  10.8 2.4 %collective-permute-done.2 = f32[4,3,4,768]{3,2,0,1:T(4,128)S(1)} collective-permute-done((f32[4,3,4,768]{3,2,0,1:T(4,128)S(1)}, f32[4,3,4,768]{3,2,0,1:T(4,128)S(1)}, u32[]{:S(2)}, u32[]{:S(2)}) %collective-permute-start.2) | collective-permute-done | bytes 147488 | tf_op jit(solution)/shard_map/ppermute | solution.py:404
  13.2 4.2 %collective-permute-start.3 = (f32[8,3,4,768]{3,2,0,1:T(4,128)S(1)}, f32[8,3,4,768]{3,2,0,1:T(4,128)S(1)}, u32[]{:S(2)}, u32[]{:S(2)}) collective-permute-start(f32[8,3,4,768]{3,2,0,1:T(4,128)S(1)} %pad_maximum_fusion), channel_id=1, source_target_pairs={{0,1},{1,0},{2,3},{3,2},{4,5},{5,4},{6,7},{7,6},{8,9},{9,8},{10,11... | collective-permute-start | bytes 884744 | tf_op jit(solution)/shard_map/ppermute | solution.py:404
  17.4 3.0 %near.10 = (f32[16,768]{1,0:T(8,128)S(1)}, f32[3,4,128]{2,1,0:T(4,128)S(1)}) custom-call(f32[4,3,4,768]{3,2,1,0:T(4,128)S(1)} %copy.12.refs_0_, f32[3,4,768]{2,1,0:T(4,128)S(1)} %get-tuple-element.34.refs_1_.own_ref, f32[3,4]{1,0:T(4,128)S(1)} %get-tuple-element.35.refs_2_.shell_ref, f32[16,768]{1,0:T(8,128)S(1)} %get-tuple-element.49.refs_3_, ...), custom_call_target="tpu_custom_call" | custom-call | flops 1179648000 | bytes 147456 | tf_op jit(solution)/shard_map/near/pallas_call | solution.py:272
  20.4 0.1 pad_maximum_fusion.1
  20.7 0.1 reduce-precision_convert_fusion.1
  20.8 0.1 maximum_bitcast_fusion
  20.8 1.4 %collective-permute-start.4 = (bf16[1,17,4,768]{3,2,1,0:T(4,128)(2,1)S(1)}, bf16[1,17,4,768]{3,2,1,0:T(4,128)(2,1)S(1)}, u32[]{:S(2)}, u32[]{:S(2)}) collective-permute-start(bf16[1,17,4,768]{3,2,1,0:T(4,128)(2,1)S(1)} %maximum_bitcast_fusion), channel_id=1, source_target_pairs={{0,1},{1,0},{2,3},{3,2},{4,5},{5,4},{6,7},{7,6},{8,16},{9,17},{10,... | collective-permute-start | bytes 313352 | tf_op jit(solution)/shard_map/ppermute | solution.py:461
  22.2 0.2 collective-permute-start.5
  22.4 2.8 %near.11 = (f32[16,768]{1,0:T(8,128)S(1)}, f32[3,4,128]{2,1,0:T(4,128)S(1)}) custom-call(f32[4,3,4,768]{3,2,1,0:T(4,128)S(1)} %copy.13.refs_0_, f32[3,4,768]{2,1,0:T(4,128)S(1)} %get-tuple-element.34.refs_1_.own_ref, f32[3,4]{1,0:T(4,128)S(1)} %get-tuple-element.35.refs_2_.shell_ref, f32[16,768]{1,0:T(8,128)S(1)} %get-tuple-element.54.refs_3_, ...), custom_call_target="tpu_custom_call" | custom-call | flops 1179648000 | bytes 147456 | tf_op jit(solution)/shard_map/near/pallas_call | solution.py:272
  25.2 3.1 %near.12 = (f32[16,768]{1,0:T(8,128)S(1)}, f32[3,4,128]{2,1,0:T(4,128)S(1)}) custom-call(f32[4,3,4,768]{3,2,1,0:T(4,128)S(1)} %copy.14.refs_0_, f32[3,4,768]{2,1,0:T(4,128)S(1)} %get-tuple-element.34.refs_1_.own_ref, f32[3,4]{1,0:T(4,128)S(1)} %get-tuple-element.35.refs_2_.shell_ref, f32[16,768]{1,0:T(8,128)S(1)} %get-tuple-element.56.refs_3_, ...), custom_call_target="tpu_custom_call" | custom-call | flops 1179648000 | bytes 147456 | tf_op jit(solution)/shard_map/near/pallas_call | solution.py:272
  28.3 1.3 %collective-permute-done.5 = f32[8,2,4,768]{3,2,0,1:T(4,128)S(1)} collective-permute-done((f32[8,2,4,768]{3,2,0,1:T(4,128)S(1)}, f32[8,2,4,768]{3,2,0,1:T(4,128)S(1)}, u32[]{:S(2)}, u32[]{:S(2)}) %collective-permute-start.5) | collective-permute-done | bytes 196640 | tf_op jit(solution)/shard_map/ppermute | solution.py:460
  29.7 0.1 collective-permute-start.6
  29.7 5.8 %near.13 = (f32[16,768]{1,0:T(8,128)S(1)}, f32[3,4,128]{2,1,0:T(4,128)S(1)}) custom-call(f32[8,2,4,768]{3,2,1,0:T(4,128)S(1)} %copy.15.refs_0_, f32[3,4,768]{2,1,0:T(4,128)S(1)} %get-tuple-element.34.refs_1_.own_ref, f32[3,4]{1,0:T(4,128)S(1)} %get-tuple-element.35.refs_2_.shell_ref, f32[16,768]{1,0:T(8,128)S(1)} %get-tuple-element.62.refs_3_, ...), custom_call_target="tpu_custom_call" | custom-call | flops 2359296000 | bytes 196608 | tf_op jit(solution)/shard_map/near/pallas_call | solution.py:272
  35.6 0.1 pad_maximum_fusion.3.held_ref
  35.8 1.9 %finish.1 = (f32[3,768]{1,0:T(4,128)}, f32[3,4]{1,0:T(4,128)}) custom-call(f32[3,4,768]{2,1,0:T(4,128)S(1)} %get-tuple-element.34.refs_1_.own_ref, f32[3,4]{1,0:T(4,128)S(1)} %get-tuple-element.35.refs_2_.shell_ref, bf16[2,17,4,768]{3,2,1,0:T(4,128)(2,1)S(1)} %pad_maximum_fusion.3.held_ref, bf16[3,4,98304]{2,1,0:T(4,128)(2,1)S(1)} %copy-done, ...), custom_call_target="tpu_custom_call" | custom-call | tf_op jit(solution)/shard_map/finish/pallas_call | solution.py:388
  (21 shorter events, 0.4 us)
Async XLA Ops:
  2.9 2.9 %collective-permute-start = (f32[1,3,4,768]{3,2,0,1:T(4,128)S(1)}, f32[1,3,4,768]{3,2,0,1:T(4,128)S(1)}, u32[]{:S(2)}, u32[]{:S(2)}) collective-permute-start(f32[1,3,4,768]{3,2,0,1:T(4,128)S(1)} %bitcast.15), channel_id=1, source_target_pairs={{0,2},{1,3},{2,0},{3,1},{4,6},{5,7},{6,4},{7,5},{8,10},{9,11},{10,... | collective-permute-start | bytes 110600 | tf_op jit(solution)/shard_map/ppermute | solution.py:404
  5.8 3.3 %collective-permute-start.1 = (f32[2,3,4,768]{3,2,0,1:T(4,128)S(1)}, f32[2,3,4,768]{3,2,0,1:T(4,128)S(1)}, u32[]{:S(2)}, u32[]{:S(2)}) collective-permute-start(f32[2,3,4,768]{3,2,0,1:T(4,128)S(1)} %pad_maximum_fusion.5), channel_id=1, source_target_pairs={{0,4},{1,5},{2,6},{3,7},{4,0},{5,1},{6,2},{7,3},{8,12},{9,13},{10,... | collective-permute-start | bytes 221192 | tf_op jit(solution)/shard_map/ppermute | solution.py:404
  9.1 4.1 %collective-permute-start.2 = (f32[4,3,4,768]{3,2,0,1:T(4,128)S(1)}, f32[4,3,4,768]{3,2,0,1:T(4,128)S(1)}, u32[]{:S(2)}, u32[]{:S(2)}) collective-permute-start(f32[4,3,4,768]{3,2,0,1:T(4,128)S(1)} %pad_maximum_fusion.4), channel_id=1, source_target_pairs={{0,8},{8,0},{16,24},{24,16},{1,9},{9,1},{17,25},{25,17},{2,10},{10... | collective-permute-start | bytes 442376 | tf_op jit(solution)/shard_map/ppermute | solution.py:404
  13.2 7.2 %collective-permute-start.3 = (f32[8,3,4,768]{3,2,0,1:T(4,128)S(1)}, f32[8,3,4,768]{3,2,0,1:T(4,128)S(1)}, u32[]{:S(2)}, u32[]{:S(2)}) collective-permute-start(f32[8,3,4,768]{3,2,0,1:T(4,128)S(1)} %pad_maximum_fusion), channel_id=1, source_target_pairs={{0,1},{1,0},{2,3},{3,2},{4,5},{5,4},{6,7},{7,6},{8,9},{9,8},{10,11... | collective-permute-start | bytes 884744 | tf_op jit(solution)/shard_map/ppermute | solution.py:404
  20.8 7.5 %collective-permute-start.4 = (bf16[1,17,4,768]{3,2,1,0:T(4,128)(2,1)S(1)}, bf16[1,17,4,768]{3,2,1,0:T(4,128)(2,1)S(1)}, u32[]{:S(2)}, u32[]{:S(2)}) collective-permute-start(bf16[1,17,4,768]{3,2,1,0:T(4,128)(2,1)S(1)} %maximum_bitcast_fusion), channel_id=1, source_target_pairs={{0,1},{1,0},{2,3},{3,2},{4,5},{5,4},{6,7},{7,6},{8,16},{9,17},{10,... | collective-permute-start | bytes 313352 | tf_op jit(solution)/shard_map/ppermute | solution.py:461
  22.2 7.4 %collective-permute-start.5 = (f32[8,2,4,768]{3,2,0,1:T(4,128)S(1)}, f32[8,2,4,768]{3,2,0,1:T(4,128)S(1)}, u32[]{:S(2)}, u32[]{:S(2)}) collective-permute-start(f32[8,2,4,768]{3,2,0,1:T(4,128)S(1)} %slice.34), channel_id=1, source_target_pairs={{0,1},{1,0},{2,3},{3,2},{4,5},{5,4},{6,7},{7,6},{8,16},{9,17},{10,... | collective-permute-start | bytes 589832 | tf_op jit(solution)/shard_map/ppermute | solution.py:460
  29.7 6.1 %copy-start = (bf16[3,4,98304]{2,1,0:T(4,128)(2,1)S(1)}, bf16[3,4,98304]{2,1,0:T(4,128)(2,1)}, u32[]{:S(2)}) copy-start(bf16[3,4,98304]{2,1,0:T(4,128)(2,1)} %block_ref.1) | copy-start | bytes 7077892
  29.7 5.9 %collective-permute-start.6 = (bf16[1,17,4,768]{3,2,1,0:T(4,128)(2,1)S(1)}, bf16[1,17,4,768]{3,2,1,0:T(4,128)(2,1)S(1)}, u32[]{:S(2)}, u32[]{:S(2)}) collective-permute-start(bf16[1,17,4,768]{3,2,1,0:T(4,128)(2,1)S(1)} %collective-permute-done.4), channel_id=1, source_target_pairs={{0,8},{8,0},{16,24},{24,16},{1,9},{9,1},{17,25},{25,17},{2,10},{10... | collective-permute-start | bytes 313352 | tf_op jit(solution)/shard_map/ppermute | solution.py:404

commit v4 on v3

v4 whole, which is shorter than its diff:
```python
import functools
import math

import jax
import jax.numpy as jnp
from jax import lax
from jax.experimental import pallas as pl
from jax.experimental.pallas import tpu as pltpu
from jax.sharding import PartitionSpec as P

smooth_sq = 0.01
stokes_scale = 1.0 / (8.0 * math.pi)
F32 = jnp.float32
BF16 = jnp.bfloat16
VMEM = pl.BlockSpec(memory_space=pltpu.VMEM)
PARAMS = pltpu.CompilerParams(vmem_limit_bytes=40 * 2**20)


def split3(value):
    high = value.astype(BF16).astype(F32)
    rest = value - high
    middle = rest.astype(BF16).astype(F32)
    return high, middle, (rest - middle).astype(BF16).astype(F32)


def prepare_kernel(*refs):
    solve_hbm, rhs_hbm, points_hbm, owner_hbm, density_hbm, shell_hbm = refs[:6]
    record_ref, target_ref, column_ref = refs[6:9]
    solve_ref, rhs_ref, points_ref, density_ref, shell_ref, owner_ref, solve_sem, sem = refs[9:]
    fibres, quads = rhs_ref.shape
    nodes = quads // 4
    width = record_ref.shape[2]
    part = math.gcd(fibres, 4)
    copies = [
        pltpu.make_async_copy(owner_hbm, owner_ref, sem.at[0]),
        pltpu.make_async_copy(points_hbm, points_ref, sem.at[1]),
        pltpu.make_async_copy(rhs_hbm, rhs_ref, sem.at[2]),
        pltpu.make_async_copy(density_hbm, density_ref, sem.at[3]),
        pltpu.make_async_copy(shell_hbm, shell_ref, sem.at[4]),
    ]
    solves = [
        pltpu.make_async_copy(
            solve_hbm.at[pl.ds(f, part)], solve_ref.at[pl.ds(f, part)], solve_sem.at[f // part]
        )
        for f in range(0, fibres, part)
    ]
    for copy in copies + solves:
        copy.start()
    for copy in copies:
        copy.wait()
    record_ref[2] = jnp.zeros(record_ref.shape[1:], F32)
    for r in range(density_ref.shape[0] // width):
        dens = density_ref[r * width : (r + 1) * width].reshape(1, width)
        record_ref[2, r : r + 1, :] = dens.astype(BF16).astype(F32)
    row = lax.broadcasted_iota(jnp.int32, (fibres, 1), 0)
    owner = jnp.zeros((fibres, 1), jnp.int32)
    for f in range(fibres):
        owner = jnp.where(row == f, owner_ref[f], owner)
    points = points_ref[...]
    corner = [owner % 2, owner // 2 % 2, owner // 4]
    place = [
        points[:, c * nodes : (c + 1) * nodes] + (corner[c].astype(F32) - 1.0) for c in range(3)
    ]
    for f in range(fibres):
        lanes = slice(f * nodes, (f + 1) * nodes)
        for c in range(3):
            record_ref[0, c : c + 1, lanes] = place[c][f : f + 1, :]
    quad_weight = points[:, 3 * nodes :]
    rhs = rhs_ref[...]
    forces = jnp.zeros((fibres, quads), F32)
    for f in range(fibres):
        if f % part == 0:
            solves[f // part].wait()
        product = lax.dot_general(
            rhs, solve_ref[f], (((1,), (1,)), ((), ())), preferred_element_type=F32
        )
        forces = jnp.where(row == f, product, forces)
    pushes = forces * jnp.concatenate([quad_weight] * 4, axis=1)
    for f in range(fibres):
        lanes = slice(f * nodes, (f + 1) * nodes)
        for c in range(4):
            record_ref[1, c : c + 1, lanes] = pushes[f : f + 1, c * nodes : (c + 1) * nodes]
    lane = lax.broadcasted_iota(jnp.int32, (fibres, width), 1)
    sums = jnp.zeros((fibres, width), F32)
    for c in range(4):
        box_sum = jnp.sum(pushes[:, c * nodes : (c + 1) * nodes], axis=1, keepdims=True)
        sums = jnp.where(lane == owner + 8 * c, box_sum, sums)
    record_ref[0, 3:4, :] = jnp.sum(sums, axis=0, keepdims=True)
    target_ref[...] = target_rows(record_ref[0, 0:3, :])
    for c, column in enumerate(point_columns(shell_ref[...])):
        column_ref[c] = jnp.broadcast_to(column, column_ref.shape[1:])


def prepare(fibre_solve, fibre_rhs, fibre_points, fibre_owner, density, shell_points):
    fibres, quads = fibre_points.shape
    width = fibres * quads // 4
    inputs = (
        fibre_solve,
        fibre_rhs,
        fibre_points,
        fibre_owner.reshape(fibres),
        density,
        shell_points,
    )
    return pl.pallas_call(
        prepare_kernel,
        out_shape=(
            jax.ShapeDtypeStruct((3, 4, width), F32),
            jax.ShapeDtypeStruct((32, width), BF16),
            jax.ShapeDtypeStruct((3, shell_points.shape[1], 128), F32),
        ),
        in_specs=[pl.BlockSpec(memory_space=pltpu.HBM)] * 6,
        out_specs=(VMEM, VMEM, VMEM),
        scratch_shapes=[
            pltpu.VMEM(fibre_solve.shape, BF16),
            pltpu.VMEM(fibre_rhs.shape, BF16),
            pltpu.VMEM(fibre_points.shape, F32),
            pltpu.VMEM(density.shape, F32),
            pltpu.VMEM(shell_points.shape, F32),
            pltpu.SMEM((fibres,), jnp.int32),
            pltpu.SemaphoreType.DMA((fibres,)),
            pltpu.SemaphoreType.DMA((5,)),
        ],
        compiler_params=PARAMS,
        name="prepare",
    )(*[pltpu.with_memory_space_constraint(value, pltpu.HBM) for value in inputs])


def target_rows(place):
    sq = jnp.sum(place * place, axis=0, keepdims=True)
    high, middle, low = split3(place)
    one = jnp.ones_like(sq)
    zero = jnp.zeros_like(sq)
    sq_parts = split3(sq)
    return jnp.concatenate(
        [-2.0 * high, one] * 3
        + [-2.0 * middle, zero] * 2
        + [-2.0 * low, zero]
        + list(sq_parts)
        + [zero] * 5,
        axis=0,
    ).astype(BF16)


def source_rows(place):
    sq = jnp.sum(place * place, axis=0, keepdims=True) + smooth_sq
    high, middle, low = split3(jnp.concatenate([place, sq], axis=0))
    one = jnp.ones((3, place.shape[1]), F32)
    zero = jnp.zeros((5, place.shape[1]), F32)
    return jnp.concatenate([high, middle, low, high, middle, high, one, zero], axis=0).astype(BF16)


def source_terms(place, push, source):
    sq = jnp.sum(place * place, axis=0, keepdims=True) + 2.0 * smooth_sq
    rest = source - jnp.sum(place * push, axis=0, keepdims=True)
    terms = jnp.concatenate(
        [push, rest, sq * push - rest * place] + [place[a : a + 1] * push for a in range(3)], axis=0
    )
    return jnp.concatenate(split3(terms), axis=0).astype(BF16)


def sum_sources(target_ref, groups, block):
    totals = []
    for t in range(0, target_ref.shape[1], block):
        total = None
        for rows, terms in groups:
            width = rows.shape[1]
            lead = terms.shape[0] // 3
            step = min(block, width)
            for s in range(0, width, step):
                d = lax.dot_general(
                    rows[:, s : s + step],
                    target_ref[:, t : t + block],
                    (((0,), (0,)), ((), ())),
                    preferred_element_type=F32,
                )
                inverse = lax.rsqrt(d)
                cube = inverse * inverse * inverse
                high = cube.astype(BF16)
                low = (cube - high.astype(F32)).astype(BF16)
                term = terms[:, s : s + step]
                part = jnp.dot(term, high, preferred_element_type=F32)
                rest = jnp.dot(term[:lead], low, preferred_element_type=F32)
                part = jnp.concatenate([part[:lead] + rest, part[lead:]], axis=0)
                total = part if total is None else total + part
        totals.append(total[:lead] + total[lead : 2 * lead] + total[2 * lead :])
    return totals


def point_columns(points):
    count = points.shape[1]
    eye = lax.broadcasted_iota(jnp.int32, (count, count), 0) == lax.broadcasted_iota(
        jnp.int32, (count, count), 1
    )
    return [
        2.0 * jnp.sum(jnp.where(eye, points[c : c + 1], 0.0), axis=1, keepdims=True) - 1.0
        for c in range(3)
    ]


def direct(columns, place, push, source):
    offset = [columns[c] - place[c : c + 1] for c in range(3)]
    sq = offset[0] * offset[0] + offset[1] * offset[1] + offset[2] * offset[2]
    inverse = lax.rsqrt(sq + smooth_sq)
    cube = inverse * inverse * inverse
    along = source + (
        offset[0] * push[0:1] + offset[1] * push[1:2] + offset[2] * push[2:3]
    )
    spread = cube * (sq + 2.0 * smooth_sq)
    along = cube * along
    return [spread * push[c : c + 1] + along * offset[c] for c in range(3)]


def fold(value, lanes):
    total = value[:, :lanes]
    for at in range(lanes, value.shape[1], lanes):
        total = total + value[:, at : at + lanes]
    return total


def near_kernel(shift, leaves, first, *refs):
    records_ref, target_ref, column_ref = refs[:3]
    total_in, shell_in = (None, None) if first else refs[3:5]
    total_ref, shell_total_ref = refs[-2:]
    columns = [column_ref[c][:, 0:1] for c in range(3)]
    if shift is not None:
        leaf = lax.axis_index("leaf")
        moved = (2 * shift(leaf)).astype(F32)
    targets = target_ref.shape[1]
    block = min(256, targets)

    def run():
        groups = []
        shell = [None if first else shell_in[c] for c in range(3)]
        for j in range(records_ref.shape[0]):
            record = records_ref.at[j]
            place = record[0, 0:3, :]
            if shift is not None:
                axis = lax.broadcasted_iota(jnp.int32, place.shape, 0)
                place = place + jnp.where(axis == 0, moved, 0.0)
            push, source = record[1, 0:3, :], record[1, 3:4, :]
            groups.append((source_rows(place), source_terms(place, push, source)))
            for c, value in enumerate(direct(columns, place, push, source)):
                value = fold(value, 128)
                shell[c] = value if shell[c] is None else shell[c] + value
        for at, value in enumerate(sum_sources(target_ref, groups, block)):
            lanes = slice(at * block, (at + 1) * block)
            total_ref[:, lanes] = value if first else value + total_in[:, lanes]
        for c in range(3):
            shell_total_ref[c] = shell[c]

    if shift is None:
        run()
        return
    there = leaf + shift(leaf)
    inside = (there >= 0) & (there < leaves)
    pl.when(inside)(run)

    @pl.when(jnp.logical_not(inside))
    def _():
        total_ref[...] = total_in[...]
        shell_total_ref[...] = shell_in[...]


def near(records, own, shift, totals):
    target_rows, columns = own
    targets = target_rows.shape[1]
    out = (jax.ShapeDtypeStruct((16, targets), F32), jax.ShapeDtypeStruct(columns.shape, F32))
    pairs = records.shape[0] * records.shape[3] * targets
    return pl.pallas_call(
        functools.partial(near_kernel, shift, lax.axis_size("leaf"), totals is None),
        out_shape=out,
        in_specs=[VMEM] * (3 if totals is None else 5),
        out_specs=(VMEM, VMEM),
        compiler_params=PARAMS,
        cost_estimate=pl.CostEstimate(
            flops=500 * pairs, bytes_accessed=records.size * 4, transcendentals=pairs
        ),
        name="near",
    )(records, target_rows, columns, *(totals or ()))


def super_box(position, leaf):
    turned = (leaf + 1) // 2 % 2
    return jnp.bitwise_xor(jnp.bitwise_xor(position, turned * (position // 2 % 2)), leaf)


def block_product(order, leaves, first, held_ref, block_ref):
    leaf, octant = lax.axis_index("leaf"), lax.axis_index("oct")
    octants = len(order)
    width = held_ref.shape[3]
    rows = block_ref.shape[2] // (leaves * octants * width)
    count = block_ref.shape[1]

    def body(at, sums):
        position = at + first
        seat = jnp.bitwise_xor(octant, position // 2 % 2)
        box = super_box(position, leaf)
        for j in range(octants):
            dens = held_ref[at // 2, (at % 2) * octants + j].astype(F32)
            owner = box * octants + jnp.bitwise_xor(seat, order[j])
            for r in range(rows):
                start = pl.multiple_of((owner * rows + r) * width, 128)
                sums = tuple(
                    sums[c] + block_ref[c, :, pl.ds(start, width)].astype(F32) * dens[r : r + 1]
                    for c in range(3)
                )
        return sums

    zero = jnp.zeros((count, width), F32)
    steps = 2 * held_ref.shape[0]
    return lax.fori_loop(0, steps, body, (zero, zero, zero), unroll=steps <= 4)


def shell_rows_kernel(order, leaves, held_ref, block_ref, product_ref):
    for c, value in enumerate(block_product(order, leaves, 0, held_ref, block_ref)):
        product_ref[c] = fold(value, 128)


def shell_rows(order, leaves, held, shell_block):
    return pl.pallas_call(
        functools.partial(shell_rows_kernel, order, leaves),
        out_shape=jax.ShapeDtypeStruct((3, shell_block.shape[1], 128), F32),
        in_specs=[VMEM] * 2,
        out_specs=VMEM,
        compiler_params=PARAMS,
        name="shell_rows",
    )(held, shell_block)


def finish_kernel(
    order,
    leaves,
    own_ref,
    target_ref,
    column_ref,
    held_ref,
    block_ref,
    product_in,
    total_in,
    shell_in,
    flow_ref,
    shell_flow_ref,
):
    leaf = lax.axis_index("leaf")
    octants = len(order)
    used = 2 * held_ref.shape[0] * octants
    boxes = -(-used // 128) * 128
    moments = []
    for c in range(4):
        parts = []
        for j in range(2 * held_ref.shape[0]):
            split = held_ref[j // 2, 2 * octants].astype(F32)
            at = ((j % 2) * 4 + c) * octants
            parts.append(jnp.sum(split[0:3, at : at + octants], axis=0, keepdims=True))
        if boxes > used:
            parts.append(jnp.zeros((1, boxes - used), F32))
        moments.append(jnp.concatenate(parts, axis=1))
    box = lax.broadcasted_iota(jnp.int32, (1, boxes), 1)
    away = super_box(box // 8 + 2, leaf) - leaf
    far = (jnp.abs(away) >= 2) & (box < used)
    away = jnp.where(far, away, 0)
    child = box % 8
    place = jnp.concatenate(
        [
            (2 * away + child % 2).astype(F32) - 0.5,
            (child // 2 % 2).astype(F32) - 0.5,
            (child // 4).astype(F32) - 0.5,
        ],
        axis=0,
    )
    push = jnp.where(far, jnp.concatenate(moments[0:3], axis=0), 0.0)
    source = jnp.where(far, moments[3], 0.0)
    x = own_ref[0, 0:3, :]
    groups = [(source_rows(place), source_terms(place, push, source))]
    far_sums = sum_sources(target_ref, groups, min(256, x.shape[1]))
    total = total_in[...] + jnp.concatenate(far_sums, axis=1)
    push_sum, rest_sum, constant = total[0:3], total[3:4], total[4:7]
    cross = [total[7 + 3 * a : 10 + 3 * a] for a in range(3)]
    flow = (
        jnp.sum(x * x, axis=0, keepdims=True) * push_sum
        + constant
        + x * (jnp.sum(x * push_sum, axis=0, keepdims=True) + rest_sum)
    )
    for a in range(3):
        flow = flow - 2.0 * x[a : a + 1] * cross[a]
    across = [
        jnp.sum(x * cross[c], axis=0, keepdims=True) for c in range(3)
    ]
    flow_ref[...] = stokes_scale * (flow - jnp.concatenate(across, axis=0))
    columns = [column_ref[c][:, 0:1] for c in range(3)]
    shell = [
        jnp.sum(shell_in[c] + fold(value, 128), axis=1, keepdims=True)
        for c, value in enumerate(direct(columns, place, push, source))
    ]
    count = block_ref.shape[1]
    product = [
        jnp.sum(product_in[c] + fold(value, 128), axis=1, keepdims=True)
        for c, value in enumerate(block_product(order, leaves, 2, held_ref, block_ref))
    ]
    eye = lax.broadcasted_iota(jnp.int32, (count, count), 0) == lax.broadcasted_iota(
        jnp.int32, (count, count), 1
    )
    for c in range(3):
        column = product[c] + stokes_scale * shell[c]
        shell_flow_ref[c : c + 1, :] = jnp.sum(jnp.where(eye, column, 0.0), axis=0, keepdims=True)


def finish(order, leaves, record, own, held, shell_block, product, totals):
    targets, points = record.shape[2], shell_block.shape[1]
    return pl.pallas_call(
        functools.partial(finish_kernel, order, leaves),
        out_shape=(
            jax.ShapeDtypeStruct((3, targets), F32),
            jax.ShapeDtypeStruct((3, points), F32),
        ),
        in_specs=[VMEM] * 8,
        out_specs=(VMEM, VMEM),
        compiler_params=PARAMS,
        name="finish",
    )(record, *own, held, shell_block, product, *totals)


def exchange(value, bits):
    devices = lax.axis_size("leaf") * lax.axis_size("oct")
    return lax.ppermute(value, ("leaf", "oct"), [(i, i ^ bits) for i in range(devices)])


def together(*values):
    return lax.optimization_barrier(values)


def shards(fibre_solve, fibre_rhs, fibre_points, fibre_owner, shell_points, shell_block, density):
    octants = lax.axis_size("oct")
    leaves = lax.axis_size("leaf")
    record, *own = prepare(
        fibre_solve, fibre_rhs, fibre_points, fibre_owner, density, shell_points
    )
    count, width = record.shape[1:]

    def inner_shift(leaf):
        return 1 - 2 * (leaf % 2)

    def outer_shift(leaf):
        return 2 * (leaf % 2) - 1

    order = [0]
    for bit in [1 << b for b in range(1, octants.bit_length() - 1)]:
        order = order + [j ^ bit ^ 1 for j in order]
    arrived = [exchange(record, j) for j in order[1:]]
    totals = near(record[None], own, None, None)
    *arrived, totals = together(*arrived, totals)
    fresh = jnp.stack(arrived)
    records = jnp.stack([record] + arrived)
    swaps = []
    for leaf in range(leaves):
        there = leaf + outer_shift(leaf)
        there = there if 0 <= there < leaves else leaf
        swaps += [(leaf * octants + o, there * octants + (o ^ 1)) for o in range(octants)]
    order = order + [j ^ 1 for j in order]
    inner = exchange(records, octants + 1)
    late = exchange(records, 1)
    totals = near(fresh, own, None, totals)
    late, totals = together(late, totals)
    records = jnp.concatenate([records, late], axis=0)
    outer = lax.ppermute(records[:, :2], ("leaf", "oct"), swaps)
    totals = near(late, own, None, totals)
    inner, totals = together(inner, totals)
    late_inner = exchange(inner, 1)
    totals = near(inner, own, inner_shift, totals)
    late_inner, totals = together(late_inner, totals)
    inner = jnp.concatenate([late_inner, inner], axis=0)
    dens = jnp.concatenate([records[:, 2], inner[:, 2]], axis=0).astype(BF16)
    moments = jnp.concatenate(
        [jnp.sum(part[:, 0, 3, : 4 * octants], axis=0)[None] for part in (records, inner)], axis=1
    )
    high = lax.reduce_precision(moments, 8, 7)
    middle = lax.reduce_precision(moments - high, 8, 7)
    low = lax.reduce_precision(moments - high - middle, 8, 7)
    parts = jnp.concatenate([high, middle, low], axis=0).astype(BF16)
    parts = jnp.pad(parts, ((0, count - 3), (0, width - parts.shape[1])))
    held = jnp.concatenate([dens, parts[None]], axis=0)[None]
    across = lax.ppermute(held, ("leaf", "oct"), swaps)
    totals = near(late_inner, own, inner_shift, totals)
    held, totals = together(held, totals)
    product = shell_rows(tuple(order), leaves, held, shell_block)
    across, product, totals = together(across, product, totals)
    relayed = exchange(across, octants)
    totals = near(outer, own, outer_shift, totals)
    straight = (lax.axis_index("leaf") + 1) // 2 % 2 == 1
    rest = jnp.where(straight, across, relayed)
    for bit in [1 << b for b in range(2, leaves.bit_length() - 1)]:
        whole = jnp.concatenate([held, rest], axis=0)
        rest = jnp.concatenate([rest, exchange(whole, bit * octants)], axis=0)
    return finish(tuple(order), leaves, record, own, rest, shell_block, product, totals)


def solution(mesh):
    placed = (
        P(("leaf", "oct"), None, None),
        P(("leaf", "oct"), None),
        P(("leaf", "oct"), None),
        P(("leaf", "oct"), None),
        P(None, ("leaf", "oct")),
        P(None, ("leaf", "oct"), None),
        P(("leaf", "oct")),
    )
    return jax.shard_map(
        shards,
        mesh=mesh,
        in_specs=placed,
        out_specs=(P(None, ("leaf", "oct")), P(None, ("leaf", "oct"))),
        check_vma=False,
    )
```

time: 38.1 us -> 33.8 us (0.89)
  waiting for transfers between devices: 5.35 us -> 3.45 us
  starting transfers between devices: 8.44 us -> 7.01 us
  Pallas kernels: 22.4 us -> 21.4 us
    ppermute x5 -> x7, starting transfers between devices: 6.91 us -> 4.05 us  [exchange(): lax.ppermute(value, ('leaf', 'oct'), [(i, i ^ bits) for i in range(device...]
    ppermute x1, starting transfers between devices: 0.17 us -> 2.86 us  [shards(): outer = lax.ppermute(records[:, :2], ('leaf', 'oct'), swaps)]
    ppermute x5 -> x7, waiting for transfers between devices: 4.03 us -> 2.39 us  [exchange(): lax.ppermute(value, ('leaf', 'oct'), [(i, i ^ bits) for i in range(device...]
    ppermute x1, waiting for transfers between devices: 1.32 us -> 0.01 us  [shards(): outer = lax.ppermute(records[:, :2], ('leaf', 'oct'), swaps)]
    ppermute x1, starting transfers between devices: 1.36 us -> 0.1 us  [shards(): across = lax.ppermute(held, ('leaf', 'oct'), swaps)]
    ppermute x1, waiting for transfers between devices: 0.01 us -> 1.05 us  [shards(): across = lax.ppermute(held, ('leaf', 'oct'), swaps)]
    pallas_call x7 -> x6, Pallas kernels: 18.2 us -> 17.4 us  [near(): pl.pallas_call(functools.partial(near_kernel, shift, lax.axis_size('leaf'...]
    pallas_call x1, Pallas kernels: 1.94 us -> 1.35 us  [finish(): pl.pallas_call(functools.partial(finish_kernel, order, leaves), out_shape...]
  transfers between devices with their start and end apart: 7 -> 9, of which waited for: 4 -> 3; matrix products, arithmetic and copies ran while one was open for 0% -> 1% of each run, Pallas kernels for 48% -> 54%
where the time goes in v4:
time: 33.8 us; the launch traced here: 33.2 us
  Pallas kernels  21.4 us (63%)
  starting transfers between devices  7.01 us (21%)
  waiting for transfers between devices  3.45 us (10%)
  between operations  0.81 us (2%)
  other arithmetic  0.36 us (1%)
    pallas_call x6, Pallas kernels, near(): pl.pallas_call(functools.partial(near_kernel, shift, lax.axis_size('leaf'...  17.4 us
    ppermute x7, starting transfers between devices, exchange(): lax.ppermute(value, ('leaf', 'oct'), [(i, i ^ bits) for i in range(device...  4.05 us
    ppermute x1, starting transfers between devices, shards(): outer = lax.ppermute(records[:, :2], ('leaf', 'oct'), swaps)  2.86 us
    ppermute x7, waiting for transfers between devices, exchange(): lax.ppermute(value, ('leaf', 'oct'), [(i, i ^ bits) for i in range(device...  2.39 us
    pallas_call x1, Pallas kernels, prepare(): pl.pallas_call(prepare_kernel, out_shape=(jax.ShapeDtypeStruct((3, 4, wid...  2.24 us
    pallas_call x1, Pallas kernels, finish(): pl.pallas_call(functools.partial(finish_kernel, order, leaves), out_shape...  1.35 us
    ppermute x1, waiting for transfers between devices, shards(): across = lax.ppermute(held, ('leaf', 'oct'), swaps)  1.05 us
  transfers between devices with their start and end apart: 9, of which 3 were waited for; matrix products, arithmetic and copies ran while one was open for 1% of the time, Pallas kernels for 54%

profile of v4, /device:TPU:9, one launch (start us, length us, event | category | flops | bytes accessed | tf_op | source)
XLA Modules:
  0.0 33.2 jit_solution(2132577928616993655)
XLA Ops:
  0.6 2.2 %prepare.1 = (f32[3,4,768]{2,1,0:T(4,128)S(1)}, bf16[32,768]{1,0:T(8,128)(2,1)S(1)}, f32[3,4,128]{2,1,0:T(4,128)S(1)}) custom-call(bf16[12,256,256]{2,1,0:T(8,128)(2,1)} %refs_0_.1, bf16[12,256]{1,0:T(8,128)(2,1)} %refs_1_.1, f32[12,256]{1,0:T(8,128)} %refs_2_.1, s32[12]{0:T(128)} %bitcast.31, f32[3072]{0:T(1024)} %refs_4_.1, f32[3,4]{1,0:T(4,128)} %refs_5_.1), custom_call_target="tpu_custom_call" | custom-call | tf_op jit(solution)/shard_map/prepare/pallas_call | solution.py:105
  2.9 2.2 %collective-permute-start.2 = (f32[3,4,768]{2,1,0:T(4,128)S(1)}, f32[3,4,768]{2,1,0:T(4,128)S(1)}, u32[]{:S(2)}, u32[]{:S(2)}) collective-permute-start(f32[3,4,768]{2,1,0:T(4,128)S(1)} %get-tuple-element.38.own_ref), channel_id=1, source_target_pairs={{0,6},{1,7},{2,4},{3,5},{4,2},{5,3},{6,0},{7,1},{8,14},{9,15},{10,... | collective-permute-start | bytes 110600 | tf_op jit(solution)/shard_map/ppermute | solution.py:426
  5.1 1.1 %collective-permute-start.1 = (f32[3,4,768]{2,1,0:T(4,128)S(1)}, f32[3,4,768]{2,1,0:T(4,128)S(1)}, u32[]{:S(2)}, u32[]{:S(2)}) collective-permute-start(f32[3,4,768]{2,1,0:T(4,128)S(1)} %get-tuple-element.38.own_ref), channel_id=1, source_target_pairs={{0,5},{1,4},{2,7},{3,6},{4,1},{5,0},{6,3},{7,2},{8,13},{9,12},{10,... | collective-permute-start | bytes 110600 | tf_op jit(solution)/shard_map/ppermute | solution.py:426
  6.2 0.0 collective-permute-start
  6.2 1.0 %near.6 = (f32[16,768]{1,0:T(8,128)S(1)}, f32[3,4,128]{2,1,0:T(4,128)S(1)}) custom-call(f32[1,3,4,768]{3,2,1,0:T(4,128)S(1)} %bitcast.21, bf16[32,768]{1,0:T(8,128)(2,1)S(1)} %get-tuple-element.39.refs_1_.target_ref, f32[3,4,128]{2,1,0:T(4,128)S(1)} %get-tuple-element.40.refs_2_.column_ref), custom_call_target="tpu_custom_call" | custom-call | flops 294912000 | bytes 36864 | tf_op jit(solution)/shard_map/near/pallas_call | solution.py:270
  7.2 1.7 %collective-permute-done.1 = f32[3,4,768]{2,1,0:T(4,128)S(1)} collective-permute-done((f32[3,4,768]{2,1,0:T(4,128)S(1)}, f32[3,4,768]{2,1,0:T(4,128)S(1)}, u32[]{:S(2)}, u32[]{:S(2)}) %collective-permute-start.1) | collective-permute-done | bytes 36896 | tf_op jit(solution)/shard_map/ppermute | solution.py:426
  8.9 0.6 %collective-permute-done = f32[3,4,768]{2,1,0:T(4,128)S(1)} collective-permute-done((f32[3,4,768]{2,1,0:T(4,128)S(1)}, f32[3,4,768]{2,1,0:T(4,128)S(1)}, u32[]{:S(2)}, u32[]{:S(2)}) %collective-permute-start) | collective-permute-done | bytes 36896 | tf_op jit(solution)/shard_map/ppermute | solution.py:426
  9.6 0.1 collective-permute-start.4
  9.7 0.5 %collective-permute-start.3 = (f32[4,3,4,768]{3,2,0,1:T(4,128)S(1)}, f32[4,3,4,768]{3,2,0,1:T(4,128)S(1)}, u32[]{:S(2)}, u32[]{:S(2)}) collective-permute-start(f32[4,3,4,768]{3,2,0,1:T(4,128)S(1)} %pad_maximum_fusion), channel_id=1, source_target_pairs={{0,1},{1,0},{2,3},{3,2},{4,5},{5,4},{6,7},{7,6},{8,9},{9,8},{10,11... | collective-permute-start | bytes 442376 | tf_op jit(solution)/shard_map/ppermute | solution.py:426
  10.3 2.2 %near.7 = (f32[16,768]{1,0:T(8,128)S(1)}, f32[3,4,128]{2,1,0:T(4,128)S(1)}) custom-call(f32[3,3,4,768]{3,2,1,0:T(4,128)S(1)} %copy.10.refs_0_, bf16[32,768]{1,0:T(8,128)(2,1)S(1)} %get-tuple-element.39.refs_1_.target_ref, f32[3,4,128]{2,1,0:T(4,128)S(1)} %get-tuple-element.40.refs_2_.column_ref, f32[16,768]{1,0:T(8,128)S(1)} %get-tuple-element.46.refs_3_, ...), custom_call_target="tpu_custom_call" | custom-call | flops 884736000 | bytes 110592 | tf_op jit(solution)/shard_map/near/pallas_call | solution.py:270
  12.6 2.9 %near.8 = (f32[16,768]{1,0:T(8,128)S(1)}, f32[3,4,128]{2,1,0:T(4,128)S(1)}) custom-call(f32[4,3,4,768]{3,2,1,0:T(4,128)S(1)} %copy.11.refs_0_, bf16[32,768]{1,0:T(8,128)(2,1)S(1)} %get-tuple-element.39.refs_1_.target_ref, f32[3,4,128]{2,1,0:T(4,128)S(1)} %get-tuple-element.40.refs_2_.column_ref, f32[16,768]{1,0:T(8,128)S(1)} %get-tuple-element.51.refs_3_, ...), custom_call_target="tpu_custom_call" | custom-call | flops 1179648000 | bytes 147456 | tf_op jit(solution)/shard_map/near/pallas_call | solution.py:270
  15.5 0.1 collective-permute-start.5
  15.6 2.9 %collective-permute-start.8 = (f32[8,2,4,768]{3,2,0,1:T(4,128)S(1)}, f32[8,2,4,768]{3,2,0,1:T(4,128)S(1)}, u32[]{:S(2)}, u32[]{:S(2)}) collective-permute-start(f32[8,2,4,768]{3,2,0,1:T(4,128)S(1)} %slice.26), channel_id=1, source_target_pairs={{0,1},{1,0},{2,3},{3,2},{4,5},{5,4},{6,7},{7,6},{8,17},{9,16},{10,... | collective-permute-start | bytes 589832 | tf_op jit(solution)/shard_map/ppermute | solution.py:466
  18.5 2.9 %near.9 = (f32[16,768]{1,0:T(8,128)S(1)}, f32[3,4,128]{2,1,0:T(4,128)S(1)}) custom-call(f32[4,3,4,768]{3,2,1,0:T(4,128)S(1)} %copy.12.refs_0_, bf16[32,768]{1,0:T(8,128)(2,1)S(1)} %get-tuple-element.39.refs_1_.target_ref, f32[3,4,128]{2,1,0:T(4,128)S(1)} %get-tuple-element.40.refs_2_.column_ref, f32[16,768]{1,0:T(8,128)S(1)} %get-tuple-element.56.refs_3_, ...), custom_call_target="tpu_custom_call" | custom-call | flops 1179648000 | bytes 147456 | tf_op jit(solution)/shard_map/near/pallas_call | solution.py:270
  21.5 0.0 copy-start
  21.5 0.1 reduce-precision_convert_fusion.1
  21.6 0.1 maximum_bitcast_fusion.held_ref
  21.7 0.1 collective-permute-start.6
  21.8 3.0 %near.10 = (f32[16,768]{1,0:T(8,128)S(1)}, f32[3,4,128]{2,1,0:T(4,128)S(1)}) custom-call(f32[4,3,4,768]{3,2,1,0:T(4,128)S(1)} %copy.13.refs_0_, bf16[32,768]{1,0:T(8,128)(2,1)S(1)} %get-tuple-element.39.refs_1_.target_ref, f32[3,4,128]{2,1,0:T(4,128)S(1)} %get-tuple-element.40.refs_2_.column_ref, f32[16,768]{1,0:T(8,128)S(1)} %get-tuple-element.61.refs_3_, ...), custom_call_target="tpu_custom_call" | custom-call | flops 1179648000 | bytes 147456 | tf_op jit(solution)/shard_map/near/pallas_call | solution.py:270
  24.9 0.4 %shell_rows.1.product_in = f32[3,4,128]{2,1,0:T(4,128)S(1)} custom-call(bf16[1,17,4,768]{3,2,1,0:T(4,128)(2,1)S(1)} %maximum_bitcast_fusion.held_ref, bf16[3,4,98304]{2,1,0:T(4,128)(2,1)S(1)} %copy-done), custom_call_target="tpu_custom_call" | custom-call | tf_op jit(solution)/shard_map/shell_rows/pallas_call | solution.py:321
  25.3 1.1 %collective-permute-done.6 = bf16[1,17,4,768]{3,2,1,0:T(4,128)(2,1)S(1)} collective-permute-done((bf16[1,17,4,768]{3,2,1,0:T(4,128)(2,1)S(1)}, bf16[1,17,4,768]{3,2,1,0:T(4,128)(2,1)S(1)}, u32[]{:S(2)}, u32[]{:S(2)}) %collective-permute-start.6) | collective-permute-done | bytes 104480 | tf_op jit(solution)/shard_map/ppermute | solution.py:483
  26.3 5.4 %near.11 = (f32[16,768]{1,0:T(8,128)S(1)}, f32[3,4,128]{2,1,0:T(4,128)S(1)}) custom-call(f32[8,2,4,768]{3,2,1,0:T(4,128)S(1)} %copy.14.refs_0_, bf16[32,768]{1,0:T(8,128)(2,1)S(1)} %get-tuple-element.39.refs_1_.target_ref, f32[3,4,128]{2,1,0:T(4,128)S(1)} %get-tuple-element.40.refs_2_.column_ref, f32[16,768]{1,0:T(8,128)S(1)} %get-tuple-element.70.refs_3_, ...), custom_call_target="tpu_custom_call" | custom-call | flops 2359296000 | bytes 196608 | tf_op jit(solution)/shard_map/near/pallas_call | solution.py:270
  31.8 0.1 broadcast_select_fusion.held_ref
  31.8 1.3 %finish.1 = (f32[3,768]{1,0:T(4,128)}, f32[3,4]{1,0:T(4,128)}) custom-call(f32[3,4,768]{2,1,0:T(4,128)S(1)} %get-tuple-element.38.own_ref, bf16[32,768]{1,0:T(8,128)(2,1)S(1)} %get-tuple-element.39.refs_1_.target_ref, f32[3,4,128]{2,1,0:T(4,128)S(1)} %get-tuple-element.40.refs_2_.column_ref, bf16[1,17,4,768]{3,2,1,0:T(4,128)(2,1)S(1)} %broadcast_select_fusion.held_ref, ...), custom_call_target="tpu_custom_call" | custom-call | tf_op jit(solution)/shard_map/finish/pallas_call | solution.py:411
  (29 shorter events, 0.4 us)
Async XLA Ops:
  2.9 4.3 %collective-permute-start.2 = (f32[3,4,768]{2,1,0:T(4,128)S(1)}, f32[3,4,768]{2,1,0:T(4,128)S(1)}, u32[]{:S(2)}, u32[]{:S(2)}) collective-permute-start(f32[3,4,768]{2,1,0:T(4,128)S(1)} %get-tuple-element.38.own_ref), channel_id=1, source_target_pairs={{0,6},{1,7},{2,4},{3,5},{4,2},{5,3},{6,0},{7,1},{8,14},{9,15},{10,... | collective-permute-start | bytes 110600 | tf_op jit(solution)/shard_map/ppermute | solution.py:426
  5.1 3.8 %collective-permute-start.1 = (f32[3,4,768]{2,1,0:T(4,128)S(1)}, f32[3,4,768]{2,1,0:T(4,128)S(1)}, u32[]{:S(2)}, u32[]{:S(2)}) collective-permute-start(f32[3,4,768]{2,1,0:T(4,128)S(1)} %get-tuple-element.38.own_ref), channel_id=1, source_target_pairs={{0,5},{1,4},{2,7},{3,6},{4,1},{5,0},{6,3},{7,2},{8,13},{9,12},{10,... | collective-permute-start | bytes 110600 | tf_op jit(solution)/shard_map/ppermute | solution.py:426
  6.2 3.4 %collective-permute-start = (f32[3,4,768]{2,1,0:T(4,128)S(1)}, f32[3,4,768]{2,1,0:T(4,128)S(1)}, u32[]{:S(2)}, u32[]{:S(2)}) collective-permute-start(f32[3,4,768]{2,1,0:T(4,128)S(1)} %get-tuple-element.38.own_ref), channel_id=1, source_target_pairs={{0,3},{1,2},{2,1},{3,0},{4,7},{5,6},{6,5},{7,4},{8,11},{9,10},{10,... | collective-permute-start | bytes 110600 | tf_op jit(solution)/shard_map/ppermute | solution.py:426
  9.6 5.8 %collective-permute-start.4 = (f32[4,3,4,768]{3,2,0,1:T(4,128)S(1)}, f32[4,3,4,768]{3,2,0,1:T(4,128)S(1)}, u32[]{:S(2)}, u32[]{:S(2)}) collective-permute-start(f32[4,3,4,768]{3,2,0,1:T(4,128)S(1)} %pad_maximum_fusion), channel_id=1, source_target_pairs={{0,9},{1,8},{2,11},{3,10},{4,13},{5,12},{6,15},{7,14},{8,1},{9,0},... | collective-permute-start | bytes 442376 | tf_op jit(solution)/shard_map/ppermute | solution.py:426
  9.7 2.8 %collective-permute-start.3 = (f32[4,3,4,768]{3,2,0,1:T(4,128)S(1)}, f32[4,3,4,768]{3,2,0,1:T(4,128)S(1)}, u32[]{:S(2)}, u32[]{:S(2)}) collective-permute-start(f32[4,3,4,768]{3,2,0,1:T(4,128)S(1)} %pad_maximum_fusion), channel_id=1, source_target_pairs={{0,1},{1,0},{2,3},{3,2},{4,5},{5,4},{6,7},{7,6},{8,9},{9,8},{10,11... | collective-permute-start | bytes 442376 | tf_op jit(solution)/shard_map/ppermute | solution.py:426
  15.5 5.9 %collective-permute-start.5 = (f32[4,3,4,768]{3,2,0,1:T(4,128)S(1)}, f32[4,3,4,768]{3,2,0,1:T(4,128)S(1)}, u32[]{:S(2)}, u32[]{:S(2)}) collective-permute-start(f32[4,3,4,768]{3,2,0,1:T(4,128)S(1)} %collective-permute-done.4), channel_id=1, source_target_pairs={{0,1},{1,0},{2,3},{3,2},{4,5},{5,4},{6,7},{7,6},{8,9},{9,8},{10,11... | collective-permute-start | bytes 442376 | tf_op jit(solution)/shard_map/ppermute | solution.py:426
  15.6 9.6 %collective-permute-start.8 = (f32[8,2,4,768]{3,2,0,1:T(4,128)S(1)}, f32[8,2,4,768]{3,2,0,1:T(4,128)S(1)}, u32[]{:S(2)}, u32[]{:S(2)}) collective-permute-start(f32[8,2,4,768]{3,2,0,1:T(4,128)S(1)} %slice.26), channel_id=1, source_target_pairs={{0,1},{1,0},{2,3},{3,2},{4,5},{5,4},{6,7},{7,6},{8,17},{9,16},{10,... | collective-permute-start | bytes 589832 | tf_op jit(solution)/shard_map/ppermute | solution.py:466
  21.5 3.3 %copy-start = (bf16[3,4,98304]{2,1,0:T(4,128)(2,1)S(1)}, bf16[3,4,98304]{2,1,0:T(4,128)(2,1)}, u32[]{:S(2)}) copy-start(bf16[3,4,98304]{2,1,0:T(4,128)(2,1)} %block_ref.3) | copy-start | bytes 7077892
  21.7 4.6 %collective-permute-start.6 = (bf16[1,17,4,768]{3,2,1,0:T(4,128)(2,1)S(1)}, bf16[1,17,4,768]{3,2,1,0:T(4,128)(2,1)S(1)}, u32[]{:S(2)}, u32[]{:S(2)}) collective-permute-start(bf16[1,17,4,768]{3,2,1,0:T(4,128)(2,1)S(1)} %maximum_bitcast_fusion.held_ref), channel_id=1, source_target_pairs={{0,1},{1,0},{2,3},{3,2},{4,5},{5,4},{6,7},{7,6},{8,17},{9,16},{10,... | collective-permute-start | bytes 313352 | tf_op jit(solution)/shard_map/ppermute | solution.py:483
  26.3 5.4 %collective-permute-start.7 = (bf16[1,17,4,768]{3,2,1,0:T(4,128)(2,1)S(1)}, bf16[1,17,4,768]{3,2,1,0:T(4,128)(2,1)S(1)}, u32[]{:S(2)}, u32[]{:S(2)}) collective-permute-start(bf16[1,17,4,768]{3,2,1,0:T(4,128)(2,1)S(1)} %collective-permute-done.6), channel_id=1, source_target_pairs={{0,8},{1,9},{2,10},{3,11},{4,12},{5,13},{6,14},{7,15},{8,0},{9,1},... | collective-permute-start | bytes 313352 | tf_op jit(solution)/shard_map/ppermute | solution.py:426

commit v5 on v4

--- a/solution.py
+++ b/solution.py
@@ -280,11 +280,6 @@
     )(records, target_rows, columns, *(totals or ()))
 
 
-def super_box(position, leaf):
-    turned = (leaf + 1) // 2 % 2
-    return jnp.bitwise_xor(jnp.bitwise_xor(position, turned * (position // 2 % 2)), leaf)
-
-
 def block_product(order, leaves, first, held_ref, block_ref):
     leaf, octant = lax.axis_index("leaf"), lax.axis_index("oct")
     octants = len(order)
@@ -295,7 +290,7 @@
     def body(at, sums):
         position = at + first
         seat = jnp.bitwise_xor(octant, position // 2 % 2)
-        box = super_box(position, leaf)
+        box = jnp.bitwise_xor(position, leaf)
         for j in range(octants):
             dens = held_ref[at // 2, (at % 2) * octants + j].astype(F32)
             owner = box * octants + jnp.bitwise_xor(seat, order[j])
@@ -357,7 +352,7 @@
             parts.append(jnp.zeros((1, boxes - used), F32))
         moments.append(jnp.concatenate(parts, axis=1))
     box = lax.broadcasted_iota(jnp.int32, (1, boxes), 1)
-    away = super_box(box // 8 + 2, leaf) - leaf
+    away = jnp.bitwise_xor(box // 8 + 2, leaf) - leaf
     far = (jnp.abs(away) >= 2) & (box < used)
     away = jnp.where(far, away, 0)
     child = box % 8
@@ -447,9 +442,10 @@
     order = [0]
     for bit in [1 << b for b in range(1, octants.bit_length() - 1)]:
         order = order + [j ^ bit ^ 1 for j in order]
-    arrived = [exchange(record, j) for j in order[1:]]
+    arrived = [exchange(record, j) for j in order[:0:-1]][::-1]
     totals = near(record[None], own, None, None)
-    *arrived, totals = together(*arrived, totals)
+    *arrived, totals = together(*arrived[::-1], totals)
+    arrived = arrived[::-1]
     fresh = jnp.stack(arrived)
     records = jnp.stack([record] + arrived)
     swaps = []
@@ -459,16 +455,17 @@
         swaps += [(leaf * octants + o, there * octants + (o ^ 1)) for o in range(octants)]
     order = order + [j ^ 1 for j in order]
     inner = exchange(records, octants + 1)
+    outer = lax.ppermute(records[:, :2], ("leaf", "oct"), swaps)
     late = exchange(records, 1)
     totals = near(fresh, own, None, totals)
     late, totals = together(late, totals)
     records = jnp.concatenate([records, late], axis=0)
-    outer = lax.ppermute(records[:, :2], ("leaf", "oct"), swaps)
     totals = near(late, own, None, totals)
-    inner, totals = together(inner, totals)
-    late_inner = exchange(inner, 1)
+    outer, inner, totals = together(outer, inner, totals)
+    late_inner, late_outer = exchange(inner, 1), exchange(outer, 1)
     totals = near(inner, own, inner_shift, totals)
-    late_inner, totals = together(late_inner, totals)
+    late_inner, late_outer, totals = together(late_inner, late_outer, totals)
+    outer = jnp.concatenate([outer, late_outer], axis=0)
     inner = jnp.concatenate([late_inner, inner], axis=0)
     dens = jnp.concatenate([records[:, 2], inner[:, 2]], axis=0).astype(BF16)
     moments = jnp.concatenate(
@@ -480,18 +477,16 @@
     parts = jnp.concatenate([high, middle, low], axis=0).astype(BF16)
     parts = jnp.pad(parts, ((0, count - 3), (0, width - parts.shape[1])))
     held = jnp.concatenate([dens, parts[None]], axis=0)[None]
-    across = lax.ppermute(held, ("leaf", "oct"), swaps)
+    bits = [(1 << b) * octants for b in range(1, leaves.bit_length() - 1)]
+    rest = exchange(held, bits[0] + 1)
     totals = near(late_inner, own, inner_shift, totals)
     held, totals = together(held, totals)
     product = shell_rows(tuple(order), leaves, held, shell_block)
-    across, product, totals = together(across, product, totals)
-    relayed = exchange(across, octants)
+    product, totals = together(product, totals)
     totals = near(outer, own, outer_shift, totals)
-    straight = (lax.axis_index("leaf") + 1) // 2 % 2 == 1
-    rest = jnp.where(straight, across, relayed)
-    for bit in [1 << b for b in range(2, leaves.bit_length() - 1)]:
+    for bit in bits[1:]:
         whole = jnp.concatenate([held, rest], axis=0)
-        rest = jnp.concatenate([rest, exchange(whole, bit * octants)], axis=0)
+        rest = jnp.concatenate([rest, exchange(whole, bit)], axis=0)
     return finish(tuple(order), leaves, record, own, rest, shell_block, product, totals)
 
 

time: 33.8 us -> 32.6 us (0.964); the launches traced: 33.2 us -> 32.4 us
  waiting for transfers between devices: 3.45 us -> 2.39 us
  starting transfers between devices: 7.01 us -> 7.46 us
    ppermute x7 -> x8, starting transfers between devices: 4.05 us -> 5.12 us  [exchange(): lax.ppermute(value, ('leaf', 'oct'), [(i, i ^ bits) for i in range(device...]
    ppermute x1 -> x0, waiting for transfers between devices: 1.05 us -> none  [shards(): across = lax.ppermute(held, ('leaf', 'oct'), swaps)]
    ppermute x1, starting transfers between devices: 2.86 us -> 2.33 us  [shards(): outer = lax.ppermute(records[:, :2], ('leaf', 'oct'), swaps)]
    ppermute x7 -> x8, waiting for transfers between devices: 2.39 us -> 2.39 us  [exchange(): lax.ppermute(value, ('leaf', 'oct'), [(i, i ^ bits) for i in range(device...]
  transfers between devices with their start and end apart: 9 -> 9, of which waited for: 3 -> 2; matrix products, arithmetic and copies ran while one was open for 1% -> 1% of each run, Pallas kernels for 54% -> 54%
where the time goes in v5:
time: 32.6 us; the launch traced here: 32.4 us
  Pallas kernels  21.2 us (65%)
  starting transfers between devices  7.46 us (23%)
  waiting for transfers between devices  2.39 us (7%)
  between operations  0.8 us (2%)
  other arithmetic  0.35 us (1%)
    pallas_call x6, Pallas kernels, near(): pl.pallas_call(functools.partial(near_kernel, shift, lax.axis_size('leaf'...  17.2 us
    ppermute x8, starting transfers between devices, exchange(): lax.ppermute(value, ('leaf', 'oct'), [(i, i ^ bits) for i in range(device...  5.12 us
    ppermute x8, waiting for transfers between devices, exchange(): lax.ppermute(value, ('leaf', 'oct'), [(i, i ^ bits) for i in range(device...  2.39 us
    ppermute x1, starting transfers between devices, shards(): outer = lax.ppermute(records[:, :2], ('leaf', 'oct'), swaps)  2.33 us
    pallas_call x1, Pallas kernels, prepare(): pl.pallas_call(prepare_kernel, out_shape=(jax.ShapeDtypeStruct((3, 4, wid...  2.24 us
    pallas_call x1, Pallas kernels, finish(): pl.pallas_call(functools.partial(finish_kernel, order, leaves), out_shape...  1.34 us
  transfers between devices with their start and end apart: 9, of which 2 were waited for; matrix products, arithmetic and copies ran while one was open for 1% of the time, Pallas kernels for 54%

profile of v5, /device:TPU:9, one launch (start us, length us, event | category | flops | bytes accessed | tf_op | source)
XLA Modules:
  0.0 32.4 jit_solution(12197684460992381710)
XLA Ops:
  0.6 2.2 %prepare.1 = (f32[3,4,768]{2,1,0:T(4,128)S(1)}, bf16[32,768]{1,0:T(8,128)(2,1)S(1)}, f32[3,4,128]{2,1,0:T(4,128)S(1)}) custom-call(bf16[12,256,256]{2,1,0:T(8,128)(2,1)} %refs_0_.1, bf16[12,256]{1,0:T(8,128)(2,1)} %refs_1_.1, f32[12,256]{1,0:T(8,128)} %refs_2_.1, s32[12]{0:T(128)} %bitcast.31, f32[3072]{0:T(1024)} %refs_4_.1, f32[3,4]{1,0:T(4,128)} %refs_5_.1), custom_call_target="tpu_custom_call" | custom-call | tf_op jit(solution)/shard_map/prepare/pallas_call | solution.py:105
  2.9 2.2 %collective-permute-start = (f32[3,4,768]{2,1,0:T(4,128)S(1)}, f32[3,4,768]{2,1,0:T(4,128)S(1)}, u32[]{:S(2)}, u32[]{:S(2)}) collective-permute-start(f32[3,4,768]{2,1,0:T(4,128)S(1)} %get-tuple-element.39.own_ref), channel_id=1, source_target_pairs={{0,6},{1,7},{2,4},{3,5},{4,2},{5,3},{6,0},{7,1},{8,14},{9,15},{10,... | collective-permute-start | bytes 110600 | tf_op jit(solution)/shard_map/ppermute | solution.py:421
  5.1 1.1 %collective-permute-start.1 = (f32[3,4,768]{2,1,0:T(4,128)S(1)}, f32[3,4,768]{2,1,0:T(4,128)S(1)}, u32[]{:S(2)}, u32[]{:S(2)}) collective-permute-start(f32[3,4,768]{2,1,0:T(4,128)S(1)} %get-tuple-element.39.own_ref), channel_id=1, source_target_pairs={{0,5},{1,4},{2,7},{3,6},{4,1},{5,0},{6,3},{7,2},{8,13},{9,12},{10,... | collective-permute-start | bytes 110600 | tf_op jit(solution)/shard_map/ppermute | solution.py:421
  6.2 0.0 collective-permute-start.2
  6.2 1.0 %near.6 = (f32[16,768]{1,0:T(8,128)S(1)}, f32[3,4,128]{2,1,0:T(4,128)S(1)}) custom-call(f32[1,3,4,768]{3,2,1,0:T(4,128)S(1)} %bitcast.21, bf16[32,768]{1,0:T(8,128)(2,1)S(1)} %get-tuple-element.40.refs_1_.target_ref, f32[3,4,128]{2,1,0:T(4,128)S(1)} %get-tuple-element.41.refs_2_.column_ref), custom_call_target="tpu_custom_call" | custom-call | flops 294912000 | bytes 36864 | tf_op jit(solution)/shard_map/near/pallas_call | solution.py:270
  7.2 1.7 %collective-permute-done.1 = f32[3,4,768]{2,1,0:T(4,128)S(1)} collective-permute-done((f32[3,4,768]{2,1,0:T(4,128)S(1)}, f32[3,4,768]{2,1,0:T(4,128)S(1)}, u32[]{:S(2)}, u32[]{:S(2)}) %collective-permute-start.1) | collective-permute-done | bytes 36896 | tf_op jit(solution)/shard_map/ppermute | solution.py:421
  8.9 0.6 %collective-permute-done.2 = f32[3,4,768]{2,1,0:T(4,128)S(1)} collective-permute-done((f32[3,4,768]{2,1,0:T(4,128)S(1)}, f32[3,4,768]{2,1,0:T(4,128)S(1)}, u32[]{:S(2)}, u32[]{:S(2)}) %collective-permute-start.2) | collective-permute-done | bytes 36896 | tf_op jit(solution)/shard_map/ppermute | solution.py:421
  9.6 0.1 collective-permute-start.3
  9.7 0.6 %collective-permute-start.5 = (f32[4,3,4,768]{3,2,0,1:T(4,128)S(1)}, f32[4,3,4,768]{3,2,0,1:T(4,128)S(1)}, u32[]{:S(2)}, u32[]{:S(2)}) collective-permute-start(f32[4,3,4,768]{3,2,0,1:T(4,128)S(1)} %pad_maximum_fusion.1), channel_id=1, source_target_pairs={{0,9},{1,8},{2,11},{3,10},{4,13},{5,12},{6,15},{7,14},{8,1},{9,0},... | collective-permute-start | bytes 442376 | tf_op jit(solution)/shard_map/ppermute | solution.py:421
  10.3 2.3 %collective-permute-start.4 = (f32[4,2,4,768]{3,2,0,1:T(4,128)S(1)}, f32[4,2,4,768]{3,2,0,1:T(4,128)S(1)}, u32[]{:S(2)}, u32[]{:S(2)}) collective-permute-start(f32[4,2,4,768]{3,2,0,1:T(4,128)S(1)} %slice.23), channel_id=1, source_target_pairs={{0,1},{1,0},{2,3},{3,2},{4,5},{5,4},{6,7},{7,6},{8,17},{9,16},{10,... | collective-permute-start | bytes 294920 | tf_op jit(solution)/shard_map/ppermute | solution.py:458
  12.7 2.2 %near.7 = (f32[16,768]{1,0:T(8,128)S(1)}, f32[3,4,128]{2,1,0:T(4,128)S(1)}) custom-call(f32[3,3,4,768]{3,2,1,0:T(4,128)S(1)} %copy.10.refs_0_, bf16[32,768]{1,0:T(8,128)(2,1)S(1)} %get-tuple-element.40.refs_1_.target_ref, f32[3,4,128]{2,1,0:T(4,128)S(1)} %get-tuple-element.41.refs_2_.column_ref, f32[16,768]{1,0:T(8,128)S(1)} %get-tuple-element.47.refs_3_, ...), custom_call_target="tpu_custom_call" | custom-call | flops 884736000 | bytes 110592 | tf_op jit(solution)/shard_map/near/pallas_call | solution.py:270
  15.0 0.0 collective-permute-done.3
  15.0 2.9 %near.8 = (f32[16,768]{1,0:T(8,128)S(1)}, f32[3,4,128]{2,1,0:T(4,128)S(1)}) custom-call(f32[4,3,4,768]{3,2,1,0:T(4,128)S(1)} %copy.11.refs_0_, bf16[32,768]{1,0:T(8,128)(2,1)S(1)} %get-tuple-element.40.refs_1_.target_ref, f32[3,4,128]{2,1,0:T(4,128)S(1)} %get-tuple-element.41.refs_2_.column_ref, f32[16,768]{1,0:T(8,128)S(1)} %get-tuple-element.52.refs_3_, ...), custom_call_target="tpu_custom_call" | custom-call | flops 1179648000 | bytes 147456 | tf_op jit(solution)/shard_map/near/pallas_call | solution.py:270
  17.9 0.5 %collective-permute-start.6 = (f32[4,3,4,768]{3,2,0,1:T(4,128)S(1)}, f32[4,3,4,768]{3,2,0,1:T(4,128)S(1)}, u32[]{:S(2)}, u32[]{:S(2)}) collective-permute-start(f32[4,3,4,768]{3,2,0,1:T(4,128)S(1)} %collective-permute-done.5), channel_id=1, source_target_pairs={{0,1},{1,0},{2,3},{3,2},{4,5},{5,4},{6,7},{7,6},{8,9},{9,8},{10,11... | collective-permute-start | bytes 442376 | tf_op jit(solution)/shard_map/ppermute | solution.py:421
  18.4 0.1 collective-permute-start.7
  18.6 2.9 %near.9 = (f32[16,768]{1,0:T(8,128)S(1)}, f32[3,4,128]{2,1,0:T(4,128)S(1)}) custom-call(f32[4,3,4,768]{3,2,1,0:T(4,128)S(1)} %copy.12.refs_0_, bf16[32,768]{1,0:T(8,128)(2,1)S(1)} %get-tuple-element.40.refs_1_.target_ref, f32[3,4,128]{2,1,0:T(4,128)S(1)} %get-tuple-element.41.refs_2_.column_ref, f32[16,768]{1,0:T(8,128)S(1)} %get-tuple-element.58.refs_3_, ...), custom_call_target="tpu_custom_call" | custom-call | flops 1179648000 | bytes 147456 | tf_op jit(solution)/shard_map/near/pallas_call | solution.py:270
  21.6 0.0 copy-start
  21.6 0.1 reduce-precision_convert_fusion.1
  21.7 0.1 maximum_bitcast_fusion.held_ref
  21.8 0.5 %collective-permute-start.8 = (bf16[1,17,4,768]{3,2,1,0:T(4,128)(2,1)S(1)}, bf16[1,17,4,768]{3,2,1,0:T(4,128)(2,1)S(1)}, u32[]{:S(2)}, u32[]{:S(2)}) collective-permute-start(bf16[1,17,4,768]{3,2,1,0:T(4,128)(2,1)S(1)} %maximum_bitcast_fusion.held_ref), channel_id=1, source_target_pairs={{0,17},{1,16},{2,19},{3,18},{4,21},{5,20},{6,23},{7,22},{8,25},{9,... | collective-permute-start | bytes 313352 | tf_op jit(solution)/shard_map/ppermute | solution.py:421
  22.3 2.9 %near.10 = (f32[16,768]{1,0:T(8,128)S(1)}, f32[3,4,128]{2,1,0:T(4,128)S(1)}) custom-call(f32[4,3,4,768]{3,2,1,0:T(4,128)S(1)} %copy.13.refs_0_, bf16[32,768]{1,0:T(8,128)(2,1)S(1)} %get-tuple-element.40.refs_1_.target_ref, f32[3,4,128]{2,1,0:T(4,128)S(1)} %get-tuple-element.41.refs_2_.column_ref, f32[16,768]{1,0:T(8,128)S(1)} %get-tuple-element.63.refs_3_, ...), custom_call_target="tpu_custom_call" | custom-call | flops 1179648000 | bytes 147456 | tf_op jit(solution)/shard_map/near/pallas_call | solution.py:270
  25.1 0.4 %shell_rows.1.product_in = f32[3,4,128]{2,1,0:T(4,128)S(1)} custom-call(bf16[1,17,4,768]{3,2,1,0:T(4,128)(2,1)S(1)} %maximum_bitcast_fusion.held_ref, bf16[3,4,98304]{2,1,0:T(4,128)(2,1)S(1)} %copy-done), custom_call_target="tpu_custom_call" | custom-call | tf_op jit(solution)/shard_map/shell_rows/pallas_call | solution.py:316
  25.6 5.4 %near.11 = (f32[16,768]{1,0:T(8,128)S(1)}, f32[3,4,128]{2,1,0:T(4,128)S(1)}) custom-call(f32[8,2,4,768]{3,2,1,0:T(4,128)S(1)} %copy.14.refs_0_, bf16[32,768]{1,0:T(8,128)(2,1)S(1)} %get-tuple-element.40.refs_1_.target_ref, f32[3,4,128]{2,1,0:T(4,128)S(1)} %get-tuple-element.41.refs_2_.column_ref, f32[16,768]{1,0:T(8,128)S(1)} %get-tuple-element.72.refs_3_, ...), custom_call_target="tpu_custom_call" | custom-call | flops 2359296000 | bytes 196608 | tf_op jit(solution)/shard_map/near/pallas_call | solution.py:270
  31.1 1.3 %finish.1 = (f32[3,768]{1,0:T(4,128)}, f32[3,4]{1,0:T(4,128)}) custom-call(f32[3,4,768]{2,1,0:T(4,128)S(1)} %get-tuple-element.39.own_ref, bf16[32,768]{1,0:T(8,128)(2,1)S(1)} %get-tuple-element.40.refs_1_.target_ref, f32[3,4,128]{2,1,0:T(4,128)S(1)} %get-tuple-element.41.refs_2_.column_ref, bf16[1,17,4,768]{3,2,1,0:T(4,128)(2,1)S(1)} %collective-permute-done.8.held_ref, ...), custom_call_target="tpu_custom_call" | custom-call | tf_op jit(solution)/shard_map/finish/pallas_call | solution.py:406
  (28 shorter events, 0.4 us)
Async XLA Ops:
  2.9 4.3 %collective-permute-start = (f32[3,4,768]{2,1,0:T(4,128)S(1)}, f32[3,4,768]{2,1,0:T(4,128)S(1)}, u32[]{:S(2)}, u32[]{:S(2)}) collective-permute-start(f32[3,4,768]{2,1,0:T(4,128)S(1)} %get-tuple-element.39.own_ref), channel_id=1, source_target_pairs={{0,6},{1,7},{2,4},{3,5},{4,2},{5,3},{6,0},{7,1},{8,14},{9,15},{10,... | collective-permute-start | bytes 110600 | tf_op jit(solution)/shard_map/ppermute | solution.py:421
  5.1 3.8 %collective-permute-start.1 = (f32[3,4,768]{2,1,0:T(4,128)S(1)}, f32[3,4,768]{2,1,0:T(4,128)S(1)}, u32[]{:S(2)}, u32[]{:S(2)}) collective-permute-start(f32[3,4,768]{2,1,0:T(4,128)S(1)} %get-tuple-element.39.own_ref), channel_id=1, source_target_pairs={{0,5},{1,4},{2,7},{3,6},{4,1},{5,0},{6,3},{7,2},{8,13},{9,12},{10,... | collective-permute-start | bytes 110600 | tf_op jit(solution)/shard_map/ppermute | solution.py:421
  6.2 3.4 %collective-permute-start.2 = (f32[3,4,768]{2,1,0:T(4,128)S(1)}, f32[3,4,768]{2,1,0:T(4,128)S(1)}, u32[]{:S(2)}, u32[]{:S(2)}) collective-permute-start(f32[3,4,768]{2,1,0:T(4,128)S(1)} %get-tuple-element.39.own_ref), channel_id=1, source_target_pairs={{0,3},{1,2},{2,1},{3,0},{4,7},{5,6},{6,5},{7,4},{8,11},{9,10},{10,... | collective-permute-start | bytes 110600 | tf_op jit(solution)/shard_map/ppermute | solution.py:421
  9.6 5.4 %collective-permute-start.3 = (f32[4,3,4,768]{3,2,0,1:T(4,128)S(1)}, f32[4,3,4,768]{3,2,0,1:T(4,128)S(1)}, u32[]{:S(2)}, u32[]{:S(2)}) collective-permute-start(f32[4,3,4,768]{3,2,0,1:T(4,128)S(1)} %pad_maximum_fusion.1), channel_id=1, source_target_pairs={{0,1},{1,0},{2,3},{3,2},{4,5},{5,4},{6,7},{7,6},{8,9},{9,8},{10,11... | collective-permute-start | bytes 442376 | tf_op jit(solution)/shard_map/ppermute | solution.py:421
  9.7 8.1 %collective-permute-start.5 = (f32[4,3,4,768]{3,2,0,1:T(4,128)S(1)}, f32[4,3,4,768]{3,2,0,1:T(4,128)S(1)}, u32[]{:S(2)}, u32[]{:S(2)}) collective-permute-start(f32[4,3,4,768]{3,2,0,1:T(4,128)S(1)} %pad_maximum_fusion.1), channel_id=1, source_target_pairs={{0,9},{1,8},{2,11},{3,10},{4,13},{5,12},{6,15},{7,14},{8,1},{9,0},... | collective-permute-start | bytes 442376 | tf_op jit(solution)/shard_map/ppermute | solution.py:421
  10.3 7.5 %collective-permute-start.4 = (f32[4,2,4,768]{3,2,0,1:T(4,128)S(1)}, f32[4,2,4,768]{3,2,0,1:T(4,128)S(1)}, u32[]{:S(2)}, u32[]{:S(2)}) collective-permute-start(f32[4,2,4,768]{3,2,0,1:T(4,128)S(1)} %slice.23), channel_id=1, source_target_pairs={{0,1},{1,0},{2,3},{3,2},{4,5},{5,4},{6,7},{7,6},{8,17},{9,16},{10,... | collective-permute-start | bytes 294920 | tf_op jit(solution)/shard_map/ppermute | solution.py:458
  17.9 3.6 %collective-permute-start.6 = (f32[4,3,4,768]{3,2,0,1:T(4,128)S(1)}, f32[4,3,4,768]{3,2,0,1:T(4,128)S(1)}, u32[]{:S(2)}, u32[]{:S(2)}) collective-permute-start(f32[4,3,4,768]{3,2,0,1:T(4,128)S(1)} %collective-permute-done.5), channel_id=1, source_target_pairs={{0,1},{1,0},{2,3},{3,2},{4,5},{5,4},{6,7},{7,6},{8,9},{9,8},{10,11... | collective-permute-start | bytes 442376 | tf_op jit(solution)/shard_map/ppermute | solution.py:421
  18.4 3.0 %collective-permute-start.7 = (f32[4,2,4,768]{3,2,0,1:T(4,128)S(1)}, f32[4,2,4,768]{3,2,0,1:T(4,128)S(1)}, u32[]{:S(2)}, u32[]{:S(2)}) collective-permute-start(f32[4,2,4,768]{3,2,0,1:T(4,128)S(1)} %collective-permute-done.4), channel_id=1, source_target_pairs={{0,1},{1,0},{2,3},{3,2},{4,5},{5,4},{6,7},{7,6},{8,9},{9,8},{10,11... | collective-permute-start | bytes 294920 | tf_op jit(solution)/shard_map/ppermute | solution.py:421
  21.6 3.6 %copy-start = (bf16[3,4,98304]{2,1,0:T(4,128)(2,1)S(1)}, bf16[3,4,98304]{2,1,0:T(4,128)(2,1)}, u32[]{:S(2)}) copy-start(bf16[3,4,98304]{2,1,0:T(4,128)(2,1)} %block_ref.3) | copy-start | bytes 7077892
  21.8 9.3 %collective-permute-start.8 = (bf16[1,17,4,768]{3,2,1,0:T(4,128)(2,1)S(1)}, bf16[1,17,4,768]{3,2,1,0:T(4,128)(2,1)S(1)}, u32[]{:S(2)}, u32[]{:S(2)}) collective-permute-start(bf16[1,17,4,768]{3,2,1,0:T(4,128)(2,1)S(1)} %maximum_bitcast_fusion.held_ref), channel_id=1, source_target_pairs={{0,17},{1,16},{2,19},{3,18},{4,21},{5,20},{6,23},{7,22},{8,25},{9,... | collective-permute-start | bytes 313352 | tf_op jit(solution)/shard_map/ppermute | solution.py:421

commit v6 on v5

--- a/solution.py
+++ b/solution.py
@@ -218,66 +218,70 @@
     return total
 
 
-def near_kernel(shift, leaves, first, *refs):
-    records_ref, target_ref, column_ref = refs[:3]
-    total_in, shell_in = (None, None) if first else refs[3:5]
+def near_kernel(shifts, leaves, first, *refs):
+    records_refs = refs[: len(shifts)]
+    target_ref, column_ref = refs[len(shifts) : len(shifts) + 2]
+    total_in, shell_in = (None, None) if first else refs[-4:-2]
     total_ref, shell_total_ref = refs[-2:]
     columns = [column_ref[c][:, 0:1] for c in range(3)]
-    if shift is not None:
-        leaf = lax.axis_index("leaf")
-        moved = (2 * shift(leaf)).astype(F32)
+    leaf = lax.axis_index("leaf")
     targets = target_ref.shape[1]
     block = min(256, targets)
 
-    def run():
+    def run(chosen):
         groups = []
         shell = [None if first else shell_in[c] for c in range(3)]
-        for j in range(records_ref.shape[0]):
-            record = records_ref.at[j]
-            place = record[0, 0:3, :]
-            if shift is not None:
-                axis = lax.broadcasted_iota(jnp.int32, place.shape, 0)
-                place = place + jnp.where(axis == 0, moved, 0.0)
-            push, source = record[1, 0:3, :], record[1, 3:4, :]
-            groups.append((source_rows(place), source_terms(place, push, source)))
-            for c, value in enumerate(direct(columns, place, push, source)):
-                value = fold(value, 128)
-                shell[c] = value if shell[c] is None else shell[c] + value
+        for at in chosen:
+            for j in range(records_refs[at].shape[0]):
+                record = records_refs[at].at[j]
+                place = record[0, 0:3, :]
+                if shifts[at] is not None:
+                    axis = lax.broadcasted_iota(jnp.int32, place.shape, 0)
+                    moved = (2 * shifts[at](leaf)).astype(F32)
+                    place = place + jnp.where(axis == 0, moved, 0.0)
+                push, source = record[1, 0:3, :], record[1, 3:4, :]
+                groups.append((source_rows(place), source_terms(place, push, source)))
+                for c, value in enumerate(direct(columns, place, push, source)):
+                    value = fold(value, 128)
+                    shell[c] = value if shell[c] is None else shell[c] + value
         for at, value in enumerate(sum_sources(target_ref, groups, block)):
             lanes = slice(at * block, (at + 1) * block)
             total_ref[:, lanes] = value if first else value + total_in[:, lanes]
         for c in range(3):
             shell_total_ref[c] = shell[c]
 
-    if shift is None:
-        run()
+    def absent(shift):
+        return shift is not None and any(not 0 <= i + shift(i) < leaves for i in range(leaves))
+
+    everything = list(range(len(shifts)))
+    always = [at for at in everything if not absent(shifts[at])]
+    if always == everything:
+        run(everything)
         return
-    there = leaf + shift(leaf)
-    inside = (there >= 0) & (there < leaves)
-    pl.when(inside)(run)
-
-    @pl.when(jnp.logical_not(inside))
-    def _():
-        total_ref[...] = total_in[...]
-        shell_total_ref[...] = shell_in[...]
-
-
-def near(records, own, shift, totals):
+    there = [leaf + shifts[at](leaf) for at in everything if at not in always]
+    inside = functools.reduce(jnp.logical_and, [(x >= 0) & (x < leaves) for x in there])
+    pl.when(inside)(lambda: run(everything))
+    pl.when(jnp.logical_not(inside))(lambda: run(always))
+
+
+def near(groups, own, totals):
     target_rows, columns = own
     targets = target_rows.shape[1]
     out = (jax.ShapeDtypeStruct((16, targets), F32), jax.ShapeDtypeStruct(columns.shape, F32))
-    pairs = records.shape[0] * records.shape[3] * targets
+    records, shifts = zip(*groups)
+    size = sum(part.size for part in records)
+    pairs = sum(part.shape[0] * part.shape[3] for part in records) * targets
     return pl.pallas_call(
-        functools.partial(near_kernel, shift, lax.axis_size("leaf"), totals is None),
+        functools.partial(near_kernel, shifts, lax.axis_size("leaf"), totals is None),
         out_shape=out,
-        in_specs=[VMEM] * (3 if totals is None else 5),
+        in_specs=[VMEM] * (len(records) + (2 if totals is None else 4)),
         out_specs=(VMEM, VMEM),
         compiler_params=PARAMS,
         cost_estimate=pl.CostEstimate(
-            flops=500 * pairs, bytes_accessed=records.size * 4, transcendentals=pairs
+            flops=500 * pairs, bytes_accessed=size * 4, transcendentals=pairs
         ),
         name="near",
-    )(records, target_rows, columns, *(totals or ()))
+    )(*records, target_rows, columns, *(totals or ()))
 
 
 def block_product(order, leaves, first, held_ref, block_ref):
@@ -443,7 +447,7 @@
     for bit in [1 << b for b in range(1, octants.bit_length() - 1)]:
         order = order + [j ^ bit ^ 1 for j in order]
     arrived = [exchange(record, j) for j in order[:0:-1]][::-1]
-    totals = near(record[None], own, None, None)
+    totals = near([(record[None], None)], own, None)
     *arrived, totals = together(*arrived[::-1], totals)
     arrived = arrived[::-1]
     fresh = jnp.stack(arrived)
@@ -457,13 +461,12 @@
     inner = exchange(records, octants + 1)
     outer = lax.ppermute(records[:, :2], ("leaf", "oct"), swaps)
     late = exchange(records, 1)
-    totals = near(fresh, own, None, totals)
     late, totals = together(late, totals)
     records = jnp.concatenate([records, late], axis=0)
-    totals = near(late, own, None, totals)
+    totals = near([(fresh, None), (late, None)], own, totals)
     outer, inner, totals = together(outer, inner, totals)
     late_inner, late_outer = exchange(inner, 1), exchange(outer, 1)
-    totals = near(inner, own, inner_shift, totals)
+    totals = near([(inner, inner_shift)], own, totals)
     late_inner, late_outer, totals = together(late_inner, late_outer, totals)
     outer = jnp.concatenate([outer, late_outer], axis=0)
     inner = jnp.concatenate([late_inner, inner], axis=0)
@@ -479,11 +482,9 @@
     held = jnp.concatenate([dens, parts[None]], axis=0)[None]
     bits = [(1 << b) * octants for b in range(1, leaves.bit_length() - 1)]
     rest = exchange(held, bits[0] + 1)
-    totals = near(late_inner, own, inner_shift, totals)
-    held, totals = together(held, totals)
     product = shell_rows(tuple(order), leaves, held, shell_block)
     product, totals = together(product, totals)
-    totals = near(outer, own, outer_shift, totals)
+    totals = near([(late_inner, inner_shift), (outer, outer_shift)], own, totals)
     for bit in bits[1:]:
         whole = jnp.concatenate([held, rest], axis=0)
         rest = jnp.concatenate([rest, exchange(whole, bit)], axis=0)

time: 32.6 us -> 32.5 us (level)
  Pallas kernels: 21.2 us -> 20.8 us
    pallas_call x6 -> x4, Pallas kernels: 17.2 us -> 16.9 us  [near(): pl.pallas_call(functools.partial(near_kernel, shifts, lax.axis_size('leaf...]
  transfers between devices with their start and end apart: 9 -> 9, of which waited for: 2 -> 2; matrix products, arithmetic and copies ran while one was open for 1% -> 1% of each run, Pallas kernels for 54% -> 53%
where the time goes in v6:
time: 32.5 us; the launch traced here: 32.3 us
  Pallas kernels  20.8 us (64%)
  starting transfers between devices  7.74 us (24%)
  waiting for transfers between devices  2.39 us (7%)
  between operations  0.8 us (2%)
  other arithmetic  0.35 us (1%)
    pallas_call x4, Pallas kernels, near(): pl.pallas_call(functools.partial(near_kernel, shifts, lax.axis_size('leaf...  16.9 us
    ppermute x8, starting transfers between devices, exchange(): lax.ppermute(value, ('leaf', 'oct'), [(i, i ^ bits) for i in range(device...  5.34 us
    ppermute x1, starting transfers between devices, shards(): outer = lax.ppermute(records[:, :2], ('leaf', 'oct'), swaps)  2.4 us
    ppermute x8, waiting for transfers between devices, exchange(): lax.ppermute(value, ('leaf', 'oct'), [(i, i ^ bits) for i in range(device...  2.39 us
    pallas_call x1, Pallas kernels, prepare(): pl.pallas_call(prepare_kernel, out_shape=(jax.ShapeDtypeStruct((3, 4, wid...  2.24 us
    pallas_call x1, Pallas kernels, finish(): pl.pallas_call(functools.partial(finish_kernel, order, leaves), out_shape...  1.34 us
  transfers between devices with their start and end apart: 9, of which 2 were waited for; matrix products, arithmetic and copies ran while one was open for 1% of the time, Pallas kernels for 53%

profile of v6, /device:TPU:9, one launch (start us, length us, event | category | flops | bytes accessed | tf_op | source)
XLA Modules:
  0.0 32.3 jit_solution(3637929143846782)
XLA Ops:
  0.6 2.2 %prepare.1 = (f32[3,4,768]{2,1,0:T(4,128)S(1)}, bf16[32,768]{1,0:T(8,128)(2,1)S(1)}, f32[3,4,128]{2,1,0:T(4,128)S(1)}) custom-call(bf16[12,256,256]{2,1,0:T(8,128)(2,1)} %refs_0_.1, bf16[12,256]{1,0:T(8,128)(2,1)} %refs_1_.1, f32[12,256]{1,0:T(8,128)} %refs_2_.1, s32[12]{0:T(128)} %bitcast.31, f32[3072]{0:T(1024)} %refs_4_.1, f32[3,4]{1,0:T(4,128)} %refs_5_.1), custom_call_target="tpu_custom_call" | custom-call | tf_op jit(solution)/shard_map/prepare/pallas_call | solution.py:105
  2.9 2.2 %collective-permute-start = (f32[3,4,768]{2,1,0:T(4,128)S(1)}, f32[3,4,768]{2,1,0:T(4,128)S(1)}, u32[]{:S(2)}, u32[]{:S(2)}) collective-permute-start(f32[3,4,768]{2,1,0:T(4,128)S(1)} %get-tuple-element.32.own_ref), channel_id=1, source_target_pairs={{0,6},{1,7},{2,4},{3,5},{4,2},{5,3},{6,0},{7,1},{8,14},{9,15},{10,... | collective-permute-start | bytes 110600 | tf_op jit(solution)/shard_map/ppermute | solution.py:425
  5.1 1.1 %collective-permute-start.1 = (f32[3,4,768]{2,1,0:T(4,128)S(1)}, f32[3,4,768]{2,1,0:T(4,128)S(1)}, u32[]{:S(2)}, u32[]{:S(2)}) collective-permute-start(f32[3,4,768]{2,1,0:T(4,128)S(1)} %get-tuple-element.32.own_ref), channel_id=1, source_target_pairs={{0,5},{1,4},{2,7},{3,6},{4,1},{5,0},{6,3},{7,2},{8,13},{9,12},{10,... | collective-permute-start | bytes 110600 | tf_op jit(solution)/shard_map/ppermute | solution.py:425
  6.2 0.0 collective-permute-start.2
  6.2 1.0 %near.4 = (f32[16,768]{1,0:T(8,128)S(1)}, f32[3,4,128]{2,1,0:T(4,128)S(1)}) custom-call(f32[1,3,4,768]{3,2,1,0:T(4,128)S(1)} %bitcast.21, bf16[32,768]{1,0:T(8,128)(2,1)S(1)} %get-tuple-element.33.refs_1_.refs_2_.target_ref, f32[3,4,128]{2,1,0:T(4,128)S(1)} %get-tuple-element.34.refs_2_.refs_3_.column_ref), custom_call_target="tpu_custom_call" | custom-call | flops 294912000 | bytes 36864 | tf_op jit(solution)/shard_map/near/pallas_call | solution.py:274
  7.2 0.0 collective-permute-done
  7.2 1.7 %collective-permute-done.1 = f32[3,4,768]{2,1,0:T(4,128)S(1)} collective-permute-done((f32[3,4,768]{2,1,0:T(4,128)S(1)}, f32[3,4,768]{2,1,0:T(4,128)S(1)}, u32[]{:S(2)}, u32[]{:S(2)}) %collective-permute-start.1) | collective-permute-done | bytes 36896 | tf_op jit(solution)/shard_map/ppermute | solution.py:425
  8.9 0.6 %collective-permute-done.2 = f32[3,4,768]{2,1,0:T(4,128)S(1)} collective-permute-done((f32[3,4,768]{2,1,0:T(4,128)S(1)}, f32[3,4,768]{2,1,0:T(4,128)S(1)}, u32[]{:S(2)}, u32[]{:S(2)}) %collective-permute-start.2) | collective-permute-done | bytes 36896 | tf_op jit(solution)/shard_map/ppermute | solution.py:425
  9.6 0.1 collective-permute-start.3
  9.7 0.6 %collective-permute-start.5 = (f32[4,3,4,768]{3,2,0,1:T(4,128)S(1)}, f32[4,3,4,768]{3,2,0,1:T(4,128)S(1)}, u32[]{:S(2)}, u32[]{:S(2)}) collective-permute-start(f32[4,3,4,768]{3,2,0,1:T(4,128)S(1)} %pad_maximum_fusion.1), channel_id=1, source_target_pairs={{0,9},{1,8},{2,11},{3,10},{4,13},{5,12},{6,15},{7,14},{8,1},{9,0},... | collective-permute-start | bytes 442376 | tf_op jit(solution)/shard_map/ppermute | solution.py:425
  10.4 2.4 %collective-permute-start.4 = (f32[4,2,4,768]{3,2,0,1:T(4,128)S(1)}, f32[4,2,4,768]{3,2,0,1:T(4,128)S(1)}, u32[]{:S(2)}, u32[]{:S(2)}) collective-permute-start(f32[4,2,4,768]{3,2,0,1:T(4,128)S(1)} %slice.23), channel_id=1, source_target_pairs={{0,1},{1,0},{2,3},{3,2},{4,5},{5,4},{6,7},{7,6},{8,17},{9,16},{10,... | collective-permute-start | bytes 294920 | tf_op jit(solution)/shard_map/ppermute | solution.py:462
  12.8 0.0 collective-permute-done.3
  12.8 4.8 %near.5 = (f32[16,768]{1,0:T(8,128)S(1)}, f32[3,4,128]{2,1,0:T(4,128)S(1)}) custom-call(f32[3,3,4,768]{3,2,1,0:T(4,128)S(1)} %copy.10.refs_0_, f32[4,3,4,768]{3,2,1,0:T(4,128)S(1)} %copy.11.refs_1_, bf16[32,768]{1,0:T(8,128)(2,1)S(1)} %get-tuple-element.33.refs_1_.refs_2_.target_ref, f32[3,4,128]{2,1,0:T(4,128)S(1)} %get-tuple-element.34.refs_2_.refs_3_.column_ref, ...), custom_call_target="tpu_custom_call" | custom-call | flops 2064384000 | bytes 258048 | tf_op jit(solution)/shard_map/near/pallas_call | solution.py:274
  17.7 0.0 collective-permute-done.4
  17.7 0.5 %collective-permute-start.6 = (f32[4,3,4,768]{3,2,0,1:T(4,128)S(1)}, f32[4,3,4,768]{3,2,0,1:T(4,128)S(1)}, u32[]{:S(2)}, u32[]{:S(2)}) collective-permute-start(f32[4,3,4,768]{3,2,0,1:T(4,128)S(1)} %collective-permute-done.5), channel_id=1, source_target_pairs={{0,1},{1,0},{2,3},{3,2},{4,5},{5,4},{6,7},{7,6},{8,9},{9,8},{10,11... | collective-permute-start | bytes 442376 | tf_op jit(solution)/shard_map/ppermute | solution.py:425
  18.2 0.1 collective-permute-start.7
  18.3 0.0 copy-start
  18.4 2.9 %near.6 = (f32[16,768]{1,0:T(8,128)S(1)}, f32[3,4,128]{2,1,0:T(4,128)S(1)}) custom-call(f32[4,3,4,768]{3,2,1,0:T(4,128)S(1)} %copy.12.refs_0_, bf16[32,768]{1,0:T(8,128)(2,1)S(1)} %get-tuple-element.33.refs_1_.refs_2_.target_ref, f32[3,4,128]{2,1,0:T(4,128)S(1)} %get-tuple-element.34.refs_2_.refs_3_.column_ref, f32[16,768]{1,0:T(8,128)S(1)} %get-tuple-element.49.refs_3_, ...), custom_call_target="tpu_custom_call" | custom-call | flops 1179648000 | bytes 147456 | tf_op jit(solution)/shard_map/near/pallas_call | solution.py:274
  21.4 0.1 reduce-precision_convert_fusion.1
  21.5 0.1 maximum_bitcast_fusion.held_ref
  21.6 0.7 %collective-permute-start.8 = (bf16[1,17,4,768]{3,2,1,0:T(4,128)(2,1)S(1)}, bf16[1,17,4,768]{3,2,1,0:T(4,128)(2,1)S(1)}, u32[]{:S(2)}, u32[]{:S(2)}) collective-permute-start(bf16[1,17,4,768]{3,2,1,0:T(4,128)(2,1)S(1)} %maximum_bitcast_fusion.held_ref), channel_id=1, source_target_pairs={{0,17},{1,16},{2,19},{3,18},{4,21},{5,20},{6,23},{7,22},{8,25},{9,... | collective-permute-start | bytes 313352 | tf_op jit(solution)/shard_map/ppermute | solution.py:425
  22.3 0.4 %shell_rows.1.product_in = f32[3,4,128]{2,1,0:T(4,128)S(1)} custom-call(bf16[1,17,4,768]{3,2,1,0:T(4,128)(2,1)S(1)} %maximum_bitcast_fusion.held_ref, bf16[3,4,98304]{2,1,0:T(4,128)(2,1)S(1)} %copy-done), custom_call_target="tpu_custom_call" | custom-call | tf_op jit(solution)/shard_map/shell_rows/pallas_call | solution.py:320
  22.7 8.2 %near.7 = (f32[16,768]{1,0:T(8,128)S(1)}, f32[3,4,128]{2,1,0:T(4,128)S(1)}) custom-call(f32[4,3,4,768]{3,2,1,0:T(4,128)S(1)} %copy.13.refs_0_, f32[8,2,4,768]{3,2,1,0:T(4,128)S(1)} %copy.14.refs_1_, bf16[32,768]{1,0:T(8,128)(2,1)S(1)} %get-tuple-element.33.refs_1_.refs_2_.target_ref, f32[3,4,128]{2,1,0:T(4,128)S(1)} %get-tuple-element.34.refs_2_.refs_3_.column_ref, ...), custom_call_target="tpu_custom_call" | custom-call | flops 3538944000 | bytes 344064 | tf_op jit(solution)/shard_map/near/pallas_call | solution.py:274
  31.0 1.3 %finish.1 = (f32[3,768]{1,0:T(4,128)}, f32[3,4]{1,0:T(4,128)}) custom-call(f32[3,4,768]{2,1,0:T(4,128)S(1)} %get-tuple-element.32.own_ref, bf16[32,768]{1,0:T(8,128)(2,1)S(1)} %get-tuple-element.33.refs_1_.refs_2_.target_ref, f32[3,4,128]{2,1,0:T(4,128)S(1)} %get-tuple-element.34.refs_2_.refs_3_.column_ref, ...), custom_call_target="tpu_custom_call" | custom-call | tf_op jit(solution)/shard_map/finish/pallas_call | solution.py:410
  (26 shorter events, 0.4 us)
Async XLA Ops:
  2.9 4.3 %collective-permute-start = (f32[3,4,768]{2,1,0:T(4,128)S(1)}, f32[3,4,768]{2,1,0:T(4,128)S(1)}, u32[]{:S(2)}, u32[]{:S(2)}) collective-permute-start(f32[3,4,768]{2,1,0:T(4,128)S(1)} %get-tuple-element.32.own_ref), channel_id=1, source_target_pairs={{0,6},{1,7},{2,4},{3,5},{4,2},{5,3},{6,0},{7,1},{8,14},{9,15},{10,... | collective-permute-start | bytes 110600 | tf_op jit(solution)/shard_map/ppermute | solution.py:425
  5.1 3.8 %collective-permute-start.1 = (f32[3,4,768]{2,1,0:T(4,128)S(1)}, f32[3,4,768]{2,1,0:T(4,128)S(1)}, u32[]{:S(2)}, u32[]{:S(2)}) collective-permute-start(f32[3,4,768]{2,1,0:T(4,128)S(1)} %get-tuple-element.32.own_ref), channel_id=1, source_target_pairs={{0,5},{1,4},{2,7},{3,6},{4,1},{5,0},{6,3},{7,2},{8,13},{9,12},{10,... | collective-permute-start | bytes 110600 | tf_op jit(solution)/shard_map/ppermute | solution.py:425
  6.2 3.4 %collective-permute-start.2 = (f32[3,4,768]{2,1,0:T(4,128)S(1)}, f32[3,4,768]{2,1,0:T(4,128)S(1)}, u32[]{:S(2)}, u32[]{:S(2)}) collective-permute-start(f32[3,4,768]{2,1,0:T(4,128)S(1)} %get-tuple-element.32.own_ref), channel_id=1, source_target_pairs={{0,3},{1,2},{2,1},{3,0},{4,7},{5,6},{6,5},{7,4},{8,11},{9,10},{10,... | collective-permute-start | bytes 110600 | tf_op jit(solution)/shard_map/ppermute | solution.py:425
  9.6 3.1 %collective-permute-start.3 = (f32[4,3,4,768]{3,2,0,1:T(4,128)S(1)}, f32[4,3,4,768]{3,2,0,1:T(4,128)S(1)}, u32[]{:S(2)}, u32[]{:S(2)}) collective-permute-start(f32[4,3,4,768]{3,2,0,1:T(4,128)S(1)} %pad_maximum_fusion.1), channel_id=1, source_target_pairs={{0,1},{1,0},{2,3},{3,2},{4,5},{5,4},{6,7},{7,6},{8,9},{9,8},{10,11... | collective-permute-start | bytes 442376 | tf_op jit(solution)/shard_map/ppermute | solution.py:425
  9.7 7.9 %collective-permute-start.5 = (f32[4,3,4,768]{3,2,0,1:T(4,128)S(1)}, f32[4,3,4,768]{3,2,0,1:T(4,128)S(1)}, u32[]{:S(2)}, u32[]{:S(2)}) collective-permute-start(f32[4,3,4,768]{3,2,0,1:T(4,128)S(1)} %pad_maximum_fusion.1), channel_id=1, source_target_pairs={{0,9},{1,8},{2,11},{3,10},{4,13},{5,12},{6,15},{7,14},{8,1},{9,0},... | collective-permute-start | bytes 442376 | tf_op jit(solution)/shard_map/ppermute | solution.py:425
  10.4 7.3 %collective-permute-start.4 = (f32[4,2,4,768]{3,2,0,1:T(4,128)S(1)}, f32[4,2,4,768]{3,2,0,1:T(4,128)S(1)}, u32[]{:S(2)}, u32[]{:S(2)}) collective-permute-start(f32[4,2,4,768]{3,2,0,1:T(4,128)S(1)} %slice.23), channel_id=1, source_target_pairs={{0,1},{1,0},{2,3},{3,2},{4,5},{5,4},{6,7},{7,6},{8,17},{9,16},{10,... | collective-permute-start | bytes 294920 | tf_op jit(solution)/shard_map/ppermute | solution.py:462
  17.7 3.6 %collective-permute-start.6 = (f32[4,3,4,768]{3,2,0,1:T(4,128)S(1)}, f32[4,3,4,768]{3,2,0,1:T(4,128)S(1)}, u32[]{:S(2)}, u32[]{:S(2)}) collective-permute-start(f32[4,3,4,768]{3,2,0,1:T(4,128)S(1)} %collective-permute-done.5), channel_id=1, source_target_pairs={{0,1},{1,0},{2,3},{3,2},{4,5},{5,4},{6,7},{7,6},{8,9},{9,8},{10,11... | collective-permute-start | bytes 442376 | tf_op jit(solution)/shard_map/ppermute | solution.py:425
  18.2 3.0 %collective-permute-start.7 = (f32[4,2,4,768]{3,2,0,1:T(4,128)S(1)}, f32[4,2,4,768]{3,2,0,1:T(4,128)S(1)}, u32[]{:S(2)}, u32[]{:S(2)}) collective-permute-start(f32[4,2,4,768]{3,2,0,1:T(4,128)S(1)} %collective-permute-done.4), channel_id=1, source_target_pairs={{0,1},{1,0},{2,3},{3,2},{4,5},{5,4},{6,7},{7,6},{8,9},{9,8},{10,11... | collective-permute-start | bytes 294920 | tf_op jit(solution)/shard_map/ppermute | solution.py:425
  18.3 3.9 %copy-start = (bf16[3,4,98304]{2,1,0:T(4,128)(2,1)S(1)}, bf16[3,4,98304]{2,1,0:T(4,128)(2,1)}, u32[]{:S(2)}) copy-start(bf16[3,4,98304]{2,1,0:T(4,128)(2,1)} %block_ref.3) | copy-start | bytes 7077892
  21.6 9.4 %collective-permute-start.8 = (bf16[1,17,4,768]{3,2,1,0:T(4,128)(2,1)S(1)}, bf16[1,17,4,768]{3,2,1,0:T(4,128)(2,1)S(1)}, u32[]{:S(2)}, u32[]{:S(2)}) collective-permute-start(bf16[1,17,4,768]{3,2,1,0:T(4,128)(2,1)S(1)} %maximum_bitcast_fusion.held_ref), channel_id=1, source_target_pairs={{0,17},{1,16},{2,19},{3,18},{4,21},{5,20},{6,23},{7,22},{8,25},{9,... | collective-permute-start | bytes 313352 | tf_op jit(solution)/shard_map/ppermute | solution.py:425

commit v7 on v6

--- a/solution.py
+++ b/solution.py
@@ -446,10 +446,10 @@
     order = [0]
     for bit in [1 << b for b in range(1, octants.bit_length() - 1)]:
         order = order + [j ^ bit ^ 1 for j in order]
-    arrived = [exchange(record, j) for j in order[:0:-1]][::-1]
+    arrived = [exchange(record, order[1 + i]) for i in (1, 2, 0)]
     totals = near([(record[None], None)], own, None)
-    *arrived, totals = together(*arrived[::-1], totals)
-    arrived = arrived[::-1]
+    *arrived, totals = together(*arrived, totals)
+    arrived = [arrived[i] for i in [2, 0, 1]]
     fresh = jnp.stack(arrived)
     records = jnp.stack([record] + arrived)
     swaps = []

time: 32.5 us -> 32.5 us (level)
  waiting for transfers between devices: 2.39 us -> 2.04 us
    ppermute x8, waiting for transfers between devices: 2.39 us -> 2.03 us  [exchange(): lax.ppermute(value, ('leaf', 'oct'), [(i, i ^ bits) for i in range(device...]
  transfers between devices with their start and end apart: 9 -> 9, of which waited for: 2 -> 2; matrix products, arithmetic and copies ran while one was open for 1% -> 1% of each run, Pallas kernels for 53% -> 54%
where the time goes in v7:
time: 32.5 us; the launch traced here: 32.1 us
  Pallas kernels  20.8 us (64%)
  starting transfers between devices  7.87 us (24%)
  waiting for transfers between devices  2.04 us (6%)
  between operations  0.8 us (2%)
  other arithmetic  0.35 us (1%)
    pallas_call x4, Pallas kernels, near(): pl.pallas_call(functools.partial(near_kernel, shifts, lax.axis_size('leaf...  16.9 us
    ppermute x8, starting transfers between devices, exchange(): lax.ppermute(value, ('leaf', 'oct'), [(i, i ^ bits) for i in range(device...  5.24 us
    ppermute x1, starting transfers between devices, shards(): outer = lax.ppermute(records[:, :2], ('leaf', 'oct'), swaps)  2.63 us
    pallas_call x1, Pallas kernels, prepare(): pl.pallas_call(prepare_kernel, out_shape=(jax.ShapeDtypeStruct((3, 4, wid...  2.24 us
    ppermute x8, waiting for transfers between devices, exchange(): lax.ppermute(value, ('leaf', 'oct'), [(i, i ^ bits) for i in range(device...  2.03 us
    pallas_call x1, Pallas kernels, finish(): pl.pallas_call(functools.partial(finish_kernel, order, leaves), out_shape...  1.34 us
  transfers between devices with their start and end apart: 9, of which 2 were waited for; matrix products, arithmetic and copies ran while one was open for 1% of the time, Pallas kernels for 54%

profile of v7, /device:TPU:9, one launch (start us, length us, event | category | flops | bytes accessed | tf_op | source)
XLA Modules:
  0.0 32.1 jit_solution(4162352458620770090)
XLA Ops:
  0.6 2.2 %prepare.1 = (f32[3,4,768]{2,1,0:T(4,128)S(1)}, bf16[32,768]{1,0:T(8,128)(2,1)S(1)}, f32[3,4,128]{2,1,0:T(4,128)S(1)}) custom-call(bf16[12,256,256]{2,1,0:T(8,128)(2,1)} %refs_0_.1, bf16[12,256]{1,0:T(8,128)(2,1)} %refs_1_.1, f32[12,256]{1,0:T(8,128)} %refs_2_.1, s32[12]{0:T(128)} %bitcast.31, f32[3072]{0:T(1024)} %refs_4_.1, f32[3,4]{1,0:T(4,128)} %refs_5_.1), custom_call_target="tpu_custom_call" | custom-call | tf_op jit(solution)/shard_map/prepare/pallas_call | solution.py:105
  2.9 1.9 %collective-permute-start = (f32[3,4,768]{2,1,0:T(4,128)S(1)}, f32[3,4,768]{2,1,0:T(4,128)S(1)}, u32[]{:S(2)}, u32[]{:S(2)}) collective-permute-start(f32[3,4,768]{2,1,0:T(4,128)S(1)} %get-tuple-element.32.own_ref), channel_id=1, source_target_pairs={{0,5},{1,4},{2,7},{3,6},{4,1},{5,0},{6,3},{7,2},{8,13},{9,12},{10,... | collective-permute-start | bytes 110600 | tf_op jit(solution)/shard_map/ppermute | solution.py:425
  4.7 1.2 %collective-permute-start.1 = (f32[3,4,768]{2,1,0:T(4,128)S(1)}, f32[3,4,768]{2,1,0:T(4,128)S(1)}, u32[]{:S(2)}, u32[]{:S(2)}) collective-permute-start(f32[3,4,768]{2,1,0:T(4,128)S(1)} %get-tuple-element.32.own_ref), channel_id=1, source_target_pairs={{0,6},{1,7},{2,4},{3,5},{4,2},{5,3},{6,0},{7,1},{8,14},{9,15},{10,... | collective-permute-start | bytes 110600 | tf_op jit(solution)/shard_map/ppermute | solution.py:425
  5.9 0.4 %collective-permute-start.2 = (f32[3,4,768]{2,1,0:T(4,128)S(1)}, f32[3,4,768]{2,1,0:T(4,128)S(1)}, u32[]{:S(2)}, u32[]{:S(2)}) collective-permute-start(f32[3,4,768]{2,1,0:T(4,128)S(1)} %get-tuple-element.32.own_ref), channel_id=1, source_target_pairs={{0,3},{1,2},{2,1},{3,0},{4,7},{5,6},{6,5},{7,4},{8,11},{9,10},{10,... | collective-permute-start | bytes 110600 | tf_op jit(solution)/shard_map/ppermute | solution.py:425
  6.3 1.0 %near.4 = (f32[16,768]{1,0:T(8,128)S(1)}, f32[3,4,128]{2,1,0:T(4,128)S(1)}) custom-call(f32[1,3,4,768]{3,2,1,0:T(4,128)S(1)} %bitcast.21, bf16[32,768]{1,0:T(8,128)(2,1)S(1)} %get-tuple-element.33.refs_1_.refs_2_.target_ref, f32[3,4,128]{2,1,0:T(4,128)S(1)} %get-tuple-element.34.refs_2_.refs_3_.column_ref), custom_call_target="tpu_custom_call" | custom-call | flops 294912000 | bytes 36864 | tf_op jit(solution)/shard_map/near/pallas_call | solution.py:274
  7.3 0.0 collective-permute-done
  7.3 1.6 %collective-permute-done.1 = f32[3,4,768]{2,1,0:T(4,128)S(1)} collective-permute-done((f32[3,4,768]{2,1,0:T(4,128)S(1)}, f32[3,4,768]{2,1,0:T(4,128)S(1)}, u32[]{:S(2)}, u32[]{:S(2)}) %collective-permute-start.1) | collective-permute-done | bytes 36896 | tf_op jit(solution)/shard_map/ppermute | solution.py:425
  8.8 0.4 %collective-permute-done.2 = f32[3,4,768]{2,1,0:T(4,128)S(1)} collective-permute-done((f32[3,4,768]{2,1,0:T(4,128)S(1)}, f32[3,4,768]{2,1,0:T(4,128)S(1)}, u32[]{:S(2)}, u32[]{:S(2)}) %collective-permute-start.2) | collective-permute-done | bytes 36896 | tf_op jit(solution)/shard_map/ppermute | solution.py:425
  9.4 0.3 %collective-permute-start.3 = (f32[4,3,4,768]{3,2,0,1:T(4,128)S(1)}, f32[4,3,4,768]{3,2,0,1:T(4,128)S(1)}, u32[]{:S(2)}, u32[]{:S(2)}) collective-permute-start(f32[4,3,4,768]{3,2,0,1:T(4,128)S(1)} %pad_maximum_fusion.1), channel_id=1, source_target_pairs={{0,1},{1,0},{2,3},{3,2},{4,5},{5,4},{6,7},{7,6},{8,9},{9,8},{10,11... | collective-permute-start | bytes 442376 | tf_op jit(solution)/shard_map/ppermute | solution.py:425
  9.7 0.4 %collective-permute-start.5 = (f32[4,3,4,768]{3,2,0,1:T(4,128)S(1)}, f32[4,3,4,768]{3,2,0,1:T(4,128)S(1)}, u32[]{:S(2)}, u32[]{:S(2)}) collective-permute-start(f32[4,3,4,768]{3,2,0,1:T(4,128)S(1)} %pad_maximum_fusion.1), channel_id=1, source_target_pairs={{0,9},{1,8},{2,11},{3,10},{4,13},{5,12},{6,15},{7,14},{8,1},{9,0},... | collective-permute-start | bytes 442376 | tf_op jit(solution)/shard_map/ppermute | solution.py:425
  10.1 2.6 %collective-permute-start.4 = (f32[4,2,4,768]{3,2,0,1:T(4,128)S(1)}, f32[4,2,4,768]{3,2,0,1:T(4,128)S(1)}, u32[]{:S(2)}, u32[]{:S(2)}) collective-permute-start(f32[4,2,4,768]{3,2,0,1:T(4,128)S(1)} %slice.23), channel_id=1, source_target_pairs={{0,1},{1,0},{2,3},{3,2},{4,5},{5,4},{6,7},{7,6},{8,17},{9,16},{10,... | collective-permute-start | bytes 294920 | tf_op jit(solution)/shard_map/ppermute | solution.py:462
  12.8 4.8 %near.5 = (f32[16,768]{1,0:T(8,128)S(1)}, f32[3,4,128]{2,1,0:T(4,128)S(1)}) custom-call(f32[3,3,4,768]{3,2,1,0:T(4,128)S(1)} %copy.10.refs_0_, f32[4,3,4,768]{3,2,1,0:T(4,128)S(1)} %copy.11.refs_1_, bf16[32,768]{1,0:T(8,128)(2,1)S(1)} %get-tuple-element.33.refs_1_.refs_2_.target_ref, f32[3,4,128]{2,1,0:T(4,128)S(1)} %get-tuple-element.34.refs_2_.refs_3_.column_ref, ...), custom_call_target="tpu_custom_call" | custom-call | flops 2064384000 | bytes 258048 | tf_op jit(solution)/shard_map/near/pallas_call | solution.py:274
  17.6 0.0 collective-permute-done.4
  17.6 0.0 collective-permute-done.5
  17.6 0.3 collective-permute-start.6
  17.9 0.3 collective-permute-start.7
  18.2 0.0 copy-start
  18.3 2.9 %near.6 = (f32[16,768]{1,0:T(8,128)S(1)}, f32[3,4,128]{2,1,0:T(4,128)S(1)}) custom-call(f32[4,3,4,768]{3,2,1,0:T(4,128)S(1)} %copy.12.refs_0_, bf16[32,768]{1,0:T(8,128)(2,1)S(1)} %get-tuple-element.33.refs_1_.refs_2_.target_ref, f32[3,4,128]{2,1,0:T(4,128)S(1)} %get-tuple-element.34.refs_2_.refs_3_.column_ref, f32[16,768]{1,0:T(8,128)S(1)} %get-tuple-element.49.refs_3_, ...), custom_call_target="tpu_custom_call" | custom-call | flops 1179648000 | bytes 147456 | tf_op jit(solution)/shard_map/near/pallas_call | solution.py:274
  21.3 0.1 reduce-precision_convert_fusion.1
  21.4 0.1 maximum_bitcast_fusion.held_ref
  21.5 0.6 %collective-permute-start.8 = (bf16[1,17,4,768]{3,2,1,0:T(4,128)(2,1)S(1)}, bf16[1,17,4,768]{3,2,1,0:T(4,128)(2,1)S(1)}, u32[]{:S(2)}, u32[]{:S(2)}) collective-permute-start(bf16[1,17,4,768]{3,2,1,0:T(4,128)(2,1)S(1)} %maximum_bitcast_fusion.held_ref), channel_id=1, source_target_pairs={{0,17},{1,16},{2,19},{3,18},{4,21},{5,20},{6,23},{7,22},{8,25},{9,... | collective-permute-start | bytes 313352 | tf_op jit(solution)/shard_map/ppermute | solution.py:425
  22.0 0.4 %shell_rows.1.product_in = f32[3,4,128]{2,1,0:T(4,128)S(1)} custom-call(bf16[1,17,4,768]{3,2,1,0:T(4,128)(2,1)S(1)} %maximum_bitcast_fusion.held_ref, bf16[3,4,98304]{2,1,0:T(4,128)(2,1)S(1)} %copy-done), custom_call_target="tpu_custom_call" | custom-call | tf_op jit(solution)/shard_map/shell_rows/pallas_call | solution.py:320
  22.5 8.2 %near.7 = (f32[16,768]{1,0:T(8,128)S(1)}, f32[3,4,128]{2,1,0:T(4,128)S(1)}) custom-call(f32[4,3,4,768]{3,2,1,0:T(4,128)S(1)} %copy.13.refs_0_, f32[8,2,4,768]{3,2,1,0:T(4,128)S(1)} %copy.14.refs_1_, bf16[32,768]{1,0:T(8,128)(2,1)S(1)} %get-tuple-element.33.refs_1_.refs_2_.target_ref, f32[3,4,128]{2,1,0:T(4,128)S(1)} %get-tuple-element.34.refs_2_.refs_3_.column_ref, ...), custom_call_target="tpu_custom_call" | custom-call | flops 3538944000 | bytes 344064 | tf_op jit(solution)/shard_map/near/pallas_call | solution.py:274
  30.8 1.3 %finish.1 = (f32[3,768]{1,0:T(4,128)}, f32[3,4]{1,0:T(4,128)}) custom-call(f32[3,4,768]{2,1,0:T(4,128)S(1)} %get-tuple-element.32.own_ref, bf16[32,768]{1,0:T(8,128)(2,1)S(1)} %get-tuple-element.33.refs_1_.refs_2_.target_ref, f32[3,4,128]{2,1,0:T(4,128)S(1)} %get-tuple-element.34.refs_2_.refs_3_.column_ref, ...), custom_call_target="tpu_custom_call" | custom-call | tf_op jit(solution)/shard_map/finish/pallas_call | solution.py:410
  (26 shorter events, 0.4 us)
Async XLA Ops:
  2.9 4.4 %collective-permute-start = (f32[3,4,768]{2,1,0:T(4,128)S(1)}, f32[3,4,768]{2,1,0:T(4,128)S(1)}, u32[]{:S(2)}, u32[]{:S(2)}) collective-permute-start(f32[3,4,768]{2,1,0:T(4,128)S(1)} %get-tuple-element.32.own_ref), channel_id=1, source_target_pairs={{0,5},{1,4},{2,7},{3,6},{4,1},{5,0},{6,3},{7,2},{8,13},{9,12},{10,... | collective-permute-start | bytes 110600 | tf_op jit(solution)/shard_map/ppermute | solution.py:425
  4.7 4.1 %collective-permute-start.1 = (f32[3,4,768]{2,1,0:T(4,128)S(1)}, f32[3,4,768]{2,1,0:T(4,128)S(1)}, u32[]{:S(2)}, u32[]{:S(2)}) collective-permute-start(f32[3,4,768]{2,1,0:T(4,128)S(1)} %get-tuple-element.32.own_ref), channel_id=1, source_target_pairs={{0,6},{1,7},{2,4},{3,5},{4,2},{5,3},{6,0},{7,1},{8,14},{9,15},{10,... | collective-permute-start | bytes 110600 | tf_op jit(solution)/shard_map/ppermute | solution.py:425
  5.9 3.4 %collective-permute-start.2 = (f32[3,4,768]{2,1,0:T(4,128)S(1)}, f32[3,4,768]{2,1,0:T(4,128)S(1)}, u32[]{:S(2)}, u32[]{:S(2)}) collective-permute-start(f32[3,4,768]{2,1,0:T(4,128)S(1)} %get-tuple-element.32.own_ref), channel_id=1, source_target_pairs={{0,3},{1,2},{2,1},{3,0},{4,7},{5,6},{6,5},{7,4},{8,11},{9,10},{10,... | collective-permute-start | bytes 110600 | tf_op jit(solution)/shard_map/ppermute | solution.py:425
  9.4 3.4 %collective-permute-start.3 = (f32[4,3,4,768]{3,2,0,1:T(4,128)S(1)}, f32[4,3,4,768]{3,2,0,1:T(4,128)S(1)}, u32[]{:S(2)}, u32[]{:S(2)}) collective-permute-start(f32[4,3,4,768]{3,2,0,1:T(4,128)S(1)} %pad_maximum_fusion.1), channel_id=1, source_target_pairs={{0,1},{1,0},{2,3},{3,2},{4,5},{5,4},{6,7},{7,6},{8,9},{9,8},{10,11... | collective-permute-start | bytes 442376 | tf_op jit(solution)/shard_map/ppermute | solution.py:425
  9.7 7.9 %collective-permute-start.5 = (f32[4,3,4,768]{3,2,0,1:T(4,128)S(1)}, f32[4,3,4,768]{3,2,0,1:T(4,128)S(1)}, u32[]{:S(2)}, u32[]{:S(2)}) collective-permute-start(f32[4,3,4,768]{3,2,0,1:T(4,128)S(1)} %pad_maximum_fusion.1), channel_id=1, source_target_pairs={{0,9},{1,8},{2,11},{3,10},{4,13},{5,12},{6,15},{7,14},{8,1},{9,0},... | collective-permute-start | bytes 442376 | tf_op jit(solution)/shard_map/ppermute | solution.py:425
  10.1 7.5 %collective-permute-start.4 = (f32[4,2,4,768]{3,2,0,1:T(4,128)S(1)}, f32[4,2,4,768]{3,2,0,1:T(4,128)S(1)}, u32[]{:S(2)}, u32[]{:S(2)}) collective-permute-start(f32[4,2,4,768]{3,2,0,1:T(4,128)S(1)} %slice.23), channel_id=1, source_target_pairs={{0,1},{1,0},{2,3},{3,2},{4,5},{5,4},{6,7},{7,6},{8,17},{9,16},{10,... | collective-permute-start | bytes 294920 | tf_op jit(solution)/shard_map/ppermute | solution.py:462
  17.6 3.5 %collective-permute-start.6 = (f32[4,3,4,768]{3,2,0,1:T(4,128)S(1)}, f32[4,3,4,768]{3,2,0,1:T(4,128)S(1)}, u32[]{:S(2)}, u32[]{:S(2)}) collective-permute-start(f32[4,3,4,768]{3,2,0,1:T(4,128)S(1)} %collective-permute-done.5), channel_id=1, source_target_pairs={{0,1},{1,0},{2,3},{3,2},{4,5},{5,4},{6,7},{7,6},{8,9},{9,8},{10,11... | collective-permute-start | bytes 442376 | tf_op jit(solution)/shard_map/ppermute | solution.py:425
  17.9 3.2 %collective-permute-start.7 = (f32[4,2,4,768]{3,2,0,1:T(4,128)S(1)}, f32[4,2,4,768]{3,2,0,1:T(4,128)S(1)}, u32[]{:S(2)}, u32[]{:S(2)}) collective-permute-start(f32[4,2,4,768]{3,2,0,1:T(4,128)S(1)} %collective-permute-done.4), channel_id=1, source_target_pairs={{0,1},{1,0},{2,3},{3,2},{4,5},{5,4},{6,7},{7,6},{8,9},{9,8},{10,11... | collective-permute-start | bytes 294920 | tf_op jit(solution)/shard_map/ppermute | solution.py:425
  18.2 3.8 %copy-start = (bf16[3,4,98304]{2,1,0:T(4,128)(2,1)S(1)}, bf16[3,4,98304]{2,1,0:T(4,128)(2,1)}, u32[]{:S(2)}) copy-start(bf16[3,4,98304]{2,1,0:T(4,128)(2,1)} %block_ref.3) | copy-start | bytes 7077892
  21.5 9.3 %collective-permute-start.8 = (bf16[1,17,4,768]{3,2,1,0:T(4,128)(2,1)S(1)}, bf16[1,17,4,768]{3,2,1,0:T(4,128)(2,1)S(1)}, u32[]{:S(2)}, u32[]{:S(2)}) collective-permute-start(bf16[1,17,4,768]{3,2,1,0:T(4,128)(2,1)S(1)} %maximum_bitcast_fusion.held_ref), channel_id=1, source_target_pairs={{0,17},{1,16},{2,19},{3,18},{4,21},{5,20},{6,23},{7,22},{8,25},{9,... | collective-permute-start | bytes 313352 | tf_op jit(solution)/shard_map/ppermute | solution.py:425
